TPU v7x, 32 devices: a whole 2x2x4 slice. The times are simulated.
32 devices in a mesh: dp: 8 (over y, x, core), seq: 4 (over z).
Axes of the slice: x: 2, y: 2, z: 4, core: 2. Of those that a mesh axis runs over, the one named last changes fastest.
Arguments:
- hidden_in: bfloat16 [8192, 1024], P(('dp', 'seq')), may hold values from -6 to 6
- doc_lengths: int32 [9], replicated, may hold values from 128 to 1792, as said below
- pad_lengths: int32 [9], replicated, may hold values from 0 to 64
- w_query: float32 [1024, 2048], P('dp'), may hold values from -0.1875 to 0.1875
- key_matrix: float32 [1024, 1024], P('dp'), may hold values from -0.1875 to 0.1875
- value_matrix: float32 [1024, 1024], P('dp'), may hold values from -0.1875 to 0.1875
- w_output: float32 [2048, 1024], P(None, 'dp'), may hold values from -1 to 1
- w_gate: float32 [1024, 3072], P('dp'), may hold values from -0.1875 to 0.1875
- w_up: float32 [1024, 3072], P('dp'), may hold values from -0.1875 to 0.1875
- w_down: float32 [3072, 1024], P(None, 'dp'), may hold values from -0.109375 to 0.109375
- attn_gain: float32 [1024], P('dp'), may hold values from 0.1 to 1.9
- mlp_gain: float32 [1024], P('dp'), may hold values from 0.1 to 1.9
- query_gain: float32 [128], P('dp'), may hold values from 0.1 to 1.9
- key_gain: float32 [128], P('dp'), may hold values from 0.1 to 1.9
- out_grad: bfloat16 [8192, 1024], P(('dp', 'seq')), may hold values from -6 to 6
Outputs:
- output_act: bfloat16 [8192, 1024], P(('dp', 'seq'))
- in_grad: bfloat16 [8192, 1024], P(('dp', 'seq'))
- grad_query: float32 [1024, 2048], P('dp')
- grad_key: float32 [1024, 1024], P('dp')
- grad_value: float32 [1024, 1024], P('dp')
- grad_output: float32 [2048, 1024], P(None, 'dp')
- grad_gate: float32 [1024, 3072], P('dp')
- grad_up: float32 [1024, 3072], P('dp')
- grad_down: float32 [3072, 1024], P(None, 'dp')
- grad_attn_gain: float32 [1024], P('dp')
- grad_mlp_gain: float32 [1024], P('dp')
- grad_query_gain: float32 [128], P('dp')
- grad_key_gain: float32 [128], P('dp')
Inputs may be any that keep to these rules, and one draw needn't show every extreme that they name: `doc_lengths`: the lengths of the documents packed in order into the stream; they sum to 8192; the shortest and the longest bound are reached in every draw.
All inputs are finite; a program needn't handle non-finite values.
Results may differ from a plain program's by a relative error of at most 0.02.
Values may be sent and summed in bfloat16 or wider, within the bound.
No kernel may reach another device: no remote copies, remote signals or barrier semaphores. Data moves between devices by JAX's collectives and lax.ppermute only.
A program may use at most 256 MiB of HBM per device.

v0:
```python
import jax
import jax.numpy as jnp
from jax import lax
from jax.sharding import PartitionSpec as P

QUERY_HEADS = 16
KEY_VALUE_HEADS = 8
HEAD_WIDTH = 128
FEEDFWD_UNITS = 3072
WINDOW_TOKENS = 1024
QBLOCK = 512


norm_eps = 1e-06
rope_base = 1000000.0
masked_score = -1e30


def passed_along(value, axis, by):
    devices = lax.axis_size(axis)
    pairs = [(i, i + by) for i in range(devices) if 0 <= i + by < devices]
    return lax.ppermute(value, axis, pairs)


def norm_rows(value_rows, scales):
    return (
        value_rows
        * lax.rsqrt(jnp.mean(value_rows * value_rows, axis=-1, keepdims=True) + norm_eps)
        * scales
    )


def rotate(value_rows, cosine, sine_table):
    half_width = value_rows.shape[-1] // 2
    turned = jnp.concatenate([-value_rows[..., half_width:], value_rows[..., :half_width]], axis=-1)
    return value_rows * cosine + turned * sine_table


def doc_tables(doc_lengths, pad_lengths):
    doc_ends = jnp.cumsum(doc_lengths)
    starts = doc_ends - doc_lengths
    return (starts, doc_ends, doc_ends - pad_lengths)


def token_info(token_index, tables):
    starts, doc_ends, pad_start = tables
    inside = (token_index[:, None] >= starts[None, :]) & (token_index[:, None] < doc_ends[None, :])
    numbers = jnp.arange(1, starts.shape[0] + 1, dtype=jnp.int32)
    doc_ids = jnp.sum(jnp.where(inside, numbers[None, :], 0), axis=1) - 1
    offset = jnp.sum(jnp.where(inside, starts[None, :], 0), axis=1)
    padded = (
        jnp.sum(jnp.where(inside & (token_index[:, None] >= pad_start[None, :]), 1, 0), axis=1) > 0
    )
    return (doc_ids, token_index - offset, padded)


def rope_tables(positions):
    inv_freq = rope_base ** (-jnp.arange(HEAD_WIDTH // 2, dtype=jnp.float32) * 2.0 / HEAD_WIDTH)
    angles = positions.astype(jnp.float32)[:, None] * inv_freq[None, :]
    cosine = jnp.concatenate([jnp.cos(angles), jnp.cos(angles)], axis=-1)[:, None, :]
    sine_table = jnp.concatenate([jnp.sin(angles), jnp.sin(angles)], axis=-1)[:, None, :]
    return (cosine, sine_table)


def allowed(q_index, k_index, q_doc, k_doc, k_pad):
    return (
        (q_doc[:, None] == k_doc[None, :])
        & (k_doc[None, :] >= 0)
        & (k_index[None, :] <= q_index[:, None])
        & (q_index[:, None] - k_index[None, :] < WINDOW_TOKENS)
        & (jnp.logical_not(k_pad)[None, :] | (k_index[None, :] == q_index[:, None]))
    )


def block_inputs(grouped_heads, keys_ext, values_ext, number, block_rows, start_row, tables):
    first_row = number * block_rows
    q_blk = lax.dynamic_slice_in_dim(grouped_heads, first_row, block_rows, 0)
    k_blk = lax.dynamic_slice_in_dim(keys_ext, first_row, block_rows + WINDOW_TOKENS, 0)
    v_blk = lax.dynamic_slice_in_dim(values_ext, first_row, block_rows + WINDOW_TOKENS, 0)
    q_index = start_row + first_row + jnp.arange(block_rows, dtype=jnp.int32)
    k_index = (
        start_row
        + first_row
        - WINDOW_TOKENS
        + jnp.arange(block_rows + WINDOW_TOKENS, dtype=jnp.int32)
    )
    q_doc, unused_pos, unused_pad = token_info(q_index, tables)
    k_doc, other_pos, k_pad = token_info(k_index, tables)
    pairs = allowed(q_index, k_index, q_doc, k_doc, k_pad)
    return (q_blk.transpose(1, 0, 2, 3), k_blk.transpose(1, 0, 2), v_blk.transpose(1, 0, 2), pairs)


def head_forward(q_head, k_head, v_head, pairs):
    scaling = HEAD_WIDTH ** (-0.5)
    raw_scores = jnp.einsum("qgd,kd->gqk", q_head, k_head, preferred_element_type=jnp.float32)
    logits = jnp.where(pairs[None], raw_scores * scaling, masked_score)
    row_max = jnp.max(logits, axis=-1, keepdims=True)
    weights_exp = jnp.where(pairs[None], jnp.exp(logits - row_max), 0.0)
    totals = jnp.sum(weights_exp, axis=-1, keepdims=True)
    probs_low = (weights_exp / totals).astype(jnp.bfloat16)
    outputs = jnp.einsum("gqk,kd->qgd", probs_low, v_head, preferred_element_type=jnp.float32)
    return (outputs, (row_max + jnp.log(totals))[..., 0])


def head_backward(q_head, k_head, v_head, lse_rows, d_out_head, pairs):
    scaling = HEAD_WIDTH ** (-0.5)
    raw_scores = jnp.einsum("qgd,kd->gqk", q_head, k_head, preferred_element_type=jnp.float32)
    logits = jnp.where(pairs[None], raw_scores * scaling, masked_score)
    probs = jnp.where(pairs[None], jnp.exp(logits - lse_rows[..., None]), 0.0)
    probs_low = probs.astype(jnp.bfloat16)
    d_probs = jnp.einsum("qgd,kd->gqk", d_out_head, v_head, preferred_element_type=jnp.float32)
    centred = jnp.sum(probs * d_probs, axis=-1, keepdims=True)
    d_scores = (scaling * probs * (d_probs - centred)).astype(jnp.bfloat16)
    d_query = jnp.einsum("gqk,kd->qgd", d_scores, k_head, preferred_element_type=jnp.float32)
    d_key = jnp.einsum("gqk,qgd->kd", d_scores, q_head, preferred_element_type=jnp.float32)
    d_value = jnp.einsum("gqk,qgd->kd", probs_low, d_out_head, preferred_element_type=jnp.float32)
    return (d_query, d_key, d_value)


def attend(query_rows, keys_ext, values_ext, start_row, tables):
    count_of_rows = query_rows.shape[0]
    kv_heads = keys_ext.shape[1]
    group_count = query_rows.shape[1] // kv_heads
    block_rows = min(QBLOCK, count_of_rows)
    grouped_heads = query_rows.reshape(count_of_rows, kv_heads, group_count, HEAD_WIDTH)

    def advance(carry, number):
        q_t, k_t, v_t, pairs = block_inputs(
            grouped_heads, keys_ext, values_ext, number, block_rows, start_row, tables
        )
        outputs, lse_rows = lax.map(
            lambda parts: head_forward(parts[0], parts[1], parts[2], pairs), (q_t, k_t, v_t)
        )
        return (carry, (outputs.transpose(1, 0, 2, 3), lse_rows))

    unused_carry, (outputs, lse_all) = lax.scan(
        advance, 0, jnp.arange(count_of_rows // block_rows, dtype=jnp.int32)
    )
    return (outputs.reshape(count_of_rows, kv_heads * group_count, HEAD_WIDTH), lse_all)


def attend_back(query_rows, keys_ext, values_ext, lse_all, d_out, start_row, tables):
    count_of_rows = query_rows.shape[0]
    kv_heads = keys_ext.shape[1]
    group_count = query_rows.shape[1] // kv_heads
    block_rows = min(QBLOCK, count_of_rows)
    span = block_rows + WINDOW_TOKENS
    grouped_heads = query_rows.reshape(count_of_rows, kv_heads, group_count, HEAD_WIDTH)
    d_grouped = d_out.reshape(count_of_rows, kv_heads, group_count, HEAD_WIDTH)
    zero_keys = jnp.zeros(keys_ext.shape, jnp.float32)

    def advance(carry, number):
        d_keys, d_values = carry
        q_t, k_t, v_t, pairs = block_inputs(
            grouped_heads, keys_ext, values_ext, number, block_rows, start_row, tables
        )
        first_row = number * block_rows
        d_blk = lax.dynamic_slice_in_dim(d_grouped, first_row, block_rows, 0).transpose(1, 0, 2, 3)
        d_query, d_key, d_value = lax.map(
            lambda parts: head_backward(parts[0], parts[1], parts[2], parts[3], parts[4], pairs),
            (q_t, k_t, v_t, lse_all[number], d_blk),
        )
        d_keys = lax.dynamic_update_slice_in_dim(
            d_keys,
            lax.dynamic_slice_in_dim(d_keys, first_row, span, 0) + d_key.transpose(1, 0, 2),
            first_row,
            0,
        )
        d_values = lax.dynamic_update_slice_in_dim(
            d_values,
            lax.dynamic_slice_in_dim(d_values, first_row, span, 0) + d_value.transpose(1, 0, 2),
            first_row,
            0,
        )
        return ((d_keys, d_values), d_query.transpose(1, 0, 2, 3))

    (d_keys, d_values), d_queries = lax.scan(
        advance, (zero_keys, zero_keys), jnp.arange(count_of_rows // block_rows, dtype=jnp.int32)
    )
    return (d_queries.reshape(count_of_rows, kv_heads * group_count, HEAD_WIDTH), d_keys, d_values)


def right_dot(left, right):
    return lax.dot_general(
        left, right, (((1,), (1,)), ((), ())), preferred_element_type=jnp.float32
    )


def left_dot(left, right):
    return lax.dot_general(
        left, right, (((0,), (0,)), ((), ())), preferred_element_type=jnp.float32
    )


def body(
    hidden_in,
    doc_lengths,
    pad_lengths,
    w_query,
    key_matrix,
    value_matrix,
    w_output,
    w_gate,
    w_up,
    w_down,
    attn_gain,
    mlp_gain,
    query_gain,
    key_gain,
    out_grad,
):
    reduced_dtype = jnp.bfloat16
    (
        wq_copy,
        wk_copy,
        wv_copy,
        wo_copy,
        wg_copy,
        wu_copy,
        wd_copy,
        ga_copy,
        gm_copy,
        gq_copy,
        gk_copy,
    ) = (
        lax.all_gather(w_query.astype(reduced_dtype), "dp", axis=0, tiled=True),
        lax.all_gather(key_matrix.astype(reduced_dtype), "dp", axis=0, tiled=True),
        lax.all_gather(value_matrix.astype(reduced_dtype), "dp", axis=0, tiled=True),
        lax.all_gather(w_output.astype(reduced_dtype), "dp", axis=1, tiled=True),
        lax.all_gather(w_gate.astype(reduced_dtype), "dp", axis=0, tiled=True),
        lax.all_gather(w_up.astype(reduced_dtype), "dp", axis=0, tiled=True),
        lax.all_gather(w_down.astype(reduced_dtype), "dp", axis=1, tiled=True),
        lax.all_gather(attn_gain.astype(reduced_dtype), "dp", axis=0, tiled=True),
        lax.all_gather(mlp_gain.astype(reduced_dtype), "dp", axis=0, tiled=True),
        lax.all_gather(query_gain.astype(reduced_dtype), "dp", axis=0, tiled=True),
        lax.all_gather(key_gain.astype(reduced_dtype), "dp", axis=0, tiled=True),
    )
    tables = doc_tables(doc_lengths, pad_lengths)
    count_of_rows = hidden_in.shape[0]
    seq_count = lax.axis_size("seq")
    first_token = (lax.axis_index("dp") * seq_count + lax.axis_index("seq")) * count_of_rows
    own_index = first_token + jnp.arange(count_of_rows, dtype=jnp.int32)
    unused_doc, positions, unused_pad = token_info(own_index, tables)
    cosine, sine_table = rope_tables(positions)
    residual = hidden_in.astype(jnp.float32)
    normed_f, norm_pull_in = jax.vjp(norm_rows, residual, ga_copy.astype(jnp.float32))
    normalized_input = normed_f.astype(reduced_dtype)
    q_proj = jnp.dot(normalized_input, wq_copy, preferred_element_type=jnp.float32).reshape(
        count_of_rows, QUERY_HEADS, HEAD_WIDTH
    )
    key_projected = jnp.dot(normalized_input, wk_copy, preferred_element_type=jnp.float32).reshape(
        count_of_rows, KEY_VALUE_HEADS, HEAD_WIDTH
    )
    v_send = (
        jnp.dot(normalized_input, wv_copy, preferred_element_type=jnp.float32)
        .astype(reduced_dtype)
        .reshape(count_of_rows, KEY_VALUE_HEADS, HEAD_WIDTH)
    )

    def qk_local(q_part, k_part, q_scales, k_scales):
        return (
            rotate(norm_rows(q_part, q_scales), cosine, sine_table),
            rotate(norm_rows(k_part, k_scales), cosine, sine_table),
        )

    (q_rot, k_rot), qk_pull = jax.vjp(
        qk_local, q_proj, key_projected, gq_copy.astype(jnp.float32), gk_copy.astype(jnp.float32)
    )
    q_send = q_rot.astype(reduced_dtype)
    k_send = k_rot.astype(reduced_dtype)
    queries_at, keys_here, values_here = (
        lax.all_to_all(q_send, "seq", split_axis=1, concat_axis=0, tiled=True),
        lax.all_to_all(k_send, "seq", split_axis=1, concat_axis=0, tiled=True),
        lax.all_to_all(v_send, "seq", split_axis=1, concat_axis=0, tiled=True),
    )
    group_rows = queries_at.shape[0]
    start_row = lax.axis_index("dp") * group_rows
    keys_tail, values_tail = passed_along(
        (keys_here[group_rows - WINDOW_TOKENS :], values_here[group_rows - WINDOW_TOKENS :]),
        "dp",
        1,
    )
    keys_ext = jnp.concatenate([keys_tail, keys_here], axis=0)
    values_ext = jnp.concatenate([values_tail, values_here], axis=0)
    attn_heads, lse_all = attend(queries_at, keys_ext, values_ext, start_row, tables)
    attn_tok = lax.all_to_all(
        attn_heads.astype(reduced_dtype), "seq", split_axis=0, concat_axis=1, tiled=True
    )
    attn_flat = attn_tok.reshape(count_of_rows, QUERY_HEADS * HEAD_WIDTH)
    middle = residual + jnp.dot(attn_flat, wo_copy, preferred_element_type=jnp.float32)
    normed_mid_f, norm_pull_mid = jax.vjp(norm_rows, middle, gm_copy.astype(jnp.float32))
    normed_mid = normed_mid_f.astype(reduced_dtype)
    gate_act = jnp.dot(normed_mid, wg_copy, preferred_element_type=jnp.float32)
    up_act = jnp.dot(normed_mid, wu_copy, preferred_element_type=jnp.float32)
    sigmoid_gate = 1.0 / (1.0 + jnp.exp(-gate_act))
    mixed_act = (gate_act * sigmoid_gate * up_act).astype(reduced_dtype)
    output_act = (middle + jnp.dot(mixed_act, wd_copy, preferred_element_type=jnp.float32)).astype(
        reduced_dtype
    )
    d_mixed = right_dot(out_grad, wd_copy)
    d_gate = (d_mixed * up_act * sigmoid_gate * (1.0 + gate_act * (1.0 - sigmoid_gate))).astype(
        reduced_dtype
    )
    d_up = (d_mixed * gate_act * sigmoid_gate).astype(reduced_dtype)
    d_normed_mid = right_dot(d_gate, wg_copy) + right_dot(d_up, wu_copy)
    d_mid_norm, d_mlp_gain = norm_pull_mid(d_normed_mid)
    d_middle = out_grad.astype(jnp.float32) + d_mid_norm
    d_proj = d_middle.astype(reduced_dtype)
    d_attn = (
        right_dot(d_proj, wo_copy)
        .astype(reduced_dtype)
        .reshape(count_of_rows, QUERY_HEADS, HEAD_WIDTH)
    )
    d_attn_heads = lax.all_to_all(d_attn, "seq", split_axis=1, concat_axis=0, tiled=True)
    d_queries, d_keys, d_values = attend_back(
        queries_at, keys_ext, values_ext, lse_all, d_attn_heads, start_row, tables
    )
    back_keys, back_values = (
        passed_along(d_keys[:WINDOW_TOKENS].astype(jnp.bfloat16), "dp", -1).astype(jnp.float32),
        passed_along(d_values[:WINDOW_TOKENS].astype(jnp.bfloat16), "dp", -1).astype(jnp.float32),
    )
    own_keys = d_keys[WINDOW_TOKENS:]
    own_values = d_values[WINDOW_TOKENS:]
    own_keys = jnp.concatenate(
        [
            own_keys[: group_rows - WINDOW_TOKENS],
            own_keys[group_rows - WINDOW_TOKENS :] + back_keys,
        ],
        axis=0,
    )
    own_values = jnp.concatenate(
        [
            own_values[: group_rows - WINDOW_TOKENS],
            own_values[group_rows - WINDOW_TOKENS :] + back_values,
        ],
        axis=0,
    )
    dq_tok, dk_tok, value_token_grad = (
        lax.all_to_all(
            d_queries.astype(reduced_dtype), "seq", split_axis=0, concat_axis=1, tiled=True
        ),
        lax.all_to_all(
            own_keys.astype(reduced_dtype), "seq", split_axis=0, concat_axis=1, tiled=True
        ),
        lax.all_to_all(
            own_values.astype(reduced_dtype), "seq", split_axis=0, concat_axis=1, tiled=True
        ),
    )
    d_qproj, key_projection_grad, d_query_gain, d_key_gain = qk_pull(
        (dq_tok.astype(jnp.float32), dk_tok.astype(jnp.float32))
    )
    d_qproj = d_qproj.reshape(count_of_rows, QUERY_HEADS * HEAD_WIDTH).astype(reduced_dtype)
    key_projection_grad = key_projection_grad.reshape(
        count_of_rows, KEY_VALUE_HEADS * HEAD_WIDTH
    ).astype(reduced_dtype)
    value_flat_grad = value_token_grad.reshape(count_of_rows, KEY_VALUE_HEADS * HEAD_WIDTH)
    d_normed_in = (
        right_dot(d_qproj, wq_copy)
        + right_dot(key_projection_grad, wk_copy)
        + right_dot(value_flat_grad, wv_copy)
    )
    d_in_norm, d_attn_gain = norm_pull_in(d_normed_in)
    in_grad = (d_middle + d_in_norm).astype(reduced_dtype)
    row_terms = jnp.concatenate(
        [
            left_dot(normalized_input, d_qproj),
            left_dot(normalized_input, key_projection_grad),
            left_dot(normalized_input, value_flat_grad),
            left_dot(normed_mid, d_gate),
            left_dot(normed_mid, d_up),
            left_dot(d_proj, attn_flat),
            left_dot(out_grad, mixed_act),
        ],
        axis=1,
    )
    gain_terms = jnp.stack([d_attn_gain, d_mlp_gain], axis=1)
    head_terms = jnp.stack([d_query_gain, d_key_gain], axis=1)
    row_sums, gain_sums, head_sums = (
        lax.psum_scatter(
            row_terms.astype(jnp.bfloat16), "dp", scatter_dimension=0, tiled=True
        ).astype(jnp.float32),
        lax.psum_scatter(
            gain_terms.astype(jnp.bfloat16), "dp", scatter_dimension=0, tiled=True
        ).astype(jnp.float32),
        lax.psum_scatter(
            head_terms.astype(jnp.bfloat16), "dp", scatter_dimension=0, tiled=True
        ).astype(jnp.float32),
    )
    row_sums, gain_sums, head_sums = (
        lax.psum(row_sums.astype(jnp.bfloat16), "seq").astype(jnp.float32),
        lax.psum(gain_sums.astype(jnp.bfloat16), "seq").astype(jnp.float32),
        lax.psum(head_sums.astype(jnp.bfloat16), "seq").astype(jnp.float32),
    )
    window_widths = [
        QUERY_HEADS * HEAD_WIDTH,
        KEY_VALUE_HEADS * HEAD_WIDTH,
        KEY_VALUE_HEADS * HEAD_WIDTH,
        FEEDFWD_UNITS,
        FEEDFWD_UNITS,
        QUERY_HEADS * HEAD_WIDTH,
        FEEDFWD_UNITS,
    ]
    pieces = []
    column = 0
    for width_now in window_widths:
        pieces.append(row_sums[:, column : column + width_now])
        column = column + width_now
    return (
        output_act,
        in_grad,
        pieces[0],
        pieces[1],
        pieces[2],
        pieces[5].T,
        pieces[3],
        pieces[4],
        pieces[6].T,
        gain_sums[:, 0],
        gain_sums[:, 1],
        head_sums[:, 0],
        head_sums[:, 1],
    )


def solution(mesh):
    in_specs = (
        P(("dp", "seq"), None),
        P(),
        P(),
        P("dp", None),
        P("dp", None),
        P("dp", None),
        P(None, "dp"),
        P("dp", None),
        P("dp", None),
        P(None, "dp"),
        P("dp"),
        P("dp"),
        P("dp"),
        P("dp"),
        P(("dp", "seq"), None),
    )
    out_specs = (
        P(("dp", "seq"), None),
        P(("dp", "seq"), None),
        P("dp", None),
        P("dp", None),
        P("dp", None),
        P(None, "dp"),
        P("dp", None),
        P("dp", None),
        P(None, "dp"),
        P("dp"),
        P("dp"),
        P("dp"),
        P("dp"),
    )
    return jax.shard_map(body, mesh=mesh, in_specs=in_specs, out_specs=out_specs, check_vma=False)
```

profile of v0, /device:TPU:0, one launch (start us, length us, event | category | flops | bytes accessed | tf_op | source)
XLA Modules:
  0.0 994.9 jit_solution(9560144753721136819)
XLA Ops:
  19.5 15.2 %all-reduce.6 = (bf16[128]{0:T(256)(128)(2,1)S(1)}, bf16[128]{0:T(256)(128)(2,1)S(1)}) all-reduce(bf16[128]{0:T(256)(128)(2,1)S(1)} %dynamic-update-slice, bf16[128]{0:T(256)(128)(2,1)S(1)} %dynamic-update-slice.1), channel_id=1, replica_groups=mesh['dp'=8,'seq'=4] {'dp'}, use_global_device_ids=true, to_apply=%add.4 | all-reduce | flops 256 | bytes 1024
  34.7 7.8 all-gather
  54.3 17.3 %all-gather.14.cloned.1.call-done = bf16[1024,1024]{1,0:T(8,128)(2,1)} async-done(((bf16[128,1024]{1,0:T(8,128)(2,1)}), bf16[1024,1024]{1,0:T(8,128)(2,1)}) %all-gather.14.cloned.1.call-update) | async-done | bytes 2097168 | tf_op jit(solution)/shard_map/all_gather | solution.py:228
  74.8 36.0 %all-gather.10.cloned.1.call-done = bf16[1024,2048]{1,0:T(8,128)(2,1)} async-done(((bf16[128,2048]{1,0:T(8,128)(2,1)}), bf16[1024,2048]{1,0:T(8,128)(2,1)}) %all-gather.10.cloned.1.call-update) | async-done | bytes 4194320 | tf_op jit(solution)/shard_map/all_gather | solution.py:226
  124.1 11.4 %all-to-all-done.2 = bf16[256,8,128]{2,0,1:T(8,128)(2,1)S(1)} async-done(((bf16[256,8,128]{2,0,1:T(8,128)(2,1)}), bf16[256,8,128]{2,0,1:T(8,128)(2,1)S(1)}, u32[]{:S(2)}, u32[]{:S(2)}) %all-to-all-start.2) | async-done | bytes 524320 | tf_op jit(solution)/shard_map/all_to_all | solution.py:274
  149.9 15.2 %all-to-all-done = bf16[256,16,128]{2,0,1:T(8,128)(2,1)} async-done(((bf16[256,16,128]{2,0,1:T(8,128)(2,1)}), bf16[256,16,128]{2,0,1:T(8,128)(2,1)}, u32[]{:S(2)}, u32[]{:S(2)}) %all-to-all-start) | async-done | bytes 1048608 | tf_op jit(solution)/shard_map/all_to_all | solution.py:272
  168.5 51.2 %while.97 = (s32[]{:T(128)}, bf16[2,512,2,2,128]{4,1,0,3,2:T(8,128)(2,1)}, f32[2,2,2,512]{3,2,1,0:T(2,128)S(1)}, s32[2]{0:T(128)S(1)}, bf16[1024,2,2,128]{3,0,2,...) while((s32[]{:T(128)}, ...), condition=%wide.region_13.14_spmd, body=%wide.region_5.13_spmd.sunk | while | flops 835343872 | bytes 38931356 | solution.py:136
  173.3 18.6 %while.100 = (s32[]{:T(128)}, bf16[2,512,2,128]{1,3,2,0:T(8,128)(2,1)}, f32[2,2,512]{2,1,0:T(2,128)S(1)}, bf16[2,1536,128]{1,2,0:T(8,128)(2,1)}, bf16[2,1536,128...) while((s32[]{:T(128)}, ...), condition=%wide.region_12.12_spmd.clone, body=%wide.region_9.11_spmd.clone.sunk | while | flops 835189760 | bytes 30987484 | solution.py:131
  198.9 18.6 %while.100 = (s32[]{:T(128)}, bf16[2,512,2,128]{1,3,2,0:T(8,128)(2,1)}, f32[2,2,512]{2,1,0:T(2,128)S(1)}, bf16[2,1536,128]{1,2,0:T(8,128)(2,1)}, bf16[2,1536,128...) while((s32[]{:T(128)}, ...), condition=%wide.region_12.12_spmd.clone, body=%wide.region_9.11_spmd.clone.sunk | while | flops 835189760 | bytes 30987484 | solution.py:131
  227.0 9.3 all-gather.1
  236.3 16.0 %all-to-all-done.3 = bf16[1024,4,128]{2,1,0:T(4,128)(2,1)} async-done(((bf16[1024,4,128]{2,1,0:T(4,128)(2,1)}), bf16[1024,4,128]{2,1,0:T(4,128)(2,1)}, u32[]{:S(2)}, u32[]{:S(2)}) %all-to-all-start.3) | async-done | bytes 1048608 | tf_op jit(solution)/shard_map/all_to_all | solution.py:286
  262.9 6.2 fusion.104
  269.1 6.5 fusion.105
  275.6 20.1 %all-gather.22.cloned.1.call-done = bf16[3072,1024]{1,0:T(8,128)(2,1)} async-done(((bf16[3072,128]{1,0:T(8,128)(2,1)}), bf16[3072,1024]{1,0:T(8,128)(2,1)}) %all-gather.22.cloned.1.call-update) | async-done | bytes 6291472 | tf_op jit(solution)/shard_map/all_gather | solution.py:232
  295.7 9.7 multiply_convert_fusion
  305.5 5.8 fusion.106
  321.7 26.3 %all-to-all-done.4 = bf16[256,16,128]{2,0,1:T(8,128)(2,1)} async-done(((bf16[256,16,128]{2,0,1:T(8,128)(2,1)}), bf16[256,16,128]{2,0,1:T(8,128)(2,1)}, u32[]{:S(2)}, u32[]{:S(2)}) %all-to-all-start.4) | async-done | bytes 1048608 | tf_op jit(solution)/shard_map/all_to_all | solution.py:314
  354.6 95.3 %while.99 = (s32[]{:T(128)}, f32[2048,2,128]{2,1,0:T(2,128)}, f32[2048,2,128]{2,1,0:T(2,128)}, bf16[2,512,2,2,128]{4,1,0,3,2:T(8,128)(2,1)}, s32[2]{0:T(128)S(1)...) while((s32[]{:T(128)}, f32[2048,2,128]{2,1,0:T(2,128)}, ...), condition=%wide.region_23.24_spmd, body=%wide.region_16.23_spmd.sunk | while | flops 2039371264 | bytes 134998304 | solution.py:177
  363.1 25.0 %while.101 = (s32[]{:T(128)}, bf16[2,512,2,128]{1,3,2,0:T(8,128)(2,1)}, f32[2,1536,128]{2,1,0:T(8,128)}, f32[2,1536,128]{2,1,0:T(8,128)}, bf16[2,1536,128]{2,1,0...) while((s32[]{:T(128)}, ...), condition=%wide.region_22.22_spmd.clone, body=%wide.region_20.21_spmd.clone.sunk | while | flops 2038430720 | bytes 82489680 | solution.py:159
  392.2 7.7 copy_dynamic-update-slice_fusion.3
  410.6 25.0 %while.101 = (s32[]{:T(128)}, bf16[2,512,2,128]{1,3,2,0:T(8,128)(2,1)}, f32[2,1536,128]{2,1,0:T(8,128)}, f32[2,1536,128]{2,1,0:T(8,128)}, bf16[2,1536,128]{2,1,0...) while((s32[]{:T(128)}, ...), condition=%wide.region_22.22_spmd.clone, body=%wide.region_20.21_spmd.clone.sunk | while | flops 2038430720 | bytes 82489680 | solution.py:159
  439.7 7.7 copy_dynamic-update-slice_fusion.3
  464.6 8.0 all-to-all-done.6
  479.3 8.7 all-to-all-done.7
  488.0 5.2 all-to-all-start.5
  510.4 8.9 all-to-all-done.5
  565.2 189.5 %reduce-scatter.8.cloned.1.call-done = bf16[128,15360]{1,0:T(8,128)(2,1)} async-done(((bf16[1024,15360]{1,0:T(8,128)(2,1)}), bf16[128,15360]{1,0:T(8,128)(2,1)}) %reduce-scatter.8.cloned.1.call-update) | async-done | bytes 3932176 | tf_op jit(solution)/shard_map/reduce_scatter | solution.py:379
  754.7 5.9 fusion.69
  761.8 27.7 %reduce-scatter.12.cloned.1.call-done = bf16[16,2]{1,0:T(8,128)(2,1)} async-done(((bf16[128,2]{1,0:T(8,128)(2,1)}), bf16[16,2]{1,0:T(8,128)(2,1)}) %reduce-scatter.12.cloned.1.call-update) | async-done | bytes 80
  790.3 36.6 %reduce-scatter.10.cloned.1.call-done = bf16[128,2]{1,0:T(8,128)(2,1)} async-done(((bf16[1024,2]{1,0:T(8,128)(2,1)}), bf16[128,2]{1,0:T(8,128)(2,1)}) %reduce-scatter.10.cloned.1.call-update) | async-done | bytes 528
  827.8 11.9 %all-reduce.7 = (bf16[128,2]{0,1:T(2,128)(2,1)S(1)}, bf16[16,2]{0,1:T(2,128)(2,1)S(1)}) all-reduce(bf16[128,2]{0,1:T(2,128)(2,1)S(1)} %copy.370, bf16[16,2]{0,1:T(2,128)(2,1)S(1)} %copy.372), channel_id=1, replica_groups=mesh['dp'=8,'seq'=4] {'seq'}, use_global_device_ids=true, to_apply=%region_32.33 | all-reduce | flops 288 | bytes 1152 | tf_op jit(solution)/shard_map/psum | solution.py:391
  840.7 135.1 %all-reduce.10.cloned.1.call-done = bf16[128,15360]{1,0:T(8,128)(2,1)} async-done(((bf16[128,15360]{1,0:T(8,128)(2,1)}), bf16[128,15360]{1,0:T(8,128)(2,1)}) %all-reduce.10.cloned.1.call-update) | async-done | bytes 3932176 | tf_op jit(solution)/shard_map/psum | solution.py:390
  (540 shorter events, 315.3 us)
Async XLA Ops:
  7.2 36.9 %all-gather.12.cloned.1.call-start = ((), (), s32[]{:S(2)}) async-start(), calls=%async_computation.12 | async-start | bytes 2359296 | tf_op jit(solution)/shard_map/all_gather | solution.py:227
  9.1 62.4 %all-gather.14.cloned.1.call-start = ((), (), s32[]{:S(2)}) async-start(), calls=%async_computation.13 | async-start | bytes 2359296 | tf_op jit(solution)/shard_map/all_gather | solution.py:228
  11.0 99.8 %all-gather.10.cloned.1.call-start = ((), (), s32[]{:S(2)}) async-start(), calls=%async_computation.11 | async-start | bytes 4718592 | tf_op jit(solution)/shard_map/all_gather | solution.py:226
  11.9 244.9 %all-gather.16.cloned.1.call-start = ((), (), s32[]{:S(2)}) async-start(), calls=%async_computation.14 | async-start | bytes 4718592 | tf_op jit(solution)/shard_map/all_gather | solution.py:229
  14.1 248.1 %all-gather.18.cloned.1.call-start = ((), (), s32[]{:S(2)}) async-start(), calls=%async_computation.15 | async-start | bytes 7077888 | tf_op jit(solution)/shard_map/all_gather | solution.py:230
  15.1 27.5 %copy-start.69 = (s32[9]{0:T(128)S(1)}, s32[9]{0:T(128)}, u32[]{:S(2)}) copy-start(s32[9]{0:T(128)} %param.24) | copy-start | bytes 112
  15.1 27.7 %copy-start.70 = (s32[9]{0:T(128)S(1)}, s32[9]{0:T(128)}, u32[]{:S(2)}) copy-start(s32[9]{0:T(128)} %param.25) | copy-start | bytes 112
  15.2 28.7 %copy-start.15 = (bf16[256,1024]{1,0:T(8,128)(2,1)S(1)}, bf16[256,1024]{1,0:T(8,128)(2,1)}, u32[]{:S(2)}) copy-start(bf16[256,1024]{1,0:T(8,128)(2,1)} %param.23) | copy-start | bytes 1572868
  15.2 253.9 %all-gather.20.cloned.1.call-start = ((), (), s32[]{:S(2)}) async-start(), calls=%async_computation.16 | async-start | bytes 7077888 | tf_op jit(solution)/shard_map/all_gather | solution.py:231
  34.7 87.3 %copy-start.66 = (f32[128]{0:T(128)}, f32[128]{0:T(128)S(1)}, u32[]{:S(2)}) copy-start(f32[128]{0:T(128)S(1)} %convert_element_type.189) | copy-start | bytes 1540
  42.6 68.2 %copy-start.54 = (f32[8,1,128]{2,1,0:T(1,128)}, f32[8,1,128]{2,1,0:T(1,128)S(1)}, u32[]{:S(2)}) copy-start(f32[8,1,128]{2,1,0:T(1,128)S(1)} %convert_element_type.242) | copy-start | bytes 12292
  43.6 78.4 %copy-start.33 = (f32[256,128]{1,0:T(8,128)}, f32[256,128]{1,0:T(8,128)S(1)}, u32[]{:S(2)}) copy-start(f32[256,128]{1,0:T(8,128)S(1)} %get-tuple-element.960) | copy-start | bytes 393220
  43.6 78.4 %copy-start.35 = (f32[256,128]{1,0:T(8,128)}, f32[256,128]{1,0:T(8,128)S(1)}, u32[]{:S(2)}) copy-start(f32[256,128]{1,0:T(8,128)S(1)} %get-tuple-element.961) | copy-start | bytes 393220
  44.1 66.7 %copy-start.58 = (f32[256]{0:T(256)}, f32[256]{0:T(256)S(1)}, u32[]{:S(2)}) copy-start(f32[256]{0:T(256)S(1)} %fusion.89) | copy-start | bytes 3076
  49.5 65.9 %all-to-all-start.1 = ((bf16[256,8,128]{2,0,1:T(8,128)(2,1)}), bf16[256,8,128]{2,0,1:T(8,128)(2,1)S(1)}, u32[]{:S(2)}, u32[]{:S(2)}) async-start(bf16[256,8,128]{2,0,1:T(8,128)(2,1)} %copy.332), calls=%async_computation.1 | async-start | bytes 1048576 | tf_op jit(solution)/shard_map/all_to_all | solution.py:273
  116.0 19.5 %all-to-all-start.2 = ((bf16[256,8,128]{2,0,1:T(8,128)(2,1)}), bf16[256,8,128]{2,0,1:T(8,128)(2,1)S(1)}, u32[]{:S(2)}, u32[]{:S(2)}) async-start(bf16[256,8,128]{2,0,1:T(8,128)(2,1)} %bitcast.386), calls=%async_computation.2 | async-start | bytes 1048576 | tf_op jit(solution)/shard_map/all_to_all | solution.py:274
  135.5 29.6 %all-to-all-start = ((bf16[256,16,128]{2,0,1:T(8,128)(2,1)}), bf16[256,16,128]{2,0,1:T(8,128)(2,1)}, u32[]{:S(2)}, u32[]{:S(2)}) async-start(bf16[256,16,128]{2,0,1:T(8,128)(2,1)} %fusion.64), calls=%async_computation | async-start | bytes 2097152 | tf_op jit(solution)/shard_map/all_to_all | solution.py:272
  139.7 156.0 %all-gather.22.cloned.1.call-start = ((), (), s32[]{:S(2)}) async-start(), calls=%async_computation.17 | async-start | bytes 7077888 | tf_op jit(solution)/shard_map/all_gather | solution.py:232
  139.8 7.5 collective-permute-start
  142.0 6.5 collective-permute-start.1
  222.7 29.5 %all-to-all-start.3 = ((bf16[1024,4,128]{2,1,0:T(4,128)(2,1)}), bf16[1024,4,128]{2,1,0:T(4,128)(2,1)}, u32[]{:S(2)}, u32[]{:S(2)}) async-start(bf16[1024,4,128]{2,1,0:T(4,128)(2,1)} %copy.338), calls=%async_computation.3 | async-start | bytes 2097152 | tf_op jit(solution)/shard_map/all_to_all | solution.py:286
  317.1 30.8 %all-to-all-start.4 = ((bf16[256,16,128]{2,0,1:T(8,128)(2,1)}), bf16[256,16,128]{2,0,1:T(8,128)(2,1)}, u32[]{:S(2)}, u32[]{:S(2)}) async-start(bf16[256,16,128]{2,0,1:T(8,128)(2,1)} %bitcast.381), calls=%async_computation.4 | async-start | bytes 2097152 | tf_op jit(solution)/shard_map/all_to_all | solution.py:314
  451.5 4.2 collective-permute-start.2
  454.4 7.6 collective-permute-start.3
  458.4 14.2 %all-to-all-start.6 = ((bf16[1024,2,128]{2,1,0:T(2,128)(2,1)}), bf16[1024,2,128]{2,1,0:T(2,128)(2,1)S(1)}, u32[]{:S(2)}, u32[]{:S(2)}) async-start(bf16[1024,2,128]{2,1,0:T(2,128)(2,1)} %add_convert_fusion.1), calls=%async_computation.6 | async-start | bytes 1048576 | tf_op jit(solution)/shard_map/all_to_all | solution.py:342
  472.5 15.4 %all-to-all-start.7 = ((bf16[1024,2,128]{2,1,0:T(2,128)(2,1)}), bf16[1024,2,128]{2,1,0:T(2,128)(2,1)S(1)}, u32[]{:S(2)}, u32[]{:S(2)}) async-start(bf16[1024,2,128]{2,1,0:T(2,128)(2,1)} %add_convert_fusion), calls=%async_computation.7 | async-start | bytes 1048576 | tf_op jit(solution)/shard_map/all_to_all | solution.py:345
  488.0 31.4 %all-to-all-start.5 = ((bf16[1024,4,128]{2,1,0:T(4,128)(2,1)}), bf16[1024,4,128]{2,1,0:T(4,128)(2,1)}, u32[]{:S(2)}, u32[]{:S(2)}) async-start(bf16[1024,4,128]{2,1,0:T(4,128)(2,1)} %copy.344), calls=%async_computation.5 | async-start | bytes 2097152 | tf_op jit(solution)/shard_map/all_to_all | solution.py:339
  493.2 261.5 %reduce-scatter.8.cloned.1.call-start = ((), (), s32[]{:S(2)}) async-start(), calls=%async_computation.18 | async-start | bytes 35389440 | tf_op jit(solution)/shard_map/reduce_scatter | solution.py:379
  555.1 234.5 %reduce-scatter.12.cloned.1.call-start = ((), (), s32[]{:S(2)}) async-start(), calls=%async_computation.21 | async-start | bytes 36864
  564.0 262.9 %reduce-scatter.10.cloned.1.call-start = ((), (), s32[]{:S(2)}) async-start(), calls=%async_computation.20 | async-start | bytes 294912
  564.9 189.8 %copy-start.32 = (f32[256,1024]{1,0:T(8,128)S(1)}, f32[256,1024]{1,0:T(8,128)}, u32[]{:S(2)}) copy-start(f32[256,1024]{1,0:T(8,128)} %copy-done.30) | copy-start | bytes 3145732
  565.0 410.8 %all-reduce.10.cloned.1.call-start = ((), (), s32[]{:S(2)}) async-start(), calls=%async_computation.19 | async-start | bytes 7864320 | tf_op jit(solution)/shard_map/psum | solution.py:390
  (106 other events, 368.9 us)
Sparse Core Ops, SparseCore 0:
  10.5 30.6 all-gather.11
  43.6 27.8 all-gather.13
  74.0 36.7 all-gather.9
  113.1 38.1 all-gather.15
  153.5 45.6 all-gather.17
  201.6 45.5 all-gather.19
  249.0 46.6 all-gather.21
  555.2 199.4 reduce-scatter.7
  758.3 31.2 reduce-scatter.11
  793.3 33.5 reduce-scatter.9
  829.3 146.4 all-reduce.9
where the time goes:
time: 1010 us; the launch traced here: 995 us
  waiting for transfers between devices  557 us (55%)
  local copies, waits for them, and re-layouts  126 us (12%)
  matrix products  126 us (12%)
  other arithmetic  73.5 us (7%)
  starting transfers between devices  44.5 us (4%)
  blocking collectives  44.3 us (4%)
  between operations  15.9 us (2%)
    reduce_scatter x1, waiting for transfers between devices, body(): lax.psum_scatter(row_terms.astype(jnp.bfloat16), 'dp', scatter_dimension=...  189 us
    psum x1, waiting for transfers between devices, body(): lax.psum(row_sums.astype(jnp.bfloat16), 'seq').astype(jnp.float32)  135 us
    unnamed x13, waiting for transfers between devices  64.5 us
    all_gather x1, waiting for transfers between devices, body(): lax.all_gather(w_query.astype(reduced_dtype), 'dp', axis=0, tiled=True)  36 us
    all_to_all x1, waiting for transfers between devices, body(): lax.all_to_all(d_attn, 'seq', split_axis=1, concat_axis=0, tiled=True)  26.3 us
    dot_general x7, matrix products, right_dot(): lax.dot_general(left, right, (((1,), (1,)), ((), ())), preferred_element_...  26.1 us
    dot_general x7, matrix products, left_dot(): lax.dot_general(left, right, (((0,), (0,)), ((), ())), preferred_element_...  26 us
  transfers between devices with their start and end apart: 23, of which 14 were waited for; matrix products, arithmetic and copies ran while one was open for 15% of the time, Pallas kernels for 0%

commit v1 on v0

v1 whole, which is shorter than its diff:
```python
import functools

import jax
import jax.numpy as jnp
from jax import lax
from jax.experimental import pallas as pl
from jax.experimental.pallas import tpu as pltpu
from jax.sharding import Mesh, PartitionSpec as P

QUERY_HEADS = 16
KEY_VALUE_HEADS = 8
HEAD_WIDTH = 128
FEEDFWD_UNITS = 3072
WINDOW_TOKENS = 1024
QROWS = 256
GROUP = QUERY_HEADS // KEY_VALUE_HEADS
SPAN_CHUNKS = (QROWS + WINDOW_TOKENS) // QROWS

norm_eps = 1e-06
rope_base = 1000000.0
score_scale = HEAD_WIDTH**-0.5
log2_e = 1.4426950408889634
bf16 = jnp.bfloat16
f32 = jnp.float32


def nt_dot(left, right):
    return lax.dot_general(left, right, (((1,), (1,)), ((), ())), preferred_element_type=f32)


def tn_dot(left, right):
    return lax.dot_general(left, right, (((0,), (0,)), ((), ())), preferred_element_type=f32)


def nn_dot(left, right):
    return jnp.dot(left, right, preferred_element_type=f32)


def chunk_mask(bounds_ref, chunk):
    low = bounds_ref[0:1, :]
    high = bounds_ref[1:2, :]
    key = lax.broadcasted_iota(jnp.int32, (QROWS, QROWS), 0) + chunk * QROWS
    mask = (key >= low) & (key <= high)
    if chunk == SPAN_CHUNKS - 1:
        own = lax.broadcasted_iota(jnp.int32, (QROWS, QROWS), 1) + WINDOW_TOKENS
        mask = mask | (key == own)
    return mask


def attend_kernel(q_ref, k_ref, v_ref, bounds_ref, out_ref, total_ref):
    base = pl.multiple_of(pl.program_id(1) * QROWS, QROWS)
    heads = [q_ref[:, g * HEAD_WIDTH : (g + 1) * HEAD_WIDTH] for g in range(GROUP)]
    sums = [jnp.zeros((1, QROWS), f32) for g in range(GROUP)]
    outs = [jnp.zeros((HEAD_WIDTH, QROWS), f32) for g in range(GROUP)]
    for chunk in range(SPAN_CHUNKS):
        rows = pl.ds(base + chunk * QROWS, QROWS)
        keys = k_ref[rows, :]
        values = v_ref[rows, :]
        mask = chunk_mask(bounds_ref, chunk)
        for g in range(GROUP):
            scores = nt_dot(keys, heads[g])
            weights = jnp.where(mask, jnp.exp2(scores * (score_scale * log2_e)), 0.0)
            sums[g] = sums[g] + jnp.sum(weights, axis=0, keepdims=True)
            outs[g] = outs[g] + tn_dot(values, weights.astype(bf16))
    for g in range(GROUP):
        normed = outs[g] * (1.0 / sums[g])
        out_ref[:, g * HEAD_WIDTH : (g + 1) * HEAD_WIDTH] = normed.T.astype(bf16)
        total_ref[g : g + 1, :] = sums[g]


def attend(queries, kv_ext, bounds):
    rows = queries.shape[0]
    ext = kv_ext.shape[0]
    kv_heads = kv_ext.shape[1] // (2 * HEAD_WIDTH)
    blocks = rows // QROWS
    wide = GROUP * HEAD_WIDTH
    pairs = blocks * kv_heads * GROUP * SPAN_CHUNKS * QROWS * QROWS
    return pl.pallas_call(
        attend_kernel,
        grid=(kv_heads, blocks),
        in_specs=[
            pl.BlockSpec((QROWS, wide), lambda j, i: (i, j)),
            pl.BlockSpec((ext, HEAD_WIDTH), lambda j, i: (0, j)),
            pl.BlockSpec((ext, HEAD_WIDTH), lambda j, i: (0, kv_heads + j)),
            pl.BlockSpec((None, 8, QROWS), lambda j, i: (i, 0, 0)),
        ],
        out_specs=[
            pl.BlockSpec((QROWS, wide), lambda j, i: (i, j)),
            pl.BlockSpec((None, None, 8, QROWS), lambda j, i: (j, i, 0, 0)),
        ],
        out_shape=[
            jax.ShapeDtypeStruct((rows, kv_heads * wide), bf16),
            jax.ShapeDtypeStruct((kv_heads, blocks, 8, QROWS), f32),
        ],
        cost_estimate=pl.CostEstimate(
            flops=4 * pairs * HEAD_WIDTH, bytes_accessed=4 << 20, transcendentals=pairs
        ),
        name="attend",
    )(queries, kv_ext, kv_ext, bounds)


def attend_back_kernel(
    q_ref, k_ref, v_ref, bounds_ref, total_ref, out_ref, d_out_ref, d_q_ref, d_k_ref, d_v_ref
):
    block = pl.program_id(1)
    base = pl.multiple_of(block * QROWS, QROWS)

    @pl.when(block == 0)
    def clear():
        d_k_ref[...] = jnp.zeros_like(d_k_ref)
        d_v_ref[...] = jnp.zeros_like(d_v_ref)

    spans = [slice(g * HEAD_WIDTH, (g + 1) * HEAD_WIDTH) for g in range(GROUP)]
    heads = [q_ref[:, s] for s in spans]
    d_outs = [d_out_ref[:, s] for s in spans]
    shares = [1.0 / total_ref[g : g + 1, :] for g in range(GROUP)]
    deltas = []
    for g in range(GROUP):
        product = d_outs[g].astype(f32) * out_ref[:, spans[g]].astype(f32)
        deltas.append(jnp.sum(product.T, axis=0, keepdims=True))
    d_queries = [jnp.zeros((HEAD_WIDTH, QROWS), f32) for g in range(GROUP)]
    for chunk in range(SPAN_CHUNKS):
        rows = pl.ds(base + chunk * QROWS, QROWS)
        keys = k_ref[rows, :]
        values = v_ref[rows, :]
        mask = chunk_mask(bounds_ref, chunk)
        d_key = jnp.zeros((QROWS, HEAD_WIDTH), f32)
        d_value = jnp.zeros((QROWS, HEAD_WIDTH), f32)
        for g in range(GROUP):
            scores = nt_dot(keys, heads[g])
            probs = jnp.where(
                mask, jnp.exp2(scores * (score_scale * log2_e)) * shares[g], 0.0
            )
            d_probs = nt_dot(values, d_outs[g])
            d_scores = (probs * (d_probs - deltas[g]) * score_scale).astype(bf16)
            d_value = d_value + nn_dot(probs.astype(bf16), d_outs[g])
            d_key = d_key + nn_dot(d_scores, heads[g])
            d_queries[g] = d_queries[g] + tn_dot(keys, d_scores)
        d_k_ref[rows, :] += d_key
        d_v_ref[rows, :] += d_value
    for g in range(GROUP):
        d_q_ref[:, spans[g]] = d_queries[g].T.astype(bf16)


def attend_back(queries, kv_ext, bounds, totals, outs, d_outs):
    rows = queries.shape[0]
    ext = kv_ext.shape[0]
    kv_heads = kv_ext.shape[1] // (2 * HEAD_WIDTH)
    blocks = rows // QROWS
    wide = GROUP * HEAD_WIDTH
    pairs = blocks * kv_heads * GROUP * SPAN_CHUNKS * QROWS * QROWS
    block_spec = pl.BlockSpec((QROWS, wide), lambda j, i: (i, j))
    return pl.pallas_call(
        attend_back_kernel,
        grid=(kv_heads, blocks),
        in_specs=[
            block_spec,
            pl.BlockSpec((ext, HEAD_WIDTH), lambda j, i: (0, j)),
            pl.BlockSpec((ext, HEAD_WIDTH), lambda j, i: (0, kv_heads + j)),
            pl.BlockSpec((None, 8, QROWS), lambda j, i: (i, 0, 0)),
            pl.BlockSpec((None, None, 8, QROWS), lambda j, i: (j, i, 0, 0)),
            block_spec,
            block_spec,
        ],
        out_specs=[
            block_spec,
            pl.BlockSpec((ext, HEAD_WIDTH), lambda j, i: (0, j)),
            pl.BlockSpec((ext, HEAD_WIDTH), lambda j, i: (0, j)),
        ],
        out_shape=[
            jax.ShapeDtypeStruct((rows, kv_heads * wide), bf16),
            jax.ShapeDtypeStruct((ext, kv_heads * HEAD_WIDTH), f32),
            jax.ShapeDtypeStruct((ext, kv_heads * HEAD_WIDTH), f32),
        ],
        cost_estimate=pl.CostEstimate(
            flops=10 * pairs * HEAD_WIDTH, bytes_accessed=12 << 20, transcendentals=pairs
        ),
        name="attend_back",
    )(queries, kv_ext, kv_ext, bounds, totals, outs, d_outs)


def norm_stats(rows):
    return lax.rsqrt(jnp.mean(rows * rows, axis=-1, keepdims=True) + norm_eps)


def norm_back(d_normed, rows, stats, gains):
    scaled = d_normed * gains
    unit = rows * stats
    return stats * (scaled - unit * jnp.mean(scaled * unit, axis=-1, keepdims=True))


def rotate(rows, cosine, sine):
    half = rows.shape[-1] // 2
    turned = jnp.concatenate([-rows[..., half:], rows[..., :half]], axis=-1)
    return rows * cosine + turned * sine


def rotate_back(d_rows, cosine, sine):
    half = d_rows.shape[-1] // 2
    turned = jnp.concatenate([d_rows[..., half:], -d_rows[..., :half]], axis=-1)
    return d_rows * cosine + turned * sine


def body(
    hidden_in,
    doc_lengths,
    pad_lengths,
    w_query,
    key_matrix,
    value_matrix,
    w_output,
    w_gate,
    w_up,
    w_down,
    attn_gain,
    mlp_gain,
    query_gain,
    key_gain,
    out_grad,
):
    dp_axes = ("q", "c")
    core = lax.axis_index("c")
    group = lax.axis_index("q") * 2 + core
    part = lax.axis_index("seq")
    groups = lax.axis_size("q") * 2
    parts = lax.axis_size("seq")
    tokens, width = hidden_in.shape
    group_rows = tokens * parts
    slice_rows = width // groups
    units = FEEDFWD_UNITS // 2
    q_cols = QUERY_HEADS * HEAD_WIDTH // parts
    kv_cols = KEY_VALUE_HEADS * HEAD_WIDTH // parts
    attn_cols = q_cols + 2 * kv_cols
    pack_cols = attn_cols + q_cols
    core_swap = [(0, 1), (1, 0)]

    hidden_all = lax.all_to_all(
        jnp.broadcast_to(hidden_in[None], (parts, tokens, width)), "seq", 0, 0, tiled=True
    ).reshape(group_rows, width)

    def head_cols(matrix, count):
        return lax.dynamic_slice_in_dim(matrix, part * count, count, 1)

    gain_cols = jnp.stack(
        [
            attn_gain,
            mlp_gain,
            jnp.pad(query_gain, (0, slice_rows - query_gain.shape[0])),
            jnp.pad(key_gain, (0, slice_rows - key_gain.shape[0])),
        ],
        axis=1,
    )
    packed = jnp.concatenate(
        [
            head_cols(w_query, q_cols),
            head_cols(key_matrix, kv_cols),
            head_cols(value_matrix, kv_cols),
            lax.dynamic_slice_in_dim(w_output, part * q_cols, q_cols, 0).T,
            jnp.pad(gain_cols, ((0, 0), (0, HEAD_WIDTH - gain_cols.shape[1]))),
        ],
        axis=1,
    ).astype(bf16)
    attn_w = lax.all_gather(packed, dp_axes, axis=0, tiled=True)
    w_qkv = attn_w[:, :attn_cols]
    w_out_t = attn_w[:, attn_cols:pack_cols]
    gains = attn_w[:, pack_cols : pack_cols + 4].astype(f32).T
    ga = gains[0]
    gm = gains[1]
    head_piece = query_gain.shape[0]
    gq = gains[2].reshape(groups, slice_rows)[:, :head_piece].reshape(HEAD_WIDTH)
    gk = gains[3].reshape(groups, slice_rows)[:, :head_piece].reshape(HEAD_WIDTH)

    def halves(matrix):
        return matrix.astype(bf16).reshape(slice_rows, 2, units).transpose(1, 0, 2)

    mlp_pack = jnp.concatenate([halves(w_gate), halves(w_up), halves(w_down.T)], axis=2)
    mlp_pack = lax.all_to_all(mlp_pack, "c", 0, 0, tiled=True).reshape(2 * slice_rows, 3 * units)
    mlp_w = lax.all_gather(mlp_pack, "q", axis=0, tiled=True)
    w_gu = mlp_w[:, : 2 * units]
    w_down_t = mlp_w[:, 2 * units :]
    grad_pair = jnp.concatenate([out_grad, lax.ppermute(out_grad, "c", core_swap)], axis=0)

    doc_ends = jnp.cumsum(doc_lengths)
    doc_starts = doc_ends - doc_lengths
    pad_starts = doc_ends - pad_lengths
    first = group * group_rows
    token = first + jnp.arange(group_rows, dtype=jnp.int32)
    inside = (token[:, None] >= doc_starts[None, :]) & (token[:, None] < doc_ends[None, :])
    start = jnp.sum(jnp.where(inside, doc_starts[None, :], 0), axis=1)
    pad_start = jnp.sum(jnp.where(inside, pad_starts[None, :], 0), axis=1)
    inv_freq = rope_base ** (-jnp.arange(HEAD_WIDTH // 2, dtype=f32) * 2.0 / HEAD_WIDTH)
    angles = (token - start).astype(f32)[:, None] * inv_freq[None, :]
    cosine = jnp.tile(jnp.cos(angles), (1, 2))[:, None, :]
    sine = jnp.tile(jnp.sin(angles), (1, 2))[:, None, :]
    blocks = group_rows // QROWS
    offset = (token // QROWS) * QROWS - WINDOW_TOKENS
    low = jnp.maximum(start, token - (WINDOW_TOKENS - 1)) - offset
    high = jnp.minimum(token, pad_start - 1) - offset
    bounds = jnp.pad(
        jnp.stack([low.reshape(blocks, QROWS), high.reshape(blocks, QROWS)], axis=1),
        ((0, 0), (0, 6), (0, 0)),
    )

    rows_all = hidden_all.astype(f32)
    stats_all = norm_stats(rows_all)
    normed_all = (rows_all * stats_all * ga).astype(bf16)
    qkv_proj = nn_dot(normed_all, w_qkv)
    qk_proj = qkv_proj[:, : q_cols + kv_cols].reshape(group_rows, -1, HEAD_WIDTH)
    qk_gain = jnp.concatenate(
        [
            jnp.broadcast_to(gq, (q_cols // HEAD_WIDTH, HEAD_WIDTH)),
            jnp.broadcast_to(gk, (kv_cols // HEAD_WIDTH, HEAD_WIDTH)),
        ],
        axis=0,
    )
    qk_stats = norm_stats(qk_proj)
    qk_rows = rotate(qk_proj * qk_stats * qk_gain, cosine, sine).astype(bf16)
    qk_rows = qk_rows.reshape(group_rows, q_cols + kv_cols)
    queries = qk_rows[:, :q_cols]
    kv_own = jnp.concatenate(
        [qk_rows[:, q_cols:], qkv_proj[:, q_cols + kv_cols :].astype(bf16)], axis=1
    )
    tail = lax.ppermute(
        kv_own[group_rows - WINDOW_TOKENS :], dp_axes, [(i, i + 1) for i in range(groups - 1)]
    )
    kv_ext = jnp.concatenate([tail, kv_own], axis=0)
    attn, totals = attend(queries, kv_ext, bounds)

    attn_part = nt_dot(attn, w_out_t).astype(bf16)
    attn_sum = lax.psum_scatter(attn_part, "seq", scatter_dimension=0, tiled=True)
    middle = hidden_in.astype(f32) + attn_sum.astype(f32)
    mid_stats = norm_stats(middle)
    normed_mid = (middle * mid_stats * gm).astype(bf16)

    mid_pair = jnp.concatenate([normed_mid, lax.ppermute(normed_mid, "c", core_swap)], axis=0)
    gate_up = nn_dot(mid_pair, w_gu)
    gate = gate_up[:, :units]
    up = gate_up[:, units:]
    sig = 1.0 / (1.0 + jnp.exp(-gate))
    mixed = (gate * sig * up).astype(bf16)
    d_mixed = nn_dot(grad_pair, w_down_t)
    d_gate = (d_mixed * up * sig * (1.0 + gate * (1.0 - sig))).astype(bf16)
    d_up = (d_mixed * gate * sig).astype(bf16)
    d_gate_up = jnp.concatenate([d_gate, d_up], axis=1)
    d_mid_part = nt_dot(d_gate_up, w_gu)
    d_mid_other = lax.ppermute(d_mid_part[tokens:].astype(bf16), "c", core_swap)
    d_normed_mid = d_mid_part[:tokens] + d_mid_other.astype(f32)
    d_middle = out_grad.astype(f32) + norm_back(d_normed_mid, middle, mid_stats, gm)
    d_mlp_gain = jnp.sum(d_normed_mid * middle * mid_stats, axis=0)
    d_proj = d_middle.astype(bf16)
    d_proj_all = lax.all_to_all(
        jnp.broadcast_to(d_proj[None], (parts, tokens, width)), "seq", 0, 0, tiled=True
    ).reshape(group_rows, width)

    out_part = nt_dot(mixed, w_down_t)
    out_other = lax.ppermute(out_part[tokens:].astype(bf16), "c", core_swap)
    output_act = (middle + out_part[:tokens] + out_other.astype(f32)).astype(bf16)

    mlp_grad = jnp.concatenate(
        [tn_dot(mid_pair, d_gate_up), tn_dot(grad_pair, mixed)], axis=1
    ).astype(bf16)
    mlp_grad = lax.psum_scatter(mlp_grad, "q", scatter_dimension=0, tiled=True)
    mlp_grad = lax.psum(mlp_grad, "seq")
    mlp_grad = lax.all_to_all(
        mlp_grad.reshape(2, slice_rows, 3 * units), "c", 0, 0, tiled=True
    )

    def unhalve(column):
        return (
            mlp_grad[:, :, column * units : (column + 1) * units]
            .transpose(1, 0, 2)
            .reshape(slice_rows, 2 * units)
            .astype(f32)
        )

    d_attn = nn_dot(d_proj_all, w_out_t).astype(bf16)
    w_out_grad = tn_dot(d_proj_all, attn)
    d_queries, d_k_ext, d_v_ext = attend_back(queries, kv_ext, bounds, totals, attn, d_attn)
    d_kv_ext = jnp.concatenate([d_k_ext, d_v_ext], axis=1)
    d_kv_tail = lax.ppermute(
        d_kv_ext[:WINDOW_TOKENS].astype(bf16), dp_axes, [(i + 1, i) for i in range(groups - 1)]
    )
    d_kv = d_kv_ext[WINDOW_TOKENS:]
    d_kv = jnp.concatenate(
        [
            d_kv[: group_rows - WINDOW_TOKENS],
            d_kv[group_rows - WINDOW_TOKENS :] + d_kv_tail.astype(f32),
        ],
        axis=0,
    ).astype(bf16)

    d_qk = jnp.concatenate([d_queries, d_kv[:, :kv_cols]], axis=1).astype(f32)
    d_qk = rotate_back(d_qk.reshape(group_rows, -1, HEAD_WIDTH), cosine, sine)
    d_qk_gain = jnp.sum(d_qk * qk_proj * qk_stats, axis=0)
    q_heads = q_cols // HEAD_WIDTH
    d_query_gain = jnp.sum(d_qk_gain[:q_heads], axis=0)
    d_key_gain = jnp.sum(d_qk_gain[q_heads:], axis=0)
    d_qk_proj = norm_back(d_qk, qk_proj, qk_stats, qk_gain).astype(bf16)
    d_qkv = jnp.concatenate(
        [d_qk_proj.reshape(group_rows, q_cols + kv_cols), d_kv[:, kv_cols:]], axis=1
    )
    d_in_part = nt_dot(d_qkv, w_qkv)
    d_attn_gain = jnp.sum(d_in_part * rows_all * stats_all, axis=0)
    d_normed_in = lax.psum_scatter(
        d_in_part.astype(bf16), "seq", scatter_dimension=0, tiled=True
    ).astype(f32)
    rows_own = hidden_in.astype(f32)
    in_grad = (
        d_middle + norm_back(d_normed_in, rows_own, norm_stats(rows_own), ga)
    ).astype(bf16)

    def spread(head_gain):
        return jnp.pad(
            head_gain.reshape(groups, head_piece), ((0, 0), (0, slice_rows - head_piece))
        ).reshape(width)

    gain_grads = jnp.stack(
        [d_attn_gain, d_mlp_gain, spread(d_query_gain), spread(d_key_gain)], axis=1
    )
    attn_grad = jnp.concatenate(
        [
            tn_dot(normed_all, d_qkv),
            w_out_grad,
            jnp.pad(gain_grads, ((0, 0), (0, HEAD_WIDTH - gain_grads.shape[1]))),
        ],
        axis=1,
    ).astype(bf16)
    by_core = attn_grad.reshape(groups // 2, 2, slice_rows, -1)
    keep = lax.dynamic_index_in_dim(by_core, core, 1, keepdims=False)
    give = lax.dynamic_index_in_dim(by_core, 1 - core, 1, keepdims=False)
    chip_sum = keep.astype(f32) + lax.ppermute(give, "c", core_swap).astype(f32)
    chip_sum = chip_sum.astype(bf16).reshape(width // 2, -1)
    attn_grad = lax.psum_scatter(chip_sum, "q", scatter_dimension=0, tiled=True)
    attn_grad = lax.all_gather(attn_grad, "seq", axis=0)
    attn_grad = attn_grad.astype(f32)

    def joined(begin, count):
        return (
            attn_grad[:, :, begin : begin + count].transpose(1, 0, 2).reshape(slice_rows, -1)
        )

    gain_sums = jnp.sum(attn_grad[:, :, pack_cols : pack_cols + 4], axis=0)
    return (
        output_act,
        in_grad,
        joined(0, q_cols),
        joined(q_cols, kv_cols),
        joined(q_cols + kv_cols, kv_cols),
        joined(attn_cols, q_cols).T,
        unhalve(0),
        unhalve(1),
        unhalve(2).T,
        gain_sums[:, 0],
        gain_sums[:, 1],
        gain_sums[:head_piece, 2],
        gain_sums[:head_piece, 3],
    )


def solution(mesh):
    groups, parts = mesh.devices.shape
    mesh = Mesh(mesh.devices.reshape(groups // 2, 2, parts), ("q", "c", "seq"))
    dp = ("q", "c")
    tokens = P(("q", "c", "seq"), None)
    rows = P(dp, None)
    cols = P(None, dp)
    in_specs = (
        tokens, P(), P(), rows, rows, rows, cols, rows, rows, cols,
        P(dp), P(dp), P(dp), P(dp), tokens,
    )
    out_specs = (
        tokens, tokens, rows, rows, rows, cols, rows, rows, cols, P(dp), P(dp), P(dp), P(dp),
    )
    return jax.shard_map(body, mesh=mesh, in_specs=in_specs, out_specs=out_specs, check_vma=False)
```

time: 1010 us -> 715 us (0.71); the launches traced: 995 us -> 711 us
  waiting for transfers between devices: 557 us -> 355 us
  matrix products: 126 us -> 49.4 us
  blocking collectives: 44.3 us -> 88.2 us
  Pallas kernels: 0 us -> 38.3 us
  starting transfers between devices: 44.5 us -> 13.2 us
  local copies, waits for them, and re-layouts: 126 us -> 95.8 us
  other arithmetic: 73.5 us -> 54.8 us
    psum x1, waiting for transfers between devices: 135 us -> 24.3 us  [body(): mlp_grad = lax.psum(mlp_grad, 'seq')]
    all_to_all x0 -> x3, blocking collectives: none -> 88.2 us  [the longest x1 63.6 us: body(): lax.all_to_all(jnp.broadcast_to(d_proj[None], (parts, tokens, width)), 's...]
    dot_general x49 -> x12, matrix products: 126 us -> 49.4 us  [the longest x4 16.7 us: tn_dot(): lax.dot_general(left, right, (((0,), (0,)), ((), ())), preferred_element_...]
    unnamed x13 -> x8, waiting for transfers between devices: 64.5 us -> 0.79 us
    all_to_all x8 -> x1, waiting for transfers between devices: 94.3 us -> 40.4 us  [body(): lax.all_to_all(jnp.broadcast_to(hidden_in[None], (parts, tokens, width)),...]
    pallas_call x0 -> x2, Pallas kernels: none -> 38.3 us  [the longest x1 24.8 us: attend_back(): pl.pallas_call(attend_back_kernel, grid=(kv_heads, blocks), in_specs=[blo...]
    reduce_scatter x1 -> x4, waiting for transfers between devices: 189 us -> 220 us  [the longest x1 98.1 us: body(): mlp_grad = lax.psum_scatter(mlp_grad, 'q', scatter_dimension=0, tiled=True)]
    all_to_all x8 -> x1, starting transfers between devices: 34.8 us -> 6.32 us  [body(): lax.all_to_all(jnp.broadcast_to(hidden_in[None], (parts, tokens, width)),...]
  transfers between devices with their start and end apart: 23 -> 16, of which waited for: 14 -> 10; matrix products, arithmetic and copies ran while one was open for 15% -> 10% of each run, Pallas kernels for 0% -> 0%
where the time goes in v1:
time: 715 us; the launch traced here: 711 us
  waiting for transfers between devices  355 us (50%)
  local copies, waits for them, and re-layouts  95.8 us (13%)
  blocking collectives  88.2 us (12%)
  other arithmetic  54.8 us (8%)
  matrix products  49.4 us (7%)
  Pallas kernels  38.3 us (5%)
  between operations  16.5 us (2%)
  starting transfers between devices  13.2 us (2%)
    reduce_scatter x1, waiting for transfers between devices, body(): mlp_grad = lax.psum_scatter(mlp_grad, 'q', scatter_dimension=0, tiled=True)  98.1 us
    reduce_scatter x1, waiting for transfers between devices, body(): lax.psum_scatter(d_in_part.astype(bf16), 'seq', scatter_dimension=0, tile...  81.8 us
    all_gather x1, waiting for transfers between devices, body(): mlp_w = lax.all_gather(mlp_pack, 'q', axis=0, tiled=True)  65.1 us
    all_to_all x1, blocking collectives, body(): lax.all_to_all(jnp.broadcast_to(d_proj[None], (parts, tokens, width)), 's...  63.6 us
    all_to_all x1, waiting for transfers between devices, body(): lax.all_to_all(jnp.broadcast_to(hidden_in[None], (parts, tokens, width)),...  40.4 us
    pallas_call x1, Pallas kernels, attend_back(): pl.pallas_call(attend_back_kernel, grid=(kv_heads, blocks), in_specs=[blo...  24.8 us
    psum x1, waiting for transfers between devices, body(): mlp_grad = lax.psum(mlp_grad, 'seq')  24.3 us
    reduce_scatter x1, waiting for transfers between devices, body(): lax.psum_scatter(attn_part, 'seq', scatter_dimension=0, tiled=True)  24 us
  transfers between devices with their start and end apart: 16, of which 10 were waited for; matrix products, arithmetic and copies ran while one was open for 10% of the time, Pallas kernels for 0%

profile of v1, /device:TPU:0, one launch (start us, length us, event | category | flops | bytes accessed | tf_op | source)
XLA Modules:
  0.0 711.4 jit_solution(14064649840659313479)
XLA Ops:
  17.2 6.3 all-to-all-start
  31.3 40.4 %all-to-all-done = bf16[4,256,1024]{2,1,0:T(8,128)(2,1)S(1)} async-done(((bf16[4,256,1024]{2,1,0:T(8,128)(2,1)}), bf16[4,256,1024]{2,1,0:T(8,128)(2,1)S(1)}, u32[]{:S(2)}, u32[]{:S(2)}) %all-to-all-start) | async-done | bytes 2097184 | tf_op jit(solution)/shard_map/all_to_all | solution.py:237
  92.3 3.6 copy.162
  95.8 5.5 add_convert_fusion
  106.5 13.5 %attend.1 = (bf16[1024,512]{1,0:T(8,128)(2,1)}, f32[2,4,8,256]{3,2,1,0:T(8,128)}) custom-call(bf16[1024,512]{1,0:T(8,128)(2,1)} %slice.204.q_ref, bf16[2048,512]{1,0:T(8,128)(2,1)} %maximum_maximum_fusion.k_ref.v_ref, bf16[2048,512]{1,0:T(8,128)(2,1)} %maximum_maximum_fusion.k_ref.v_ref, s32[4,8,256]{2,1,0:T(8,128)} %pad.35.bounds_ref), custom_call_target="tpu_custom_call" | custom-call | flops 2684354560 | bytes 4194304 | tf_op jit(solution)/shard_map/attend/pallas_call | solution.py:78
  120.0 4.1 convolution_convert_fusion.2
  133.4 17.7 %all_to_all.20 = bf16[2,128,4608]{1,2,0:T(8,128)(2,1)} all-to-all(bf16[2,128,4608]{1,2,0:T(8,128)(2,1)S(1)} %pad_maximum_fusion.3), channel_id=1, replica_groups=mesh['q'=4,'c'=2,'seq'=4] {'c'}, dimensions={0} | all-to-all | bytes 4718592 | tf_op jit(solution)/shard_map/all_to_all | solution.py:277
  151.1 4.4 copy.168
  155.7 24.0 %reduce-scatter.5.cloned.1.call-done = bf16[256,1024]{1,0:T(8,128)(2,1)} async-done(((bf16[1024,1024]{1,0:T(8,128)(2,1)}), bf16[256,1024]{1,0:T(8,128)(2,1)}) %reduce-scatter.5.cloned.1.call-update) | async-done | bytes 524304 | tf_op jit(solution)/shard_map/reduce_scatter | solution.py:330
  187.2 65.1 %all-gather.7.cloned.1.call-done = bf16[1024,4608]{1,0:T(8,128)(2,1)} async-done(((bf16[256,4608]{1,0:T(8,128)(2,1)}), bf16[1024,4608]{1,0:T(8,128)(2,1)}) %all-gather.7.cloned.1.call-update) | async-done | bytes 9437200 | tf_op jit(solution)/shard_map/all_gather | solution.py:278
  252.3 5.9 fusion.2
  258.2 4.2 multiply_convert_fusion.2
  275.3 63.6 %all_to_all.21 = bf16[4,256,1024]{1,2,0:T(8,128)(2,1)} all-to-all(bf16[4,256,1024]{1,2,0:T(8,128)(2,1)S(1)} %broadcast_in_dim.29), channel_id=1, replica_groups=mesh['q'=4,'c'=2,'seq'=4] {'seq'}, dimensions={0} | all-to-all | bytes 4194304 | tf_op jit(solution)/shard_map/all_to_all | solution.py:351
  338.9 4.0 copy.170
  343.0 4.1 convolution_convert_fusion.4.d_out_ref
  347.1 24.8 %attend_back.1 = (bf16[1024,512]{1,0:T(8,128)(2,1)}, f32[2048,256]{1,0:T(8,128)}, f32[2048,256]{1,0:T(8,128)}) custom-call(bf16[1024,512]{1,0:T(8,128)(2,1)} %slice.204.q_ref, bf16[2048,512]{1,0:T(8,128)(2,1)} %maximum_maximum_fusion.k_ref.v_ref, bf16[2048,512]{1,0:T(8,128)(2,1)} %maximum_maximum_fusion.k_ref.v_ref, s32[4,8,256]{2,1,0:T(8,128)} %pad.35.bounds_ref, ...), custom_call_target="tpu_custom_call" | custom-call | flops 6710886400 | bytes 12582912 | tf_op jit(solution)/shard_map/attend_back/pallas_call | solution.py:153
  378.8 4.0 copy.190
  382.8 4.0 copy.177
  386.7 4.2 convolution_convert_fusion.3
  396.2 3.6 copy.172
  411.4 3.7 copy.174
  415.1 6.9 multiply_reduce_fusion
  422.3 6.8 fusion.8
  429.3 3.8 fusion.17
  444.6 3.7 convolution_convert_fusion.1
  448.3 4.9 convolution_convert_fusion
  453.3 4.7 pad_maximum_fusion
  458.8 16.0 %reduce-scatter.9.cloned.1.call-done = bf16[128,1664]{1,0:T(8,128)(2,1)} async-done(((bf16[512,1664]{1,0:T(8,128)(2,1)}), bf16[128,1664]{1,0:T(8,128)(2,1)}) %reduce-scatter.9.cloned.1.call-update) | async-done | bytes 426000 | tf_op jit(solution)/shard_map/reduce_scatter | solution.py:433
  474.9 98.1 %reduce-scatter.11.cloned.1.call-done = bf16[256,4608]{1,0:T(8,128)(2,1)} async-done(((bf16[1024,4608]{1,0:T(8,128)(2,1)}), bf16[256,4608]{1,0:T(8,128)(2,1)}) %reduce-scatter.11.cloned.1.call-update) | async-done | bytes 2359312 | tf_op jit(solution)/shard_map/reduce_scatter | solution.py:362
  573.0 81.8 %reduce-scatter.7.cloned.1.call-done = bf16[256,1024]{1,0:T(8,128)(2,1)} async-done(((bf16[1024,1024]{1,0:T(8,128)(2,1)}), bf16[256,1024]{1,0:T(8,128)(2,1)}) %reduce-scatter.7.cloned.1.call-update) | async-done | bytes 524304 | tf_op jit(solution)/shard_map/reduce_scatter | solution.py:404
  668.1 24.3 %all-reduce.9.cloned.1.call-done = bf16[2,128,4608]{2,1,0:T(8,128)(2,1)} async-done(((bf16[2,128,4608]{2,1,0:T(8,128)(2,1)}), bf16[2,128,4608]{2,1,0:T(8,128)(2,1)}) %all-reduce.9.cloned.1.call-update) | async-done | bytes 2359312 | tf_op jit(solution)/shard_map/psum | solution.py:363
  692.4 6.8 all_to_all.22
  (225 shorter events, 126.2 us)
Async XLA Ops:
  8.0 64.2 %all-gather.5.cloned.1.call-start = ((), (), s32[]{:S(2)}) async-start(), calls=%async_computation.8 | async-start | bytes 3833856 | tf_op jit(solution)/shard_map/all_gather | solution.py:263
  14.5 9.0 %copy-start.28 = (s32[9]{0:T(128)S(1)}, s32[9]{0:T(128)}, u32[]{:S(2)}) copy-start(s32[9]{0:T(128)} %param.16) | copy-start | bytes 112
  14.5 9.2 %copy-start.29 = (s32[9]{0:T(128)S(1)}, s32[9]{0:T(128)}, u32[]{:S(2)}) copy-start(s32[9]{0:T(128)} %param.17) | copy-start | bytes 112
  17.2 54.5 %all-to-all-start = ((bf16[4,256,1024]{2,1,0:T(8,128)(2,1)}), bf16[4,256,1024]{2,1,0:T(8,128)(2,1)S(1)}, u32[]{:S(2)}, u32[]{:S(2)}) async-start(bf16[4,256,1024]{2,1,0:T(8,128)(2,1)} %broadcast_in_dim.24), calls=%async_computation | async-start | bytes 4194304 | tf_op jit(solution)/shard_map/all_to_all | solution.py:237
  23.5 156.3 %reduce-scatter.5.cloned.1.call-start = ((), (), s32[]{:S(2)}) async-start(), calls=%async_computation.9 | async-start | bytes 2621440 | tf_op jit(solution)/shard_map/reduce_scatter | solution.py:330
  95.8 5.5 copy-start.17
  101.5 3.6 collective-permute-start
  124.1 128.2 %all-gather.7.cloned.1.call-start = ((), (), s32[]{:S(2)}) async-start(), calls=%async_computation.10 | async-start | bytes 11796480 | tf_op jit(solution)/shard_map/all_gather | solution.py:278
  155.5 319.3 %reduce-scatter.9.cloned.1.call-start = ((), (), s32[]{:S(2)}) async-start(), calls=%async_computation.12 | async-start | bytes 2129920 | tf_op jit(solution)/shard_map/reduce_scatter | solution.py:433
  155.5 29.8 %collective-permute-start.3 = (bf16[256,1024]{1,0:T(8,128)(2,1)}, bf16[256,1024]{1,0:T(8,128)(2,1)}, u32[]{:S(2)}, u32[]{:S(2)}) collective-permute-start(bf16[256,1024]{1,0:T(8,128)(2,1)} %param.29), channel_id=1, source_target_pairs={{0,4},{4,0},{1,5},{5,1},{2,6},{6,2},{3,7},{7,3},{8,12},{12,8},{9,1... | collective-permute-start | bytes 1572872 | tf_op jit(solution)/shard_map/ppermute | solution.py:281
  183.5 3.8 collective-permute-start.1
  252.3 5.9 copy-start.31
  262.5 3.5 copy-start.33
  262.5 3.6 copy-start.32
  266.1 2.6 collective-permute-start.4
  268.1 2.1 collective-permute-start.2
  377.5 13.5 %collective-permute-start.5 = (bf16[1024,512]{1,0:T(8,128)(2,1)}, bf16[1024,512]{1,0:T(8,128)(2,1)}, u32[]{:S(2)}, u32[]{:S(2)}) collective-permute-start(bf16[1024,512]{1,0:T(8,128)(2,1)} %slice.298), channel_id=1, source_target_pairs={{4,0},{8,4},{12,8},{16,12},{20,16},{24,20},{28,24},{5,1},{9,5},{13... | collective-permute-start | bytes 3145736 | tf_op jit(solution)/shard_map/ppermute | solution.py:380
  386.7 4.2 copy-start.11
  411.4 3.7 copy-start.3
  422.2 7.0 copy-start.20
  422.3 7.0 copy-start.27
  429.3 3.9 copy-start.23
  434.8 6.3 collective-permute-start.6
  444.3 4.0 copy-start.26
  444.3 4.0 copy-start.34
  444.3 128.7 %reduce-scatter.11.cloned.1.call-start = ((), (), s32[]{:S(2)}) async-start(), calls=%async_computation.13 | async-start | bytes 11796480 | tf_op jit(solution)/shard_map/reduce_scatter | solution.py:362
  444.6 3.7 copy-start.36
  458.0 196.9 %copy-start.5 = (bf16[256,1024]{1,0:T(8,128)(2,1)S(1)}, bf16[256,1024]{1,0:T(8,128)(2,1)}, u32[]{:S(2)}) copy-start(bf16[256,1024]{1,0:T(8,128)(2,1)} %param.15) | copy-start | bytes 1572868
  458.0 198.3 %copy-start.19 = (f32[256,1024]{1,0:T(8,128)S(1)}, f32[256,1024]{1,0:T(8,128)}, u32[]{:S(2)}) copy-start(f32[256,1024]{1,0:T(8,128)} %get-tuple-element.35) | copy-start | bytes 3145732
  458.0 196.9 %reduce-scatter.7.cloned.1.call-start = ((), (), s32[]{:S(2)}) async-start(), calls=%async_computation.11 | async-start | bytes 2621440 | tf_op jit(solution)/shard_map/reduce_scatter | solution.py:404
  458.7 199.7 %all-gather.9.cloned.1.call-start = ((), (), s32[]{:S(2)}) async-start(), calls=%async_computation.15 | async-start | bytes 2129920 | tf_op jit(solution)/shard_map/all_gather | solution.py:434
  474.8 217.5 %all-reduce.9.cloned.1.call-start = ((), (), s32[]{:S(2)}) async-start(), calls=%async_computation.14 | async-start | bytes 4718592 | tf_op jit(solution)/shard_map/psum | solution.py:363
  (21 other events, 46.0 us)
Sparse Core Ops, SparseCore 0:
  14.6 36.6 all-gather.4
  124.3 55.4 reduce-scatter.4
  475.0 39.2 all-gather.8
  573.1 119.1 all-reduce.8
Sparse Core Ops, SparseCore 1:
  155.6 96.7 all-gather.6
  444.4 30.4 reduce-scatter.8
  478.1 94.8 reduce-scatter.10
  575.4 79.4 reduce-scatter.6

commit v2 on v1

v2 whole, which is shorter than its diff:
```python
import functools

import jax
import jax.numpy as jnp
from jax import lax
from jax.experimental import pallas as pl
from jax.experimental.pallas import tpu as pltpu
from jax.sharding import Mesh, PartitionSpec as P

QUERY_HEADS = 16
KEY_VALUE_HEADS = 8
HEAD_WIDTH = 128
FEEDFWD_UNITS = 3072
WINDOW_TOKENS = 1024
QROWS = 256
GROUP = QUERY_HEADS // KEY_VALUE_HEADS
TAIL_CHUNKS = WINDOW_TOKENS // QROWS

norm_eps = 1e-06
rope_base = 1000000.0
score_scale = HEAD_WIDTH**-0.5
log2_e = 1.4426950408889634
bf16 = jnp.bfloat16
f32 = jnp.float32
dp_axes = ("q", "c")
core_swap = [(0, 1), (1, 0)]


def nt_dot(left, right):
    return lax.dot_general(left, right, (((1,), (1,)), ((), ())), preferred_element_type=f32)


def tn_dot(left, right):
    return lax.dot_general(left, right, (((0,), (0,)), ((), ())), preferred_element_type=f32)


def nn_dot(left, right):
    return jnp.dot(left, right, preferred_element_type=f32)


def shape_of(dims, kind):
    return jax.ShapeDtypeStruct(dims, kind)


def cost(flops, moved, exps=0):
    return pl.CostEstimate(flops=int(flops), bytes_accessed=int(moved), transcendentals=int(exps))


def norm_stats(rows):
    return lax.rsqrt(jnp.mean(rows * rows, axis=-1, keepdims=True) + norm_eps)


def norm_back(d_normed, rows, stats, gains):
    scaled = d_normed * gains
    unit = rows * stats
    return stats * (scaled - unit * jnp.mean(scaled * unit, axis=-1, keepdims=True))


def pack_attn_kernel(part_ref, wq_ref, wk_ref, wv_ref, wo_ref, gains_ref, out_ref):
    column = 0
    for piece in (
        wq_ref[...].astype(bf16),
        wk_ref[...].astype(bf16),
        wv_ref[...].astype(bf16),
        wo_ref[...].T.astype(bf16),
        gains_ref[...].astype(bf16),
    ):
        out_ref[:, column : column + piece.shape[1]] = piece
        column += piece.shape[1]


def pack_attn(part, parts, w_query, key_matrix, value_matrix, w_output, gain_cols):
    rows = w_query.shape[0]
    q_cols = w_query.shape[1] // parts
    kv_cols = key_matrix.shape[1] // parts
    total = 2 * q_cols + 2 * kv_cols + HEAD_WIDTH
    return pl.pallas_call(
        pack_attn_kernel,
        grid_spec=pltpu.PrefetchScalarGridSpec(
            num_scalar_prefetch=1,
            grid=(1,),
            in_specs=[
                pl.BlockSpec((rows, q_cols), lambda i, p: (0, p[0])),
                pl.BlockSpec((rows, kv_cols), lambda i, p: (0, p[0])),
                pl.BlockSpec((rows, kv_cols), lambda i, p: (0, p[0])),
                pl.BlockSpec((q_cols, rows), lambda i, p: (p[0], 0)),
                pl.BlockSpec((rows, HEAD_WIDTH), lambda i, p: (0, 0)),
            ],
            out_specs=pl.BlockSpec((rows, total), lambda i, p: (0, 0)),
        ),
        out_shape=shape_of((rows, total), bf16),
        cost_estimate=cost(0, rows * total * 6),
        name="pack_attn",
    )(part, w_query, key_matrix, value_matrix, w_output, gain_cols)


def pack_mlp_kernel(core_ref, wg_ref, wu_ref, wd_ref, own_ref, give_ref):
    units = wg_ref.shape[1]

    def fill(out_ref):
        out_ref[:, :units] = wg_ref[...].astype(bf16)
        out_ref[:, units : 2 * units] = wu_ref[...].astype(bf16)
        out_ref[:, 2 * units :] = wd_ref[...].T.astype(bf16)

    @pl.when(pl.program_id(0) == 0)
    def first():
        fill(give_ref)

    @pl.when(pl.program_id(0) == 1)
    def second():
        fill(own_ref)


def pack_mlp(core, w_gate, w_up, w_down):
    rows = w_gate.shape[0]
    units = w_gate.shape[1] // 2
    half = lambda i, c: (c[0] + 1 - i) % 2
    return pl.pallas_call(
        pack_mlp_kernel,
        grid_spec=pltpu.PrefetchScalarGridSpec(
            num_scalar_prefetch=1,
            grid=(2,),
            in_specs=[
                pl.BlockSpec((rows, units), lambda i, c: (0, half(i, c))),
                pl.BlockSpec((rows, units), lambda i, c: (0, half(i, c))),
                pl.BlockSpec((units, rows), lambda i, c: (half(i, c), 0)),
            ],
            out_specs=[
                pl.BlockSpec((rows, 3 * units), lambda i, c: (c[0], 0)),
                pl.BlockSpec((rows, 3 * units), lambda i, c: (0, 0)),
            ],
        ),
        out_shape=[shape_of((2 * rows, 3 * units), bf16), shape_of((rows, 3 * units), bf16)],
        cost_estimate=cost(0, rows * units * 36),
        name="pack_mlp",
    )(core, w_gate, w_up, w_down)


def unpack_mlp_kernel(core_ref, own_ref, got_ref, gate_ref, up_ref, down_ref):
    units = gate_ref.shape[1]

    def fill(in_ref):
        gate_ref[...] = in_ref[:, :units].astype(f32)
        up_ref[...] = in_ref[:, units : 2 * units].astype(f32)
        down_ref[...] = in_ref[:, 2 * units :].astype(f32).T

    @pl.when(pl.program_id(0) == 0)
    def first():
        fill(own_ref)

    @pl.when(pl.program_id(0) == 1)
    def second():
        fill(got_ref)


def unpack_mlp(core, sums, got):
    rows = got.shape[0]
    units = got.shape[1] // 3
    half = lambda i, c: (c[0] + i) % 2
    return pl.pallas_call(
        unpack_mlp_kernel,
        grid_spec=pltpu.PrefetchScalarGridSpec(
            num_scalar_prefetch=1,
            grid=(2,),
            in_specs=[
                pl.BlockSpec((rows, 3 * units), lambda i, c: (c[0], 0)),
                pl.BlockSpec((rows, 3 * units), lambda i, c: (0, 0)),
            ],
            out_specs=[
                pl.BlockSpec((rows, units), lambda i, c: (0, half(i, c))),
                pl.BlockSpec((rows, units), lambda i, c: (0, half(i, c))),
                pl.BlockSpec((units, rows), lambda i, c: (half(i, c), 0)),
            ],
        ),
        out_shape=[
            shape_of((rows, 2 * units), f32),
            shape_of((rows, 2 * units), f32),
            shape_of((2 * units, rows), f32),
        ],
        cost_estimate=cost(0, rows * units * 36),
        name="unpack_mlp",
    )(core, sums, got)


def unpack_attn_kernel(in_ref, wq_ref, wk_ref, wv_ref, wo_ref):
    column = 0
    for out_ref in (wq_ref, wk_ref, wv_ref):
        count = out_ref.shape[1]
        out_ref[...] = in_ref[:, column : column + count].astype(f32)
        column += count
    wo_ref[...] = in_ref[:, column : column + wo_ref.shape[0]].astype(f32).T


def unpack_attn(gathered, q_cols, kv_cols):
    parts, rows, total = gathered.shape
    return pl.pallas_call(
        unpack_attn_kernel,
        grid=(parts,),
        in_specs=[pl.BlockSpec((None, rows, total), lambda i: (i, 0, 0))],
        out_specs=[
            pl.BlockSpec((rows, q_cols), lambda i: (0, i)),
            pl.BlockSpec((rows, kv_cols), lambda i: (0, i)),
            pl.BlockSpec((rows, kv_cols), lambda i: (0, i)),
            pl.BlockSpec((q_cols, rows), lambda i: (i, 0)),
        ],
        out_shape=[
            shape_of((rows, parts * q_cols), f32),
            shape_of((rows, parts * kv_cols), f32),
            shape_of((rows, parts * kv_cols), f32),
            shape_of((parts * q_cols, rows), f32),
        ],
        cost_estimate=cost(0, parts * rows * total * 6),
        name="unpack_attn",
    )(gathered)


def pick(refs, scratch):
    for k, ref in enumerate(refs):

        @pl.when(pl.program_id(0) == k)
        def take(ref=ref):
            scratch[...] = ref[...]


def turn(rows):
    half = HEAD_WIDTH // 2
    return jnp.concatenate([rows[:, half:], rows[:, :half]], axis=1)


def project_kernel(parts, q_cols, kv_cols, part_ref, *refs):
    blocks = refs[:parts]
    w_ref, ga_ref, gqk_ref, cos_ref, sin_ref, normed_ref, q_ref, kv_ref, proj_ref, x_ref = refs[parts:]
    pick(blocks, x_ref)
    rows = x_ref[...].astype(f32)
    normed = (rows * norm_stats(rows) * ga_ref[...]).astype(bf16)
    normed_ref[...] = normed
    cosine = cos_ref[...]
    sine = sin_ref[...]
    qk_cols = q_cols + kv_cols
    proj = nn_dot(normed, w_ref[...])
    proj_ref[...] = proj[:, :qk_cols]
    kv_ref[:, kv_cols:] = proj[:, qk_cols:].astype(bf16)
    for column in range(0, qk_cols, HEAD_WIDTH):
        head = proj[:, column : column + HEAD_WIDTH]
        gain = gqk_ref[0:1, :] if column < q_cols else gqk_ref[1:2, :]
        head = head * norm_stats(head) * gain
        head = (head * cosine + turn(head) * sine).astype(bf16)
        if column < q_cols:
            q_ref[:, column : column + HEAD_WIDTH] = head
        else:
            kv_ref[:, column - q_cols : column - q_cols + HEAD_WIDTH] = head


def project(part, blocks, attn_w, ga, gqk, cosine, sine, q_cols, kv_cols):
    parts = len(blocks)
    tokens, width = blocks[0].shape
    attn_cols = q_cols + 2 * kv_cols
    place = lambda k, p: ((p[0] + parts - k) % parts, 0)
    fixed = lambda k, p: (0, 0)
    rows = parts * tokens
    return pl.pallas_call(
        functools.partial(project_kernel, parts, q_cols, kv_cols),
        grid_spec=pltpu.PrefetchScalarGridSpec(
            num_scalar_prefetch=1,
            grid=(parts,),
            in_specs=[pl.BlockSpec((tokens, width), fixed)] * parts
            + [
                pl.BlockSpec((width, attn_cols), fixed),
                pl.BlockSpec((1, width), fixed),
                pl.BlockSpec((2, HEAD_WIDTH), fixed),
                pl.BlockSpec((tokens, HEAD_WIDTH), place),
                pl.BlockSpec((tokens, HEAD_WIDTH), place),
            ],
            out_specs=[
                pl.BlockSpec((tokens, width), place),
                pl.BlockSpec((tokens, q_cols), place),
                pl.BlockSpec((tokens, 2 * kv_cols), place),
                pl.BlockSpec((tokens, q_cols + kv_cols), place),
            ],
            scratch_shapes=[pltpu.VMEM((tokens, width), bf16)],
        ),
        out_shape=[
            shape_of((rows, width), bf16),
            shape_of((rows, q_cols), bf16),
            shape_of((rows, 2 * kv_cols), bf16),
            shape_of((rows, q_cols + kv_cols), f32),
        ],
        cost_estimate=cost(2 * rows * width * attn_cols, 12 << 20),
        name="project",
    )(part, *blocks, attn_w, ga, gqk, cosine, sine)


def project_back_kernel(
    parts, tail_from, q_cols, kv_cols, part_ref, dq_ref, dkv_ref, tail_ref, proj_ref,
    w_ref, gqk_ref, cos_ref, sin_ref, *refs
):
    blocks = refs[:parts]
    outs = refs[parts : 2 * parts]
    dqkv_ref, gain_ref, head_gain_ref, x_ref = refs[2 * parts :]
    step = pl.program_id(0)
    pick(blocks, x_ref)
    block = (part_ref[0] + step) % parts

    @pl.when(step == 0)
    def clear():
        gain_ref[...] = jnp.zeros_like(gain_ref)
        head_gain_ref[...] = jnp.zeros_like(head_gain_ref)

    cosine = cos_ref[...]
    sine = sin_ref[...]
    has_tail = jnp.where(block >= tail_from, 1.0, 0.0)
    dkv = (dkv_ref[...] + tail_ref[...].astype(f32) * has_tail).astype(bf16)
    dqkv_ref[:, q_cols + kv_cols :] = dkv[:, kv_cols:]
    for column in range(0, q_cols + kv_cols, HEAD_WIDTH):
        index = 0 if column < q_cols else 1
        if index == 0:
            d_head = dq_ref[:, column : column + HEAD_WIDTH].astype(f32)
        else:
            d_head = dkv[:, column - q_cols : column - q_cols + HEAD_WIDTH].astype(f32)
        d_head = d_head * cosine + turn(d_head * sine)
        head = proj_ref[:, column : column + HEAD_WIDTH]
        stats = norm_stats(head)
        unit = head * stats
        head_gain_ref[index : index + 1, :] += jnp.sum(d_head * unit, axis=0, keepdims=True)
        scaled = d_head * gqk_ref[index : index + 1, :]
        d_proj = stats * (scaled - unit * jnp.mean(scaled * unit, axis=-1, keepdims=True))
        dqkv_ref[:, column : column + HEAD_WIDTH] = d_proj.astype(bf16)
    d_in = nt_dot(dqkv_ref[...], w_ref[...])
    rows = x_ref[...].astype(f32)
    gain_ref[0:1, :] += jnp.sum(d_in * (rows * norm_stats(rows)), axis=0, keepdims=True)
    d_in = d_in.astype(bf16)
    for k, out_ref in enumerate(outs):

        @pl.when(step == k)
        def put(out_ref=out_ref):
            out_ref[...] = d_in


def project_back(part, blocks, dq, dkv, tail, proj, attn_w, gqk, cosine, sine):
    parts = len(blocks)
    rows, q_cols = dq.shape
    kv_cols = dkv.shape[1] // 2
    tokens, width = blocks[0].shape
    attn_cols = q_cols + 2 * kv_cols
    tail_from = (rows - WINDOW_TOKENS) // tokens
    place = lambda k, p: ((p[0] + k) % parts, 0)
    tail_place = lambda k, p: (jnp.maximum((p[0] + k) % parts - tail_from, 0), 0)
    fixed = lambda k, p: (0, 0)
    return pl.pallas_call(
        functools.partial(project_back_kernel, parts, tail_from, q_cols, kv_cols),
        grid_spec=pltpu.PrefetchScalarGridSpec(
            num_scalar_prefetch=1,
            grid=(parts,),
            in_specs=[
                pl.BlockSpec((tokens, q_cols), place),
                pl.BlockSpec((tokens, 2 * kv_cols), place),
                pl.BlockSpec((tokens, 2 * kv_cols), tail_place),
                pl.BlockSpec((tokens, q_cols + kv_cols), place),
                pl.BlockSpec((width, attn_cols), fixed),
                pl.BlockSpec((2, HEAD_WIDTH), fixed),
                pl.BlockSpec((tokens, HEAD_WIDTH), place),
                pl.BlockSpec((tokens, HEAD_WIDTH), place),
            ]
            + [pl.BlockSpec((tokens, width), fixed)] * parts,
            out_specs=[pl.BlockSpec((tokens, width), fixed)] * parts
            + [
                pl.BlockSpec((tokens, attn_cols), place),
                pl.BlockSpec((8, width), fixed),
                pl.BlockSpec((8, HEAD_WIDTH), fixed),
            ],
            scratch_shapes=[pltpu.VMEM((tokens, width), bf16)],
        ),
        out_shape=[shape_of((tokens, width), bf16)] * parts
        + [
            shape_of((rows, attn_cols), bf16),
            shape_of((8, width), f32),
            shape_of((8, HEAD_WIDTH), f32),
        ],
        cost_estimate=cost(2 * rows * width * attn_cols, 16 << 20),
        name="project_back",
    )(part, dq, dkv, tail, proj, attn_w, gqk, cosine, sine, *blocks)


def out_proj_kernel(parts, part_ref, attn_ref, w_ref, *outs):
    result = nt_dot(attn_ref[...], w_ref[...]).astype(bf16)
    for k, out_ref in enumerate(outs):

        @pl.when(pl.program_id(0) == k)
        def put(out_ref=out_ref):
            out_ref[...] = result


def out_proj(part, parts, attn, attn_w, w_block):
    rows, q_cols = attn.shape
    width = attn_w.shape[0]
    tokens = rows // parts
    return pl.pallas_call(
        functools.partial(out_proj_kernel, parts),
        grid_spec=pltpu.PrefetchScalarGridSpec(
            num_scalar_prefetch=1,
            grid=(parts,),
            in_specs=[
                pl.BlockSpec((tokens, q_cols), lambda k, p: ((p[0] + k) % parts, 0)),
                pl.BlockSpec((width, q_cols), lambda k, p: (0, w_block)),
            ],
            out_specs=[pl.BlockSpec((tokens, width), lambda k, p: (0, 0))] * parts,
        ),
        out_shape=[shape_of((tokens, width), bf16)] * parts,
        cost_estimate=cost(2 * rows * width * q_cols, 4 << 20),
        name="out_proj",
    )(part, attn, attn_w)


def out_proj_back_kernel(parts, part_ref, *refs):
    blocks = refs[:parts]
    attn_ref, w_ref, d_attn_ref, d_w_ref, x_ref = refs[parts:]
    pick(blocks, x_ref)
    d_proj = x_ref[...]
    d_attn_ref[...] = nn_dot(d_proj, w_ref[...]).astype(bf16)

    @pl.when(pl.program_id(0) == 0)
    def clear():
        d_w_ref[...] = jnp.zeros_like(d_w_ref)

    d_w_ref[...] += tn_dot(d_proj, attn_ref[...])


def out_proj_back(part, blocks, attn, attn_w, w_block):
    parts = len(blocks)
    rows, q_cols = attn.shape
    tokens, width = blocks[0].shape
    place = lambda k, p: ((p[0] + parts - k) % parts, 0)
    fixed = lambda k, p: (0, 0)
    return pl.pallas_call(
        functools.partial(out_proj_back_kernel, parts),
        grid_spec=pltpu.PrefetchScalarGridSpec(
            num_scalar_prefetch=1,
            grid=(parts,),
            in_specs=[pl.BlockSpec((tokens, width), fixed)] * parts
            + [
                pl.BlockSpec((tokens, q_cols), place),
                pl.BlockSpec((width, q_cols), lambda k, p: (0, w_block)),
            ],
            out_specs=[
                pl.BlockSpec((tokens, q_cols), place),
                pl.BlockSpec((width, q_cols), fixed),
            ],
            scratch_shapes=[pltpu.VMEM((tokens, width), bf16)],
        ),
        out_shape=[shape_of((rows, q_cols), bf16), shape_of((width, q_cols), f32)],
        cost_estimate=cost(4 * rows * width * q_cols, 8 << 20),
        name="out_proj_back",
    )(part, *blocks, attn, attn_w)


def chunk_mask(bounds_ref, block, chunk):
    low = bounds_ref[block, 0:1, :]
    high = bounds_ref[block, 1:2, :]
    key = lax.broadcasted_iota(jnp.int32, (QROWS, QROWS), 0) + chunk * QROWS
    mask = (key >= low) & (key <= high)
    if chunk == TAIL_CHUNKS:
        own = lax.broadcasted_iota(jnp.int32, (QROWS, QROWS), 1) + WINDOW_TOKENS
        mask = mask | (key == own)
    return mask


def head_span(g):
    return slice(g * HEAD_WIDTH, (g + 1) * HEAD_WIDTH)


def chunk_forward(q_ref, k_ref, v_ref, bounds_ref, block, chunk, row, sums, outs):
    here = slice(block * QROWS, (block + 1) * QROWS)
    there = slice(row, row + QROWS)
    mask = chunk_mask(bounds_ref, block, chunk)
    keys = k_ref[there, :]
    values = v_ref[there, :]
    for g in range(GROUP):
        scores = nt_dot(keys, q_ref[here, head_span(g)])
        weights = jnp.where(mask, jnp.exp2(scores * (score_scale * log2_e)), 0.0)
        sums[g] = sums[g] + jnp.sum(weights, axis=0, keepdims=True)
        outs[g] = outs[g] + tn_dot(values, weights.astype(bf16))


def attend_own_kernel(q_ref, k_ref, v_ref, bounds_ref, out_ref, total_ref):
    for block in range(q_ref.shape[0] // QROWS):
        here = slice(block * QROWS, (block + 1) * QROWS)
        sums = [jnp.zeros((1, QROWS), f32) for g in range(GROUP)]
        outs = [jnp.zeros((HEAD_WIDTH, QROWS), f32) for g in range(GROUP)]
        for chunk in range(max(TAIL_CHUNKS - block, 0), TAIL_CHUNKS + 1):
            row = (block + chunk - TAIL_CHUNKS) * QROWS
            chunk_forward(q_ref, k_ref, v_ref, bounds_ref, block, chunk, row, sums, outs)
        for g in range(GROUP):
            out_ref[head_span(g), here] = outs[g]
            total_ref[g : g + 1, here] = sums[g]


def attend_tail_kernel(
    q_ref, k_ref, v_ref, bounds_ref, part_ref, part_total_ref, out_ref, total_ref
):
    for block in range(q_ref.shape[0] // QROWS):
        here = slice(block * QROWS, (block + 1) * QROWS)
        sums = [part_total_ref[g : g + 1, here] for g in range(GROUP)]
        outs = [part_ref[head_span(g), here] for g in range(GROUP)]
        for chunk in range(0, max(TAIL_CHUNKS - block, 0)):
            row = (block + chunk) * QROWS
            chunk_forward(q_ref, k_ref, v_ref, bounds_ref, block, chunk, row, sums, outs)
        for g in range(GROUP):
            out_ref[here, head_span(g)] = (outs[g] * (1.0 / sums[g])).T.astype(bf16)
            total_ref[g : g + 1, here] = sums[g]


def attend_specs(rows, kv_rows, kv_heads, blocks):
    wide = GROUP * HEAD_WIDTH
    return [
        pl.BlockSpec((rows, wide), lambda j: (0, j)),
        pl.BlockSpec((kv_rows, HEAD_WIDTH), lambda j: (0, j)),
        pl.BlockSpec((kv_rows, HEAD_WIDTH), lambda j: (0, kv_heads + j)),
        pl.BlockSpec((blocks, 8, QROWS), lambda j: (0, 0, 0)),
    ]


def counts(rows, kv_heads):
    blocks = rows // QROWS
    own = sum(min(block, TAIL_CHUNKS) + 1 for block in range(blocks))
    tail = sum(max(TAIL_CHUNKS - block, 0) for block in range(blocks))
    unit = kv_heads * GROUP * QROWS * QROWS
    return own * unit, tail * unit


def attend(queries, kv_own, kv_tail, bounds):
    rows = queries.shape[0]
    kv_heads = kv_own.shape[1] // (2 * HEAD_WIDTH)
    blocks = rows // QROWS
    wide = GROUP * HEAD_WIDTH
    own_pairs, tail_pairs = counts(rows, kv_heads)
    turned_spec = pl.BlockSpec((wide, rows), lambda j: (j, 0))
    total_spec = pl.BlockSpec((None, 8, rows), lambda j: (j, 0, 0))
    turned_shape = shape_of((kv_heads * wide, rows), f32)
    total_shape = shape_of((kv_heads, 8, rows), f32)
    outs, totals = pl.pallas_call(
        attend_own_kernel,
        grid=(kv_heads,),
        in_specs=attend_specs(rows, rows, kv_heads, blocks),
        out_specs=[turned_spec, total_spec],
        out_shape=[turned_shape, total_shape],
        cost_estimate=cost(4 * own_pairs * HEAD_WIDTH, 4 << 20, own_pairs),
        name="attend_own",
    )(queries, kv_own, kv_own, bounds)
    return pl.pallas_call(
        attend_tail_kernel,
        grid=(kv_heads,),
        in_specs=attend_specs(rows, WINDOW_TOKENS, kv_heads, blocks) + [turned_spec, total_spec],
        out_specs=[pl.BlockSpec((rows, wide), lambda j: (0, j)), total_spec],
        out_shape=[shape_of((rows, kv_heads * wide), bf16), total_shape],
        cost_estimate=cost(4 * tail_pairs * HEAD_WIDTH, 4 << 20, tail_pairs),
        name="attend_tail",
    )(queries, kv_tail, kv_tail, bounds, outs, totals)


def chunk_backward(
    q_ref, k_ref, v_ref, bounds_ref, d_out_ref, block, chunk, row, shares, deltas, d_queries
):
    here = slice(block * QROWS, (block + 1) * QROWS)
    there = slice(row, row + QROWS)
    mask = chunk_mask(bounds_ref, block, chunk)
    keys = k_ref[there, :]
    values = v_ref[there, :]
    d_key = None
    d_value = None
    for g in range(GROUP):
        query = q_ref[here, head_span(g)]
        d_out = d_out_ref[here, head_span(g)]
        scores = nt_dot(keys, query)
        probs = jnp.where(mask, jnp.exp2(scores * (score_scale * log2_e)) * shares[g], 0.0)
        d_probs = nt_dot(values, d_out)
        d_scores = (probs * (d_probs - deltas[g]) * score_scale).astype(bf16)
        d_value_now = nn_dot(probs.astype(bf16), d_out)
        d_key_now = nn_dot(d_scores, query)
        d_value = d_value_now if g == 0 else d_value + d_value_now
        d_key = d_key_now if g == 0 else d_key + d_key_now
        d_queries[g] = d_queries[g] + tn_dot(keys, d_scores)
    return d_key, d_value


def attend_back_tail_kernel(
    q_ref, k_ref, v_ref, bounds_ref, total_ref, out_ref, d_out_ref,
    d_q_ref, d_k_ref, d_v_ref, delta_ref, dk_ref, dv_ref
):
    for block in range(q_ref.shape[0] // QROWS):
        here = slice(block * QROWS, (block + 1) * QROWS)
        shares = [1.0 / total_ref[g : g + 1, here] for g in range(GROUP)]
        deltas = []
        for g in range(GROUP):
            product = d_out_ref[here, head_span(g)].astype(f32) * out_ref[
                here, head_span(g)
            ].astype(f32)
            delta = jnp.sum(product.T, axis=0, keepdims=True)
            deltas.append(delta)
            delta_ref[g : g + 1, here] = delta
        d_queries = [jnp.zeros((HEAD_WIDTH, QROWS), f32) for g in range(GROUP)]
        for chunk in range(0, max(TAIL_CHUNKS - block, 0)):
            row = (block + chunk) * QROWS
            there = slice(row, row + QROWS)
            d_key, d_value = chunk_backward(
                q_ref, k_ref, v_ref, bounds_ref, d_out_ref, block, chunk, row,
                shares, deltas, d_queries,
            )
            if block == 0:
                dk_ref[there, :] = d_key
                dv_ref[there, :] = d_value
            else:
                dk_ref[there, :] += d_key
                dv_ref[there, :] += d_value
        for g in range(GROUP):
            d_q_ref[head_span(g), here] = d_queries[g]
    d_k_ref[...] = dk_ref[...].astype(bf16)
    d_v_ref[...] = dv_ref[...].astype(bf16)


def attend_back_own_kernel(
    q_ref, k_ref, v_ref, bounds_ref, total_ref, d_out_ref, d_q_part_ref, delta_ref,
    d_q_ref, d_k_ref, d_v_ref
):
    for block in range(q_ref.shape[0] // QROWS):
        here = slice(block * QROWS, (block + 1) * QROWS)
        shares = [1.0 / total_ref[g : g + 1, here] for g in range(GROUP)]
        deltas = [delta_ref[g : g + 1, here] for g in range(GROUP)]
        d_queries = [d_q_part_ref[head_span(g), here] for g in range(GROUP)]
        for chunk in range(max(TAIL_CHUNKS - block, 0), TAIL_CHUNKS + 1):
            row = (block + chunk - TAIL_CHUNKS) * QROWS
            there = slice(row, row + QROWS)
            d_key, d_value = chunk_backward(
                q_ref, k_ref, v_ref, bounds_ref, d_out_ref, block, chunk, row,
                shares, deltas, d_queries,
            )
            if chunk == TAIL_CHUNKS:
                d_k_ref[there, :] = d_key
                d_v_ref[there, :] = d_value
            else:
                d_k_ref[there, :] += d_key
                d_v_ref[there, :] += d_value
        for g in range(GROUP):
            d_q_ref[here, head_span(g)] = d_queries[g].T.astype(bf16)


def attend_back_tail(queries, kv_tail, bounds, totals, outs, d_outs):
    rows = queries.shape[0]
    kv_heads = kv_tail.shape[1] // (2 * HEAD_WIDTH)
    blocks = rows // QROWS
    wide = GROUP * HEAD_WIDTH
    own_pairs, tail_pairs = counts(rows, kv_heads)
    total_spec = pl.BlockSpec((None, 8, rows), lambda j: (j, 0, 0))
    head_spec = pl.BlockSpec((rows, wide), lambda j: (0, j))
    kv_spec = pl.BlockSpec((WINDOW_TOKENS, HEAD_WIDTH), lambda j: (0, j))
    kv_shape = shape_of((WINDOW_TOKENS, kv_heads * HEAD_WIDTH), bf16)
    return pl.pallas_call(
        attend_back_tail_kernel,
        grid=(kv_heads,),
        in_specs=attend_specs(rows, WINDOW_TOKENS, kv_heads, blocks)
        + [total_spec, head_spec, head_spec],
        out_specs=[pl.BlockSpec((wide, rows), lambda j: (j, 0)), kv_spec, kv_spec, total_spec],
        out_shape=[
            shape_of((kv_heads * wide, rows), f32),
            kv_shape,
            kv_shape,
            shape_of((kv_heads, 8, rows), f32),
        ],
        scratch_shapes=[pltpu.VMEM((WINDOW_TOKENS, HEAD_WIDTH), f32)] * 2,
        cost_estimate=cost(10 * tail_pairs * HEAD_WIDTH, 8 << 20, tail_pairs),
        name="attend_back_tail",
    )(queries, kv_tail, kv_tail, bounds, totals, outs, d_outs)


def attend_back_own(queries, kv_own, bounds, totals, d_outs, d_q_part, deltas):
    rows = queries.shape[0]
    kv_heads = kv_own.shape[1] // (2 * HEAD_WIDTH)
    blocks = rows // QROWS
    wide = GROUP * HEAD_WIDTH
    own_pairs, tail_pairs = counts(rows, kv_heads)
    total_spec = pl.BlockSpec((None, 8, rows), lambda j: (j, 0, 0))
    head_spec = pl.BlockSpec((rows, wide), lambda j: (0, j))
    kv_spec = pl.BlockSpec((rows, HEAD_WIDTH), lambda j: (0, j))
    kv_shape = shape_of((rows, kv_heads * HEAD_WIDTH), f32)
    return pl.pallas_call(
        attend_back_own_kernel,
        grid=(kv_heads,),
        in_specs=attend_specs(rows, rows, kv_heads, blocks)
        + [total_spec, head_spec, pl.BlockSpec((wide, rows), lambda j: (j, 0)), total_spec],
        out_specs=[head_spec, kv_spec, kv_spec],
        out_shape=[shape_of((rows, kv_heads * wide), bf16), kv_shape, kv_shape],
        cost_estimate=cost(10 * own_pairs * HEAD_WIDTH, 8 << 20, own_pairs),
        name="attend_back_own",
    )(queries, kv_own, kv_own, bounds, totals, d_outs, d_q_part, deltas)


def body(
    hidden_in,
    doc_lengths,
    pad_lengths,
    w_query,
    key_matrix,
    value_matrix,
    w_output,
    w_gate,
    w_up,
    w_down,
    attn_gain,
    mlp_gain,
    query_gain,
    key_gain,
    out_grad,
):
    core = lax.axis_index("c")
    group = lax.axis_index("q") * 2 + core
    part = lax.axis_index("seq")
    groups = lax.axis_size("q") * 2
    parts = lax.axis_size("seq")
    tokens, width = hidden_in.shape
    group_rows = tokens * parts
    slice_rows = width // groups
    units = FEEDFWD_UNITS // 2
    q_cols = QUERY_HEADS * HEAD_WIDTH // parts
    kv_cols = KEY_VALUE_HEADS * HEAD_WIDTH // parts
    attn_cols = q_cols + 2 * kv_cols
    pack_cols = attn_cols + q_cols
    w_block = attn_cols // q_cols
    core_at = core.astype(jnp.int32).reshape(1)
    part_at = part.astype(jnp.int32).reshape(1)

    def sent(value, shift):
        return lax.ppermute(value, "seq", [(i, (i + shift) % parts) for i in range(parts)])

    def from_all(value):
        return [value] + [sent(value, shift) for shift in range(1, parts)]

    def to_all(values):
        return [values[0]] + [sent(values[shift], shift) for shift in range(1, parts)]

    gain_cols = jnp.stack(
        [
            attn_gain,
            mlp_gain,
            jnp.pad(query_gain, (0, slice_rows - query_gain.shape[0])),
            jnp.pad(key_gain, (0, slice_rows - key_gain.shape[0])),
        ],
        axis=1,
    )
    gain_cols = jnp.pad(gain_cols, ((0, 0), (0, HEAD_WIDTH - gain_cols.shape[1])))
    packed = pack_attn(
        part_at, parts, w_query, key_matrix, value_matrix, w_output, gain_cols
    )
    attn_w = lax.all_gather(packed, dp_axes, axis=0, tiled=True)

    hidden_blocks = from_all(hidden_in)

    mlp_pack, mlp_give = pack_mlp(core_at, w_gate, w_up, w_down)
    mlp_got = lax.ppermute(mlp_give, "c", core_swap)
    mlp_pack = lax.dynamic_update_slice_in_dim(mlp_pack, mlp_got, (1 - core) * slice_rows, 0)
    mlp_w = lax.all_gather(mlp_pack, "q", axis=0, tiled=True)
    w_gu = mlp_w[:, : 2 * units]
    w_down_t = mlp_w[:, 2 * units :]
    grad_pair = jnp.concatenate([out_grad, lax.ppermute(out_grad, "c", core_swap)], axis=0)

    gains = attn_w[:, pack_cols : pack_cols + 4].astype(f32).T
    head_piece = query_gain.shape[0]
    ga = gains[0:1]
    gm = gains[1:2]
    gqk = gains[2:4].reshape(2, groups, slice_rows)[:, :, :head_piece].reshape(2, HEAD_WIDTH)

    doc_ends = jnp.cumsum(doc_lengths)
    doc_starts = doc_ends - doc_lengths
    pad_starts = doc_ends - pad_lengths
    first = group * group_rows
    token = first + jnp.arange(group_rows, dtype=jnp.int32)
    inside = (token[:, None] >= doc_starts[None, :]) & (token[:, None] < doc_ends[None, :])
    start = jnp.sum(jnp.where(inside, doc_starts[None, :], 0), axis=1)
    pad_start = jnp.sum(jnp.where(inside, pad_starts[None, :], 0), axis=1)
    inv_freq = rope_base ** (-jnp.arange(HEAD_WIDTH // 2, dtype=f32) * 2.0 / HEAD_WIDTH)
    angles = (token - start).astype(f32)[:, None] * inv_freq[None, :]
    cosine = jnp.cos(angles)
    sine = jnp.sin(angles)
    cosine = jnp.concatenate([cosine, cosine], axis=1)
    sine = jnp.concatenate([-sine, sine], axis=1)
    blocks = group_rows // QROWS
    offset = (token // QROWS) * QROWS - WINDOW_TOKENS
    low = jnp.maximum(start, token - (WINDOW_TOKENS - 1)) - offset
    high = jnp.minimum(token, pad_start - 1) - offset
    bounds = jnp.pad(
        jnp.stack([low.reshape(blocks, QROWS), high.reshape(blocks, QROWS)], axis=1),
        ((0, 0), (0, 6), (0, 0)),
    )

    normed_all, queries, kv_own, qk_proj = project(
        part_at, hidden_blocks, attn_w, ga, gqk, cosine, sine, q_cols, kv_cols
    )
    kv_tail = lax.ppermute(
        kv_own[group_rows - WINDOW_TOKENS :], dp_axes, [(i, i + 1) for i in range(groups - 1)]
    )
    attn, totals = attend(queries, kv_own, kv_tail, bounds)
    attn_terms = to_all(out_proj(part_at, parts, attn, attn_w, w_block))
    rows_own = hidden_in.astype(f32)
    middle = rows_own
    for term in attn_terms:
        middle = middle + term.astype(f32)
    mid_stats = norm_stats(middle)
    normed_mid = (middle * mid_stats * gm).astype(bf16)

    mid_pair = jnp.concatenate([normed_mid, lax.ppermute(normed_mid, "c", core_swap)], axis=0)
    gate_up = nn_dot(mid_pair, w_gu)
    gate = gate_up[:, :units]
    up = gate_up[:, units:]
    sig = 1.0 / (1.0 + jnp.exp(-gate))
    mixed = (gate * sig * up).astype(bf16)
    d_mixed = nn_dot(grad_pair, w_down_t)
    d_gate = (d_mixed * up * sig * (1.0 + gate * (1.0 - sig))).astype(bf16)
    d_up = (d_mixed * gate * sig).astype(bf16)
    d_gate_up = jnp.concatenate([d_gate, d_up], axis=1)
    d_mid_part = nt_dot(d_gate_up, w_gu)
    d_mid_other = lax.ppermute(d_mid_part[tokens:].astype(bf16), "c", core_swap)
    d_normed_mid = d_mid_part[:tokens] + d_mid_other.astype(f32)
    d_middle = out_grad.astype(f32) + norm_back(d_normed_mid, middle, mid_stats, gm)
    d_mlp_gain = jnp.sum(d_normed_mid * middle * mid_stats, axis=0)
    d_proj_blocks = from_all(d_middle.astype(bf16))

    out_part = nt_dot(mixed, w_down_t)
    out_other = lax.ppermute(out_part[tokens:].astype(bf16), "c", core_swap)
    output_act = (middle + out_part[:tokens] + out_other.astype(f32)).astype(bf16)

    mlp_grad = jnp.concatenate(
        [tn_dot(mid_pair, d_gate_up), tn_dot(grad_pair, mixed)], axis=1
    ).astype(bf16)
    mlp_grad = lax.psum_scatter(mlp_grad, "q", scatter_dimension=0, tiled=True)
    mlp_grad = lax.psum(mlp_grad, "seq")
    grad_give = lax.dynamic_slice_in_dim(mlp_grad, (1 - core) * slice_rows, slice_rows, 0)
    grad_got = lax.ppermute(grad_give, "c", core_swap)
    grad_gate, grad_up, grad_down = unpack_mlp(core_at, mlp_grad, grad_got)

    d_attn, w_out_grad = out_proj_back(part_at, d_proj_blocks, attn, attn_w, w_block)
    d_q_part, d_k_tail, d_v_tail, deltas = attend_back_tail(
        queries, kv_tail, bounds, totals, attn, d_attn
    )
    d_kv_tail = lax.ppermute(
        jnp.concatenate([d_k_tail, d_v_tail], axis=1),
        dp_axes,
        [(i + 1, i) for i in range(groups - 1)],
    )
    d_queries, d_k, d_v = attend_back_own(
        queries, kv_own, bounds, totals, d_attn, d_q_part, deltas
    )
    *d_in_terms, d_qkv, attn_gain_rows, head_gain_rows = project_back(
        part_at, [hidden_blocks[(parts - k) % parts] for k in range(parts)], d_queries,
        jnp.concatenate([d_k, d_v], axis=1), d_kv_tail, qk_proj, attn_w, gqk, cosine, sine,
    )
    d_normed_in = jnp.zeros((tokens, width), f32)
    for term in to_all(d_in_terms):
        d_normed_in = d_normed_in + term.astype(f32)
    in_grad = (d_middle + norm_back(d_normed_in, rows_own, norm_stats(rows_own), ga)).astype(bf16)

    def spread(head_gain):
        return jnp.pad(
            head_gain.reshape(groups, head_piece), ((0, 0), (0, slice_rows - head_piece))
        ).reshape(width)

    gain_grads = jnp.stack(
        [attn_gain_rows[0], d_mlp_gain, spread(head_gain_rows[0]), spread(head_gain_rows[1])],
        axis=1,
    )
    attn_grad = jnp.concatenate(
        [
            tn_dot(normed_all, d_qkv),
            w_out_grad,
            jnp.pad(gain_grads, ((0, 0), (0, HEAD_WIDTH - gain_grads.shape[1]))),
        ],
        axis=1,
    ).astype(bf16)
    by_core = attn_grad.reshape(groups // 2, 2, slice_rows, -1)
    keep = lax.dynamic_index_in_dim(by_core, core, 1, keepdims=False)
    give = lax.dynamic_index_in_dim(by_core, 1 - core, 1, keepdims=False)
    chip_sum = keep.astype(f32) + lax.ppermute(give, "c", core_swap).astype(f32)
    chip_sum = chip_sum.astype(bf16).reshape(width // 2, -1)
    attn_grad = lax.psum_scatter(chip_sum, "q", scatter_dimension=0, tiled=True)
    attn_grad = lax.all_gather(attn_grad, "seq", axis=0)
    gain_sums = jnp.sum(attn_grad[:, :, pack_cols : pack_cols + 4].astype(f32), axis=0)
    grad_query, grad_key, grad_value, grad_output = unpack_attn(attn_grad, q_cols, kv_cols)
    return (
        output_act,
        in_grad,
        grad_query,
        grad_key,
        grad_value,
        grad_output,
        grad_gate,
        grad_up,
        grad_down,
        gain_sums[:, 0],
        gain_sums[:, 1],
        gain_sums[:head_piece, 2],
        gain_sums[:head_piece, 3],
    )


def solution(mesh):
    groups, parts = mesh.devices.shape
    mesh = Mesh(mesh.devices.reshape(groups // 2, 2, parts), ("q", "c", "seq"))
    tokens = P(("q", "c", "seq"), None)
    rows = P(dp_axes, None)
    cols = P(None, dp_axes)
    flat = P(dp_axes)
    in_specs = (
        tokens, P(), P(), rows, rows, rows, cols, rows, rows, cols, flat, flat, flat, flat, tokens,
    )
    out_specs = (
        tokens, tokens, rows, rows, rows, cols, rows, rows, cols, flat, flat, flat, flat,
    )
    return jax.shard_map(body, mesh=mesh, in_specs=in_specs, out_specs=out_specs, check_vma=False)
```

time: 715 us -> 564 us (0.79)
  blocking collectives: 88.2 us -> 0 us
  local copies, waits for them, and re-layouts: 95.8 us -> 16.7 us
  Pallas kernels: 38.3 us -> 98.4 us
  waiting for transfers between devices: 355 us -> 303 us
  starting transfers between devices: 13.2 us -> 60.7 us
  other arithmetic: 54.8 us -> 29.3 us
  matrix products: 49.4 us -> 32.2 us
    reduce_scatter x2 -> x0, waiting for transfers between devices: 106 us -> none  [the longest x1 81.8 us: body(): lax.psum_scatter(d_in_part.astype(bf16), 'seq', scatter_dimension=0, tile...]
    psum x1, waiting for transfers between devices: 24.3 us -> 129 us  [body(): mlp_grad = lax.psum(mlp_grad, 'seq')]
    reduce_scatter x1, waiting for transfers between devices: 98.1 us -> 0.02 us  [body(): mlp_grad = lax.psum_scatter(mlp_grad, 'q', scatter_dimension=0, tiled=True)]
    all_to_all x3 -> x0, blocking collectives: 88.2 us -> none  [the longest x1 63.6 us: body(): lax.all_to_all(jnp.broadcast_to(d_proj[None], (parts, tokens, width)), 's...]
    ppermute x1 -> x15, waiting for transfers between devices: 0.01 us -> 78.3 us  [the longest x12 75.6 us: sent(): lax.ppermute(value, 'seq', [(i, (i + shift) % parts) for i in range(parts)])]
    all_gather x1, waiting for transfers between devices: 65.1 us -> 0.01 us  [body(): mlp_w = lax.all_gather(mlp_pack, 'q', axis=0, tiled=True)]
    pallas_call x2 -> x12, Pallas kernels: 38.3 us -> 98.4 us  [the longest x1 15.4 us: project_back(): pl.pallas_call(functools.partial(project_back_kernel, parts, tail_from, q...]
    all_to_all x1 -> x0, waiting for transfers between devices: 40.4 us -> none  [body(): lax.all_to_all(jnp.broadcast_to(hidden_in[None], (parts, tokens, width)),...]
  transfers between devices with their start and end apart: 16 -> 27, of which waited for: 10 -> 12; matrix products, arithmetic and copies ran while one was open for 10% -> 9% of each run, Pallas kernels for 0% -> 17%
where the time goes in v2:
time: 564 us; the launch traced here: 555 us
  waiting for transfers between devices  303 us (54%)
  Pallas kernels  98.4 us (17%)
  starting transfers between devices  60.7 us (11%)
  matrix products  32.2 us (6%)
  other arithmetic  29.3 us (5%)
  local copies, waits for them, and re-layouts  16.7 us (3%)
  between operations  15 us (3%)
    psum x1, waiting for transfers between devices, body(): mlp_grad = lax.psum(mlp_grad, 'seq')  129 us
    ppermute x12, waiting for transfers between devices, sent(): lax.ppermute(value, 'seq', [(i, (i + shift) % parts) for i in range(parts)])  75.6 us
    reduce_scatter x1, waiting for transfers between devices, body(): attn_grad = lax.psum_scatter(chip_sum, 'q', scatter_dimension=0, tiled=True)  37.4 us
    all_gather x1, waiting for transfers between devices, body(): attn_grad = lax.all_gather(attn_grad, 'seq', axis=0)  33.4 us
    ppermute x12, starting transfers between devices, sent(): lax.ppermute(value, 'seq', [(i, (i + shift) % parts) for i in range(parts)])  28.1 us
    all_gather x1, waiting for transfers between devices, body(): attn_w = lax.all_gather(packed, dp_axes, axis=0, tiled=True)  17.3 us
    pallas_call x1, Pallas kernels, project_back(): pl.pallas_call(functools.partial(project_back_kernel, parts, tail_from, q...  15.4 us
    pallas_call x1, Pallas kernels, attend_back_own(): pl.pallas_call(attend_back_own_kernel, grid=(kv_heads,), in_specs=attend_...  14.6 us
  transfers between devices with their start and end apart: 27, of which 12 were waited for; matrix products, arithmetic and copies ran while one was open for 9% of the time, Pallas kernels for 17%

profile of v2, /device:TPU:0, one launch (start us, length us, event | category | flops | bytes accessed | tf_op | source)
XLA Modules:
  0.0 555.3 jit_solution(7008774875641871748)
XLA Ops:
  11.4 4.0 pack_mlp.1
  30.3 17.3 %all-gather.5.cloned.1.call-done.refs_4_.w_ref.refs_5_ = bf16[1024,1664]{1,0:T(8,128)(2,1)} async-done(((bf16[128,1664]{1,0:T(8,128)(2,1)}), bf16[1024,1664]{1,0:T(8,128)(2,1)}) %all-gather.5.cloned.1.call-update) | async-done | bytes 3407888 | tf_op jit(solution)/shard_map/all_gather | solution.py:752
  50.8 8.9 %collective-permute-done.1.refs_2_ = bf16[256,1024]{1,0:T(8,128)(2,1)S(1)} collective-permute-done((bf16[256,1024]{1,0:T(8,128)(2,1)S(1)}, bf16[256,1024]{1,0:T(8,128)(2,1)S(1)}, u32[]{:S(2)}, u32[]{:S(2)}) %collective-permute-start.1) | collective-permute-done | bytes 524320 | tf_op jit(solution)/shard_map/ppermute | solution.py:731
  60.6 8.4 %project.1 = (bf16[1024,1024]{1,0:T(8,128)(2,1)}, bf16[1024,512]{1,0:T(8,128)(2,1)}, bf16[1024,512]{1,0:T(8,128)(2,1)}, f32[1024,768]{1,0:T(8,128)}) custom-call(s32[1]{0:T(128)} %bitcast.part_ref, bf16[256,1024]{1,0:T(8,128)(2,1)} %refs_0_.3, bf16[256,1024]{1,0:T(8,128)(2,1)} %copy-done.10, bf16[256,1024]{1,0:T(8,128)(2,1)} %copy-done.11, ...), custom_call_target="tpu_custom_call" | custom-call | flops 2147483648 | bytes 12582912 | tf_op jit(solution)/shard_map/project/pallas_call | solution.py:261
  71.8 7.2 %attend_own.1 = (f32[512,1024]{1,0:T(8,128)}, f32[2,8,1024]{2,1,0:T(8,128)}) custom-call(bf16[1024,512]{1,0:T(8,128)(2,1)} %get-tuple-element.50.q_ref, bf16[1024,512]{1,0:T(8,128)(2,1)} %get-tuple-element.51.k_ref.v_ref, bf16[1024,512]{1,0:T(8,128)(2,1)} %get-tuple-element.51.k_ref.v_ref, s32[4,8,256]{2,1,0:T(8,128)} %pad.32.bounds_ref), custom_call_target="tpu_custom_call" | custom-call | flops 1342177280 | bytes 4194304 | tf_op jit(solution)/shard_map/attend_own/pallas_call | solution.py:540
  80.0 12.4 %attend_tail.1 = (bf16[1024,512]{1,0:T(8,128)(2,1)}, f32[2,8,1024]{2,1,0:T(8,128)}) custom-call(bf16[1024,512]{1,0:T(8,128)(2,1)} %get-tuple-element.50.q_ref, bf16[1024,512]{1,0:T(8,128)(2,1)} %copy-done.5, bf16[1024,512]{1,0:T(8,128)(2,1)} %copy-done.5, s32[4,8,256]{2,1,0:T(8,128)} %pad.32.bounds_ref, f32[512,1024]{1,0:T(8,128)} %get-tuple-element.52.part_ref, ...), custom_call_target="tpu_custom_call" | custom-call | flops 1342177280 | bytes 4194304 | tf_op jit(solution)/shard_map/attend_tail/pallas_call | solution.py:549
  92.4 5.5 out_proj.1
  97.8 11.5 %collective-permute-start.6 = (bf16[256,1024]{1,0:T(8,128)(2,1)}, bf16[256,1024]{1,0:T(8,128)(2,1)S(1)}, u32[]{:S(2)}, u32[]{:S(2)}) collective-permute-start(bf16[256,1024]{1,0:T(8,128)(2,1)} %get-tuple-element.58), channel_id=1, source_target_pairs={{0,3},{1,0},{2,1},{3,2},{4,7},{5,4},{6,5},{7,6},{8,11},{9,8},{10,9... | collective-permute-start | bytes 1572872 | tf_op jit(solution)/shard_map/ppermute | solution.py:731
  110.5 9.2 %collective-permute-start.10 = (bf16[256,1024]{1,0:T(8,128)(2,1)S(1)}, bf16[256,1024]{1,0:T(8,128)(2,1)S(1)}, u32[]{:S(2)}, u32[]{:S(2)}) collective-permute-start(bf16[256,1024]{1,0:T(8,128)(2,1)S(1)} %copy-done.8), channel_id=1, source_target_pairs={{0,4},{4,0},{1,5},{5,1},{2,6},{6,2},{3,7},{7,3},{8,12},{12,8},{9,1... | collective-permute-start | bytes 1572872 | tf_op jit(solution)/shard_map/ppermute | solution.py:762
  119.7 32.5 %collective-permute-done.5 = bf16[256,1024]{1,0:T(8,128)(2,1)S(1)} collective-permute-done((bf16[256,1024]{1,0:T(8,128)(2,1)}, bf16[256,1024]{1,0:T(8,128)(2,1)S(1)}, u32[]{:S(2)}, u32[]{:S(2)}) %collective-permute-start.5) | collective-permute-done | bytes 524320 | tf_op jit(solution)/shard_map/ppermute | solution.py:731
  154.0 4.7 collective-permute-start.7
  160.3 5.6 %fusion.2 = f32[512,3072]{1,0:T(8,128)S(1)} fusion(bf16[1024,4608]{1,0:T(8,128)(2,1)} %all-gather.7.cloned.1.call-done, bf16[256,1024]{1,0:T(8,128)(2,1)} %collective-permute-done.7, bf16[256,1024]{1,0:T(8,128)(2,1)S(1)} %multiply_convert_fusion.3), kind=kOutput, calls=%fused_computation.4 | convolution fusion | flops 3223322624 | bytes 13631488 | tf_op jit(solution)/shard_map/dot_general | solution.py:38
  166.0 4.8 multiply_convert_fusion.1
  172.9 4.9 convolution_convert_fusion
  177.8 4.7 pad_maximum_fusion
  182.8 6.6 %fusion = f32[512,1024]{1,0:T(8,128)S(1)} fusion(bf16[1024,4608]{1,0:T(8,128)(2,1)} %all-gather.7.cloned.1.call-done, bf16[512,1536]{1,0:T(8,128)(2,1)} %copy-done.22, bf16[512,1536]{1,0:T(8,128)(2,1)} %copy-done.21), kind=kOutput, calls=%fused_computation.2 | convolution fusion | flops 3227516928 | bytes 11534336 | tf_op jit(solution)/shard_map/dot_general | solution.py:30
  190.0 3.7 fusion.7
  201.4 12.7 %collective-permute-done.12.refs_1_ = bf16[256,1024]{1,0:T(8,128)(2,1)S(1)} collective-permute-done((bf16[256,1024]{1,0:T(8,128)(2,1)S(1)}, bf16[256,1024]{1,0:T(8,128)(2,1)S(1)}, u32[]{:S(2)}, u32[]{:S(2)}) %collective-permute-start.12) | collective-permute-done | bytes 524320 | tf_op jit(solution)/shard_map/ppermute | solution.py:731
  214.1 21.5 %collective-permute-done.13.refs_2_ = bf16[256,1024]{1,0:T(8,128)(2,1)S(1)} collective-permute-done((bf16[256,1024]{1,0:T(8,128)(2,1)S(1)}, bf16[256,1024]{1,0:T(8,128)(2,1)S(1)}, u32[]{:S(2)}, u32[]{:S(2)}) %collective-permute-start.13) | collective-permute-done | bytes 524320 | tf_op jit(solution)/shard_map/ppermute | solution.py:731
  237.2 7.7 %out_proj_back.1 = (bf16[1024,512]{1,0:T(8,128)(2,1)}, f32[1024,512]{1,0:T(8,128)}) custom-call(s32[1]{0:T(128)} %bitcast.part_ref, bf16[256,1024]{1,0:T(8,128)(2,1)} %copy-done.13, bf16[256,1024]{1,0:T(8,128)(2,1)} %copy-done.16, bf16[256,1024]{1,0:T(8,128)(2,1)} %copy-done.17, bf16[256,1024]{1,0:T(8,128)(2,1)} %copy-done.18, ...), custom_call_target="tpu_custom_call" | custom-call | flops 2147483648 | bytes 8388608 | tf_op jit(solution)/shard_map/out_proj_back/pallas_call | solution.py:434
  244.9 13.3 %attend_back_tail.1 = (f32[512,1024]{1,0:T(8,128)}, bf16[1024,256]{1,0:T(8,128)(2,1)}, bf16[1024,256]{1,0:T(8,128)(2,1)}, f32[2,8,1024]{2,1,0:T(8,128)}) custom-call(bf16[1024,512]{1,0:T(8,128)(2,1)} %get-tuple-element.50.q_ref, bf16[1024,512]{1,0:T(8,128)(2,1)} %copy-done.5, bf16[1024,512]{1,0:T(8,128)(2,1)} %copy-done.5, s32[4,8,256]{2,1,0:T(8,128)} %pad.32.bounds_ref, ...), custom_call_target="tpu_custom_call" | custom-call | flops 3355443200 | bytes 8388608 | tf_op jit(solution)/shard_map/attend_back_tail/pallas_call | solution.py:656
  263.4 14.6 %attend_back_own.1 = (bf16[1024,512]{1,0:T(8,128)(2,1)}, f32[1024,256]{1,0:T(8,128)}, f32[1024,256]{1,0:T(8,128)}) custom-call(bf16[1024,512]{1,0:T(8,128)(2,1)} %get-tuple-element.50.q_ref, bf16[1024,512]{1,0:T(8,128)(2,1)} %get-tuple-element.51.k_ref.v_ref, bf16[1024,512]{1,0:T(8,128)(2,1)} %get-tuple-element.51.k_ref.v_ref, s32[4,8,256]{2,1,0:T(8,128)} %pad.32.bounds_ref, ...), custom_call_target="tpu_custom_call" | custom-call | flops 3355443200 | bytes 8388608 | tf_op jit(solution)/shard_map/attend_back_own/pallas_call | solution.py:684
  282.1 15.4 %project_back.1 = (bf16[256,1024]{1,0:T(8,128)(2,1)}, bf16[256,1024]{1,0:T(8,128)(2,1)}, bf16[256,1024]{1,0:T(8,128)(2,1)}, bf16[256,1024]{1,0:T(8,128)(2,1)}, b...) custom-call(s32[1]{0:T(128)} %bitcast.part_ref, bf16[1024,512]{1,0:T(8,128)(2,1)} %get-tuple-element.65.dq_ref, ...), custom_call_target="tpu_custom_call" | custom-call | flops 2147483648 | bytes 16777216 | tf_op jit(solution)/shard_map/project_back/pallas_call | solution.py:349
  299.5 4.7 convolution_convert_fusion.2
  305.9 13.6 %collective-permute-start.19 = (bf16[4,128,1664]{2,1,0:T(8,128)(2,1)}, bf16[4,128,1664]{2,1,0:T(8,128)(2,1)}, u32[]{:S(2)}, u32[]{:S(2)}) collective-permute-start(bf16[4,128,1664]{2,1,0:T(8,128)(2,1)} %dynamic-slice_bitcast_fusion), channel_id=1, source_target_pairs={{0,4},{4,0},{1,5},{5,1},{2,6},{6,2},{3,7},{7,3},{8,12},{12,8},{9,1... | collective-permute-start | bytes 5111816 | tf_op jit(solution)/shard_map/ppermute | solution.py:879
  319.4 3.6 collective-permute-done.19
  326.7 37.4 %reduce-scatter.3.cloned.1.call-done = bf16[128,1664]{1,0:T(8,128)(2,1)} async-done(((bf16[512,1664]{1,0:T(8,128)(2,1)}), bf16[128,1664]{1,0:T(8,128)(2,1)}) %reduce-scatter.3.cloned.1.call-update) | async-done | bytes 426000 | tf_op jit(solution)/shard_map/reduce_scatter | solution.py:881
  364.2 3.4 collective-permute-start.18
  368.6 129.4 %all-reduce.9.cloned.1.call-done.own_ref = bf16[256,4608]{1,0:T(8,128)(2,1)} async-done(((bf16[256,4608]{1,0:T(8,128)(2,1)}), bf16[256,4608]{1,0:T(8,128)(2,1)}) %all-reduce.9.cloned.1.call-update) | async-done | bytes 2359312 | tf_op jit(solution)/shard_map/psum | solution.py:833
  504.3 33.4 %all-gather.9.cloned.1.call-done = bf16[512,1664]{1,0:T(8,128)(2,1)} async-done(((bf16[128,1664]{1,0:T(8,128)(2,1)}), bf16[512,1664]{1,0:T(8,128)(2,1)}) %all-gather.9.cloned.1.call-update) | async-done | bytes 1703952 | tf_op jit(solution)/shard_map/all_gather | solution.py:882
  537.7 3.9 unpack_attn.1
  543.9 4.0 unpack_mlp.1
  (154 shorter events, 69.8 us)
Async XLA Ops:
  7.2 40.5 %all-gather.5.cloned.1.call-start = ((), (), s32[]{:S(2)}) async-start(), calls=%async_computation.2 | async-start | bytes 3833856 | tf_op jit(solution)/shard_map/all_gather | solution.py:752
  11.4 149.0 %all-gather.7.cloned.1.call-start = ((), (), s32[]{:S(2)}) async-start(), calls=%async_computation.3 | async-start | bytes 11796480 | tf_op jit(solution)/shard_map/all_gather | solution.py:759
  15.4 3.2 collective-permute-start.8
  19.7 306.4 %reduce-scatter.5.cloned.1.call-start = ((), (), s32[]{:S(2)}) async-start(), calls=%async_computation.5 | async-start | bytes 11796480 | tf_op jit(solution)/shard_map/reduce_scatter | solution.py:832
  19.8 31.0 %collective-permute-start = (bf16[256,1024]{1,0:T(8,128)(2,1)S(1)}, bf16[256,1024]{1,0:T(8,128)(2,1)S(1)}, u32[]{:S(2)}, u32[]{:S(2)}) collective-permute-start(bf16[256,1024]{1,0:T(8,128)(2,1)S(1)} %copy-done), channel_id=1, source_target_pairs={{0,1},{1,2},{2,3},{3,0},{4,5},{5,6},{6,7},{7,4},{8,9},{9,10},{10,1... | collective-permute-start | bytes 1572872 | tf_op jit(solution)/shard_map/ppermute | solution.py:731
  22.8 36.9 %collective-permute-start.1 = (bf16[256,1024]{1,0:T(8,128)(2,1)S(1)}, bf16[256,1024]{1,0:T(8,128)(2,1)S(1)}, u32[]{:S(2)}, u32[]{:S(2)}) collective-permute-start(bf16[256,1024]{1,0:T(8,128)(2,1)S(1)} %copy-done), channel_id=1, source_target_pairs={{0,2},{1,3},{2,0},{3,1},{4,6},{5,7},{6,4},{7,5},{8,10},{9,11},{10,... | collective-permute-start | bytes 1572872 | tf_op jit(solution)/shard_map/ppermute | solution.py:731
  25.4 34.3 %collective-permute-start.2 = (bf16[256,1024]{1,0:T(8,128)(2,1)S(1)}, bf16[256,1024]{1,0:T(8,128)(2,1)S(1)}, u32[]{:S(2)}, u32[]{:S(2)}) collective-permute-start(bf16[256,1024]{1,0:T(8,128)(2,1)S(1)} %copy-done), channel_id=1, source_target_pairs={{0,3},{1,0},{2,1},{3,2},{4,7},{5,4},{6,5},{7,6},{8,11},{9,8},{10,9... | collective-permute-start | bytes 1572872 | tf_op jit(solution)/shard_map/ppermute | solution.py:731
  69.1 9.9 %collective-permute-start.3 = (bf16[1024,512]{1,0:T(8,128)(2,1)}, bf16[1024,512]{1,0:T(8,128)(2,1)S(1)}, u32[]{:S(2)}, u32[]{:S(2)}) collective-permute-start(bf16[1024,512]{1,0:T(8,128)(2,1)} %get-tuple-element.51.k_ref.v_ref), channel_id=1, source_target_pairs={{0,4},{4,8},{8,12},{12,16},{16,20},{20,24},{24,28},{1,5},{5,9},{9,... | collective-permute-start | bytes 3145736 | tf_op jit(solution)/shard_map/ppermute | solution.py:796
  92.4 59.9 %copy-start.1 = (bf16[256,1024]{1,0:T(8,128)(2,1)S(1)}, bf16[256,1024]{1,0:T(8,128)(2,1)}, u32[]{:S(2)}) copy-start(bf16[256,1024]{1,0:T(8,128)(2,1)} %refs_0_.3) | copy-start | bytes 1572868
  97.8 21.9 %collective-permute-start.6 = (bf16[256,1024]{1,0:T(8,128)(2,1)}, bf16[256,1024]{1,0:T(8,128)(2,1)S(1)}, u32[]{:S(2)}, u32[]{:S(2)}) collective-permute-start(bf16[256,1024]{1,0:T(8,128)(2,1)} %get-tuple-element.58), channel_id=1, source_target_pairs={{0,3},{1,0},{2,1},{3,2},{4,7},{5,4},{6,5},{7,6},{8,11},{9,8},{10,9... | collective-permute-start | bytes 1572872 | tf_op jit(solution)/shard_map/ppermute | solution.py:731
  109.3 42.9 %collective-permute-start.5 = (bf16[256,1024]{1,0:T(8,128)(2,1)}, bf16[256,1024]{1,0:T(8,128)(2,1)S(1)}, u32[]{:S(2)}, u32[]{:S(2)}) collective-permute-start(bf16[256,1024]{1,0:T(8,128)(2,1)} %get-tuple-element.57), channel_id=1, source_target_pairs={{0,2},{1,3},{2,0},{3,1},{4,6},{5,7},{6,4},{7,5},{8,10},{9,11},{10,... | collective-permute-start | bytes 1572872 | tf_op jit(solution)/shard_map/ppermute | solution.py:731
  110.3 41.9 %collective-permute-start.4 = (bf16[256,1024]{1,0:T(8,128)(2,1)}, bf16[256,1024]{1,0:T(8,128)(2,1)S(1)}, u32[]{:S(2)}, u32[]{:S(2)}) collective-permute-start(bf16[256,1024]{1,0:T(8,128)(2,1)} %get-tuple-element.56), channel_id=1, source_target_pairs={{0,1},{1,2},{2,3},{3,0},{4,5},{5,6},{6,7},{7,4},{8,9},{9,10},{10,1... | collective-permute-start | bytes 1572872 | tf_op jit(solution)/shard_map/ppermute | solution.py:731
  110.5 48.2 %collective-permute-start.10 = (bf16[256,1024]{1,0:T(8,128)(2,1)S(1)}, bf16[256,1024]{1,0:T(8,128)(2,1)S(1)}, u32[]{:S(2)}, u32[]{:S(2)}) collective-permute-start(bf16[256,1024]{1,0:T(8,128)(2,1)S(1)} %copy-done.8), channel_id=1, source_target_pairs={{0,4},{4,0},{1,5},{5,1},{2,6},{6,2},{3,7},{7,3},{8,12},{12,8},{9,1... | collective-permute-start | bytes 1572872 | tf_op jit(solution)/shard_map/ppermute | solution.py:762
  154.0 6.3 %collective-permute-start.7 = (bf16[256,1024]{1,0:T(8,128)(2,1)S(1)}, bf16[256,1024]{1,0:T(8,128)(2,1)}, u32[]{:S(2)}, u32[]{:S(2)}) collective-permute-start(bf16[256,1024]{1,0:T(8,128)(2,1)S(1)} %multiply_convert_fusion.3), channel_id=1, source_target_pairs={{0,4},{4,0},{1,5},{5,1},{2,6},{6,2},{3,7},{7,3},{8,12},{12,8},{9,1... | collective-permute-start | bytes 1572872 | tf_op jit(solution)/shard_map/ppermute | solution.py:808
  182.5 181.6 %reduce-scatter.3.cloned.1.call-start = ((), (), s32[]{:S(2)}) async-start(), calls=%async_computation.4 | async-start | bytes 2129920 | tf_op jit(solution)/shard_map/reduce_scatter | solution.py:881
  189.5 4.4 collective-permute-start.11
  193.8 2.0 collective-permute-start.9
  197.4 38.2 %copy-start.13 = (bf16[256,1024]{1,0:T(8,128)(2,1)}, bf16[256,1024]{1,0:T(8,128)(2,1)S(1)}, u32[]{:S(2)}) copy-start(bf16[256,1024]{1,0:T(8,128)(2,1)S(1)} %get-tuple-element.99.refs_0_) | copy-start | bytes 1572868
  197.4 16.7 %collective-permute-start.12 = (bf16[256,1024]{1,0:T(8,128)(2,1)S(1)}, bf16[256,1024]{1,0:T(8,128)(2,1)S(1)}, u32[]{:S(2)}, u32[]{:S(2)}) collective-permute-start(bf16[256,1024]{1,0:T(8,128)(2,1)S(1)} %get-tuple-element.99.refs_0_), channel_id=1, source_target_pairs={{0,1},{1,2},{2,3},{3,0},{4,5},{5,6},{6,7},{7,4},{8,9},{9,10},{10,1... | collective-permute-start | bytes 1572872 | tf_op jit(solution)/shard_map/ppermute | solution.py:731
  197.4 38.2 %collective-permute-start.13 = (bf16[256,1024]{1,0:T(8,128)(2,1)S(1)}, bf16[256,1024]{1,0:T(8,128)(2,1)S(1)}, u32[]{:S(2)}, u32[]{:S(2)}) collective-permute-start(bf16[256,1024]{1,0:T(8,128)(2,1)S(1)} %get-tuple-element.99.refs_0_), channel_id=1, source_target_pairs={{0,2},{1,3},{2,0},{3,1},{4,6},{5,7},{6,4},{7,5},{8,10},{9,11},{10,... | collective-permute-start | bytes 1572872 | tf_op jit(solution)/shard_map/ppermute | solution.py:731
  198.5 37.1 %collective-permute-start.14 = (bf16[256,1024]{1,0:T(8,128)(2,1)S(1)}, bf16[256,1024]{1,0:T(8,128)(2,1)S(1)}, u32[]{:S(2)}, u32[]{:S(2)}) collective-permute-start(bf16[256,1024]{1,0:T(8,128)(2,1)S(1)} %get-tuple-element.99.refs_0_), channel_id=1, source_target_pairs={{0,3},{1,0},{2,1},{3,2},{4,7},{5,4},{6,5},{7,6},{8,11},{9,8},{10,9... | collective-permute-start | bytes 1572872 | tf_op jit(solution)/shard_map/ppermute | solution.py:731
  260.7 20.4 %collective-permute-start.15 = (bf16[1024,512]{1,0:T(8,128)(2,1)}, bf16[1024,512]{1,0:T(8,128)(2,1)S(1)}, u32[]{:S(2)}, u32[]{:S(2)}) collective-permute-start(bf16[1024,512]{1,0:T(8,128)(2,1)} %pad_maximum_fusion.7), channel_id=1, source_target_pairs={{4,0},{8,4},{12,8},{16,12},{20,16},{24,20},{28,24},{5,1},{9,5},{13... | collective-permute-start | bytes 3145736 | tf_op jit(solution)/shard_map/ppermute | solution.py:842
  305.9 17.1 %collective-permute-start.19 = (bf16[4,128,1664]{2,1,0:T(8,128)(2,1)}, bf16[4,128,1664]{2,1,0:T(8,128)(2,1)}, u32[]{:S(2)}, u32[]{:S(2)}) collective-permute-start(bf16[4,128,1664]{2,1,0:T(8,128)(2,1)} %dynamic-slice_bitcast_fusion), channel_id=1, source_target_pairs={{0,4},{4,0},{1,5},{5,1},{2,6},{6,2},{3,7},{7,3},{8,12},{12,8},{9,1... | collective-permute-start | bytes 5111816 | tf_op jit(solution)/shard_map/ppermute | solution.py:879
  326.0 174.4 %copy-start.2 = (bf16[256,1024]{1,0:T(8,128)(2,1)S(1)}, bf16[256,1024]{1,0:T(8,128)(2,1)}, u32[]{:S(2)}) copy-start(bf16[256,1024]{1,0:T(8,128)(2,1)} %refs_0_.3) | copy-start | bytes 1572868
  326.0 174.4 %copy-start.7 = (bf16[256,1024]{1,0:T(8,128)(2,1)S(1)}, bf16[256,1024]{1,0:T(8,128)(2,1)}, u32[]{:S(2)}) copy-start(bf16[256,1024]{1,0:T(8,128)(2,1)} %get-tuple-element.71) | copy-start | bytes 1572868
  326.1 171.9 %all-reduce.9.cloned.1.call-start = ((), (), s32[]{:S(2)}) async-start(), calls=%async_computation.6 | async-start | bytes 4718592 | tf_op jit(solution)/shard_map/psum | solution.py:833
  326.7 175.3 %copy-start.3 = (f32[256,1024]{1,0:T(8,128)S(1)}, f32[256,1024]{1,0:T(8,128)}, u32[]{:S(2)}) copy-start(f32[256,1024]{1,0:T(8,128)} %get-tuple-element.100) | copy-start | bytes 3145732
  326.7 211.1 %all-gather.9.cloned.1.call-start = ((), (), s32[]{:S(2)}) async-start(), calls=%async_computation.7 | async-start | bytes 2129920 | tf_op jit(solution)/shard_map/all_gather | solution.py:882
  364.2 136.2 %collective-permute-start.18 = (bf16[256,1024]{1,0:T(8,128)(2,1)}, bf16[256,1024]{1,0:T(8,128)(2,1)S(1)}, u32[]{:S(2)}, u32[]{:S(2)}) collective-permute-start(bf16[256,1024]{1,0:T(8,128)(2,1)} %get-tuple-element.74), channel_id=1, source_target_pairs={{0,3},{1,0},{2,1},{3,2},{4,7},{5,4},{6,5},{7,6},{8,11},{9,8},{10,9... | collective-permute-start | bytes 1572872 | tf_op jit(solution)/shard_map/ppermute | solution.py:731
  367.5 132.8 %collective-permute-start.17 = (bf16[256,1024]{1,0:T(8,128)(2,1)}, bf16[256,1024]{1,0:T(8,128)(2,1)S(1)}, u32[]{:S(2)}, u32[]{:S(2)}) collective-permute-start(bf16[256,1024]{1,0:T(8,128)(2,1)} %get-tuple-element.73), channel_id=1, source_target_pairs={{0,2},{1,3},{2,0},{3,1},{4,6},{5,7},{6,4},{7,5},{8,10},{9,11},{10,... | collective-permute-start | bytes 1572872 | tf_op jit(solution)/shard_map/ppermute | solution.py:731
  367.5 132.9 %collective-permute-start.16 = (bf16[256,1024]{1,0:T(8,128)(2,1)}, bf16[256,1024]{1,0:T(8,128)(2,1)}, u32[]{:S(2)}, u32[]{:S(2)}) collective-permute-start(bf16[256,1024]{1,0:T(8,128)(2,1)} %get-tuple-element.72), channel_id=1, source_target_pairs={{0,1},{1,2},{2,3},{3,0},{4,5},{5,6},{6,7},{7,4},{8,9},{9,10},{10,1... | collective-permute-start | bytes 1572872 | tf_op jit(solution)/shard_map/ppermute | solution.py:731
  500.4 43.6 %collective-permute-start.20 = (bf16[128,4608]{1,0:T(8,128)(2,1)}, bf16[128,4608]{1,0:T(8,128)(2,1)}, u32[]{:S(2)}, u32[]{:S(2)}) collective-permute-start(bf16[128,4608]{1,0:T(8,128)(2,1)} %constant_dynamic-slice_fusion), channel_id=1, source_target_pairs={{0,4},{4,0},{1,5},{5,1},{2,6},{6,2},{3,7},{7,3},{8,12},{12,8},{9,1... | collective-permute-start | bytes 3538952 | tf_op jit(solution)/shard_map/ppermute | solution.py:835
  (18 other events, 103.0 us)
Sparse Core Ops, SparseCore 0:
  11.5 36.1 all-gather.4
  49.5 99.4 all-gather.6
  182.7 107.4 reduce-scatter.4
  326.2 37.8 reduce-scatter.2
  366.3 131.6 all-reduce.8
  499.4 38.2 all-gather.8

commit v3 on v2

v3 whole, which is shorter than its diff:
```python
import functools

import jax
import jax.numpy as jnp
from jax import lax
from jax.experimental import pallas as pl
from jax.experimental.pallas import tpu as pltpu
from jax.sharding import Mesh, PartitionSpec as P

QUERY_HEADS = 16
KEY_VALUE_HEADS = 8
HEAD_WIDTH = 128
FEEDFWD_UNITS = 3072
WINDOW_TOKENS = 1024
QROWS = 256
GROUP = QUERY_HEADS // KEY_VALUE_HEADS
TAIL_CHUNKS = WINDOW_TOKENS // QROWS

norm_eps = 1e-06
rope_base = 1000000.0
score_scale = HEAD_WIDTH**-0.5
log2_e = 1.4426950408889634
bf16 = jnp.bfloat16
f32 = jnp.float32
dp_axes = ("q", "c")
core_swap = [(0, 1), (1, 0)]


def nt_dot(left, right):
    return lax.dot_general(left, right, (((1,), (1,)), ((), ())), preferred_element_type=f32)


def tn_dot(left, right):
    return lax.dot_general(left, right, (((0,), (0,)), ((), ())), preferred_element_type=f32)


def nn_dot(left, right):
    return jnp.dot(left, right, preferred_element_type=f32)


def shape_of(dims, kind):
    return jax.ShapeDtypeStruct(dims, kind)


def call(
    kernel, args, *, grid, in_specs, out_specs, out_shape, name, estimate, prefetch=0, scratch=(),
    mib=32, after=()
):
    count = prefetch + len(in_specs)

    def body_of(*refs):
        kernel(*refs[:count], *refs[count + len(after) :])

    return pl.pallas_call(
        body_of,
        grid_spec=pltpu.PrefetchScalarGridSpec(
            num_scalar_prefetch=prefetch,
            grid=grid,
            in_specs=list(in_specs) + [pl.BlockSpec(memory_space=pl.ANY)] * len(after),
            out_specs=out_specs,
            scratch_shapes=list(scratch),
        ),
        out_shape=out_shape,
        compiler_params=pltpu.CompilerParams(vmem_limit_bytes=mib << 20),
        cost_estimate=estimate,
        name=name,
    )(*args, *after)


def cost(flops, moved, exps=0, scale=100):
    flops, moved, exps = flops * scale, moved * scale, exps * scale
    return pl.CostEstimate(flops=int(flops), bytes_accessed=int(moved), transcendentals=int(exps))


def norm_stats(rows):
    return lax.rsqrt(jnp.mean(rows * rows, axis=-1, keepdims=True) + norm_eps)


def norm_back(d_normed, rows, stats, gains):
    scaled = d_normed * gains
    unit = rows * stats
    return stats * (scaled - unit * jnp.mean(scaled * unit, axis=-1, keepdims=True))


def pack_attn_kernel(
    part_ref, wq_ref, wk_ref, wv_ref, wo_ref, ga_ref, gm_ref, gq_ref, gk_ref, out_ref, gains_ref
):
    gains_ref[...] = jnp.zeros_like(gains_ref)
    for row, gain_ref in enumerate((ga_ref, gm_ref, gq_ref, gk_ref)):
        gains_ref[row : row + 1, : gain_ref.shape[1]] = gain_ref[...]
    column = 0
    for piece in (
        wq_ref[...].astype(bf16),
        wk_ref[...].astype(bf16),
        wv_ref[...].astype(bf16),
        wo_ref[...].T.astype(bf16),
    ):
        out_ref[:, column : column + piece.shape[1]] = piece
        column += piece.shape[1]
    gains = gains_ref[...].T
    rest = jnp.zeros((gains.shape[0], HEAD_WIDTH - gains.shape[1]), f32)
    out_ref[:, column:] = jnp.concatenate([gains, rest], axis=1).astype(bf16)


def pack_attn(part, parts, w_query, key_matrix, value_matrix, w_output, gains, after=()):
    gains = [gain[None] for gain in gains]
    rows = w_query.shape[0]
    q_cols = w_query.shape[1] // parts
    kv_cols = key_matrix.shape[1] // parts
    total = 2 * q_cols + 2 * kv_cols + HEAD_WIDTH
    return call(
        pack_attn_kernel,
        (part, w_query, key_matrix, value_matrix, w_output, *gains),
        prefetch=1,
        grid=(1,),
        in_specs=[
            pl.BlockSpec((rows, q_cols), lambda i, p: (0, p[0])),
            pl.BlockSpec((rows, kv_cols), lambda i, p: (0, p[0])),
            pl.BlockSpec((rows, kv_cols), lambda i, p: (0, p[0])),
            pl.BlockSpec((q_cols, rows), lambda i, p: (p[0], 0)),
        ]
        + [pl.BlockSpec(gain.shape, lambda i, p: (0, 0)) for gain in gains],
        scratch=[pltpu.VMEM((8, rows), f32)],
        mib=60,
        out_specs=pl.BlockSpec((rows, total), lambda i, p: (0, 0)),
        out_shape=shape_of((rows, total), bf16),
        estimate=cost(0, rows * total * 6),
        name="pack_attn",
        after=after,
    )


def add_kernel(left_ref, right_ref, out_ref):
    out_ref[...] = (left_ref[...].astype(f32) + right_ref[...].astype(f32)).astype(bf16)


def add(left, right, after=()):
    rows, cols = left.shape
    spec = pl.BlockSpec((rows // 4, cols), lambda i: (i, 0))
    return call(
        add_kernel,
        (left, right),
        grid=(4,),
        in_specs=[spec, spec],
        out_specs=spec,
        out_shape=shape_of((rows, cols), bf16),
        estimate=cost(rows * cols, 6 * rows * cols),
        name="add",
        after=after,
    )


def touch_kernel(in_ref, out_ref):
    out_ref[...] = in_ref[...]


def touch(value, after):
    rows, cols = value.shape
    spec = pl.BlockSpec((rows // 4, cols), lambda i: (i, 0))
    return call(
        touch_kernel,
        (value,),
        grid=(4,),
        in_specs=[spec],
        out_specs=spec,
        out_shape=shape_of((rows, cols), value.dtype),
        estimate=cost(0, 4 * rows * cols),
        name="touch",
        after=after,
    )


def sum_kernel(*refs):
    total = refs[0][...].astype(f32)
    for ref in refs[1:-1]:
        total = total + ref[...].astype(f32)
    refs[-1][...] = total.astype(bf16)


def sum_all(terms, after=()):
    rows, cols = terms[0].shape
    steps = 4 if rows % 64 == 0 else 1
    spec = pl.BlockSpec((rows // steps, cols), lambda i: (i, 0))
    return call(
        sum_kernel,
        tuple(terms),
        grid=(steps,),
        in_specs=[spec] * len(terms),
        out_specs=spec,
        out_shape=shape_of((rows, cols), bf16),
        estimate=cost(len(terms) * rows * cols, 2 * (len(terms) + 1) * rows * cols),
        name="sum_all",
        after=after,
    )


def finish_in_kernel(d_normed_ref, d_middle_ref, x_ref, gain_ref, out_ref):
    rows = x_ref[...].astype(f32)
    back = norm_back(d_normed_ref[...].astype(f32), rows, norm_stats(rows), gain_ref[...])
    out_ref[...] = (d_middle_ref[...] + back).astype(bf16)


def finish_in(d_normed, d_middle, hidden, gain, after=()):
    rows, cols = hidden.shape
    spec = pl.BlockSpec((rows // 4, cols), lambda i: (i, 0))
    return call(
        finish_in_kernel,
        (d_normed, d_middle, hidden, gain),
        grid=(4,),
        in_specs=[spec] * 3 + [pl.BlockSpec((1, cols), lambda i: (0, 0))],
        out_specs=spec,
        out_shape=shape_of((rows, cols), bf16),
        estimate=cost(20 * rows * cols, 12 * rows * cols, scale=1),
        name="finish_in",
        after=after,
    )


def sum_blocks_kernel(in_ref, out_ref):
    total = in_ref[0].astype(f32)
    for index in range(1, in_ref.shape[0]):
        total = total + in_ref[index].astype(f32)
    out_ref[...] = total.astype(bf16)


def sum_blocks(stacked, after=()):
    count, rows, cols = stacked.shape
    return call(
        sum_blocks_kernel,
        (stacked,),
        grid=(4,),
        in_specs=[pl.BlockSpec((count, rows // 4, cols), lambda i: (0, i, 0))],
        out_specs=pl.BlockSpec((rows // 4, cols), lambda i: (i, 0)),
        out_shape=shape_of((rows, cols), bf16),
        estimate=cost(count * rows * cols, 2 * (count + 1) * rows * cols),
        name="sum_blocks",
        after=after,
    )


def read_gains_kernel(in_ref, out_ref):
    out_ref[...] = in_ref[...].astype(f32).T[:8, :]


def read_gains(attn_w, column, after=()):
    width = attn_w.shape[0]
    return call(
        read_gains_kernel,
        (attn_w,),
        grid=(1,),
        in_specs=[pl.BlockSpec((width, HEAD_WIDTH), lambda i: (0, column // HEAD_WIDTH))],
        out_specs=pl.BlockSpec((8, width), lambda i: (0, 0)),
        out_shape=shape_of((8, width), f32),
        estimate=cost(0, width * HEAD_WIDTH * 4),
        name="read_gains",
        after=after,
    )


def pack_mlp_kernel(core_ref, wg_ref, wu_ref, wd_ref, own_ref, give_ref):
    units = wg_ref.shape[1]

    def fill(out_ref):
        out_ref[:, :units] = wg_ref[...].astype(bf16)
        out_ref[:, units : 2 * units] = wu_ref[...].astype(bf16)
        out_ref[:, 2 * units :] = wd_ref[...].T.astype(bf16)

    @pl.when(pl.program_id(0) == 0)
    def first():
        fill(give_ref)

    @pl.when(pl.program_id(0) == 1)
    def second():
        fill(own_ref)


def pack_mlp(core, w_gate, w_up, w_down, after=()):
    rows = w_gate.shape[0]
    units = w_gate.shape[1] // 2
    half = lambda i, c: (c[0] + 1 - i) % 2
    return call(
        pack_mlp_kernel,
        (core, w_gate, w_up, w_down,),
        prefetch=1,
        grid=(2,),
        in_specs=[
            pl.BlockSpec((rows, units), lambda i, c: (0, half(i, c))),
            pl.BlockSpec((rows, units), lambda i, c: (0, half(i, c))),
            pl.BlockSpec((units, rows), lambda i, c: (half(i, c), 0)),
        ],
        out_specs=[
            pl.BlockSpec((rows, 3 * units), lambda i, c: (c[0], 0)),
            pl.BlockSpec((rows, 3 * units), lambda i, c: (0, 0)),
        ],
        out_shape=[shape_of((2 * rows, 3 * units), bf16), shape_of((rows, 3 * units), bf16)],
        estimate=cost(0, rows * units * 36),
        name="pack_mlp",
        after=after,
    )


def unpack_half_kernel(turned, core_ref, own_ref, got_ref, out_ref):
    def fill(in_ref):
        rows = in_ref[...].astype(f32)
        out_ref[...] = rows.T if turned else rows

    @pl.when(pl.program_id(0) == 0)
    def first():
        fill(own_ref)

    @pl.when(pl.program_id(0) == 1)
    def second():
        fill(got_ref)


def unpack_half(core, sums, got, column, turned, after=()):
    rows, units = got.shape
    half = lambda i, c: (c[0] + i) % 2
    if turned:
        out_spec = pl.BlockSpec((units, rows), lambda i, c: (half(i, c), 0))
        out_shape = shape_of((2 * units, rows), f32)
    else:
        out_spec = pl.BlockSpec((rows, units), lambda i, c: (0, half(i, c)))
        out_shape = shape_of((rows, 2 * units), f32)
    return call(
        functools.partial(unpack_half_kernel, turned),
        (core, sums, got,),
        prefetch=1,
        grid=(2,),
        in_specs=[
            pl.BlockSpec((rows, units), lambda i, c: (c[0], column)),
            pl.BlockSpec((rows, units), lambda i, c: (0, 0)),
        ],
        out_specs=out_spec,
        out_shape=out_shape,
        estimate=cost(0, rows * units * 12, scale=1),
        name="unpack_half",
        after=after,
    )


def unpack_attn_kernel(in_ref, wq_ref, wk_ref, wv_ref, wo_ref):
    column = 0
    for out_ref in (wq_ref, wk_ref, wv_ref):
        count = out_ref.shape[1]
        out_ref[...] = in_ref[:, column : column + count].astype(f32)
        column += count
    wo_ref[...] = in_ref[:, column : column + wo_ref.shape[0]].astype(f32).T


def unpack_attn(gathered, q_cols, kv_cols, after=()):
    parts, rows, total = gathered.shape
    return call(
        unpack_attn_kernel,
        (gathered,),
        grid=(parts,),
        in_specs=[pl.BlockSpec((None, rows, total), lambda i: (i, 0, 0))],
        out_specs=[
            pl.BlockSpec((rows, q_cols), lambda i: (0, i)),
            pl.BlockSpec((rows, kv_cols), lambda i: (0, i)),
            pl.BlockSpec((rows, kv_cols), lambda i: (0, i)),
            pl.BlockSpec((q_cols, rows), lambda i: (i, 0)),
        ],
        out_shape=[
            shape_of((rows, parts * q_cols), f32),
            shape_of((rows, parts * kv_cols), f32),
            shape_of((rows, parts * kv_cols), f32),
            shape_of((parts * q_cols, rows), f32),
        ],
        estimate=cost(0, parts * rows * total * 6, scale=1),
        name="unpack_attn",
        after=after,
    )


def pick(refs, scratch):
    for k, ref in enumerate(refs):

        @pl.when(pl.program_id(0) == k)
        def take(ref=ref):
            scratch[...] = ref[...]


def turn(rows):
    half = HEAD_WIDTH // 2
    return jnp.concatenate([rows[:, half:], rows[:, :half]], axis=1)


def project_kernel(parts, q_cols, kv_cols, part_ref, *refs):
    blocks = refs[:parts]
    w_ref, ga_ref, gqk_ref, cos_ref, sin_ref, normed_ref, q_ref, kv_ref, proj_ref, x_ref = refs[parts:]
    pick(blocks, x_ref)
    rows = x_ref[...].astype(f32)
    normed = (rows * norm_stats(rows) * ga_ref[...]).astype(bf16)
    normed_ref[...] = normed
    cosine = cos_ref[...]
    sine = sin_ref[...]
    qk_cols = q_cols + kv_cols
    proj = nn_dot(normed, w_ref[...])
    proj_ref[...] = proj[:, :qk_cols]
    kv_ref[:, kv_cols:] = proj[:, qk_cols:].astype(bf16)
    for column in range(0, qk_cols, HEAD_WIDTH):
        head = proj[:, column : column + HEAD_WIDTH]
        gain = gqk_ref[0:1, :] if column < q_cols else gqk_ref[1:2, :]
        head = head * norm_stats(head) * gain
        head = (head * cosine + turn(head) * sine).astype(bf16)
        if column < q_cols:
            q_ref[:, column : column + HEAD_WIDTH] = head
        else:
            kv_ref[:, column - q_cols : column - q_cols + HEAD_WIDTH] = head


def project(part, blocks, attn_w, ga, gqk, cosine, sine, q_cols, kv_cols, after=()):
    parts = len(blocks)
    tokens, width = blocks[0].shape
    attn_cols = q_cols + 2 * kv_cols
    place = lambda k, p: ((p[0] + parts - k) % parts, 0)
    fixed = lambda k, p: (0, 0)
    rows = parts * tokens
    return call(
        functools.partial(project_kernel, parts, q_cols, kv_cols),
        (part, *blocks, attn_w, ga, gqk, cosine, sine,),
        prefetch=1,
        grid=(parts,),
        in_specs=[pl.BlockSpec((tokens, width), fixed)] * parts
        + [
            pl.BlockSpec((width, attn_cols), fixed),
            pl.BlockSpec((1, width), fixed),
            pl.BlockSpec((2, HEAD_WIDTH), fixed),
            pl.BlockSpec((tokens, HEAD_WIDTH), place),
            pl.BlockSpec((tokens, HEAD_WIDTH), place),
        ],
        out_specs=[
            pl.BlockSpec((tokens, width), place),
            pl.BlockSpec((tokens, q_cols), place),
            pl.BlockSpec((tokens, 2 * kv_cols), place),
            pl.BlockSpec((tokens, q_cols + kv_cols), place),
        ],
        scratch=[pltpu.VMEM((tokens, width), bf16)],
        out_shape=[
            shape_of((rows, width), bf16),
            shape_of((rows, q_cols), bf16),
            shape_of((rows, 2 * kv_cols), bf16),
            shape_of((rows, q_cols + kv_cols), f32),
        ],
        mib=32,
        estimate=cost(2 * rows * width * attn_cols, 12 << 20),
        name="project",
        after=after,
    )


def project_back_kernel(
    parts, groups, tail_from, q_cols, kv_cols, part_ref, *refs
):
    blocks = refs[:parts]
    (dq_ref, d_kv_ref, tail_ref, proj_ref, w_ref, gqk_ref, cos_ref, sin_ref, normed_ref,
     w_out_ref, mlp_gain_ref, out_ref, term_ref,
     x_ref, dqkv_ref, acc_ref, gain_ref, head_gain_ref) = refs[parts:]
    step = pl.program_id(0)
    block = (part_ref[0] + step) % parts
    pick(blocks, x_ref)

    @pl.when(step == 0)
    def clear():
        gain_ref[...] = jnp.zeros_like(gain_ref)
        head_gain_ref[...] = jnp.zeros_like(head_gain_ref)
        acc_ref[...] = jnp.zeros_like(acc_ref)

    cosine = cos_ref[...]
    sine = sin_ref[...]
    has_tail = jnp.where(block >= tail_from, 1.0, 0.0)
    dk = (d_kv_ref[0] + tail_ref[0].astype(f32) * has_tail).astype(bf16)
    dqkv_ref[:, q_cols + kv_cols :] = (
        d_kv_ref[1] + tail_ref[1].astype(f32) * has_tail
    ).astype(bf16)
    head_gains = [jnp.zeros((1, HEAD_WIDTH), f32) for _ in range(2)]
    for column in range(0, q_cols + kv_cols, HEAD_WIDTH):
        index = 0 if column < q_cols else 1
        if index == 0:
            d_head = dq_ref[:, column : column + HEAD_WIDTH].astype(f32)
        else:
            d_head = dk[:, column - q_cols : column - q_cols + HEAD_WIDTH].astype(f32)
        d_head = d_head * cosine + turn(d_head * sine)
        head = proj_ref[:, column : column + HEAD_WIDTH]
        stats = norm_stats(head)
        unit = head * stats
        head_gains[index] = head_gains[index] + jnp.sum(d_head * unit, axis=0, keepdims=True)
        scaled = d_head * gqk_ref[index : index + 1, :]
        d_proj = stats * (scaled - unit * jnp.mean(scaled * unit, axis=-1, keepdims=True))
        dqkv_ref[:, column : column + HEAD_WIDTH] = d_proj.astype(bf16)
    head_gain_ref[0:1, :] += head_gains[0]
    head_gain_ref[1:2, :] += head_gains[1]
    d_in = nt_dot(dqkv_ref[...], w_ref[...])
    rows = x_ref[...].astype(f32)
    gain_ref[0:1, :] += jnp.sum(d_in * (rows * norm_stats(rows)), axis=0, keepdims=True)
    out_ref[...] = d_in.astype(bf16)
    acc_ref[...] += tn_dot(normed_ref[...], dqkv_ref[...])

    @pl.when(step == parts - 1)
    def finish():
        attn_cols = acc_ref.shape[1]
        term_ref[:, :attn_cols] = acc_ref[...].astype(bf16)
        term_ref[:, attn_cols : attn_cols + q_cols] = w_out_ref[...]
        gain_ref[1:2, :] = mlp_gain_ref[0:1, :]
        piece = HEAD_WIDTH // groups
        slice_rows = gain_ref.shape[1] // groups
        for index in range(2):
            for group in range(groups):
                gain_ref[2 + index : 3 + index, group * slice_rows : group * slice_rows + piece] = (
                    head_gain_ref[index : index + 1, group * piece : (group + 1) * piece]
                )
        gains = gain_ref[...].T
        rest = jnp.zeros((gains.shape[0], HEAD_WIDTH - gains.shape[1]), f32)
        term_ref[:, attn_cols + q_cols :] = jnp.concatenate([gains, rest], axis=1).astype(bf16)


def project_back(
    part, groups, hidden, dq, d_kv, tail, proj, attn_w, gqk, cosine, sine, normed,
    w_out_grad, mlp_gain_rows, after=()
):
    parts = len(hidden)
    tokens, width = hidden[0].shape
    rows, q_cols = dq.shape
    kv_cols = d_kv.shape[2]
    attn_cols = q_cols + 2 * kv_cols
    tail_from = (rows - WINDOW_TOKENS) // tokens
    place = lambda k, p: ((p[0] + k) % parts, 0)
    kv_place = lambda k, p: (0, (p[0] + k) % parts, 0)
    tail_place = lambda k, p: (0, jnp.maximum((p[0] + k) % parts - tail_from, 0), 0)
    fixed = lambda k, p: (0, 0)
    total = attn_cols + q_cols + HEAD_WIDTH
    return call(
        functools.partial(project_back_kernel, parts, groups, tail_from, q_cols, kv_cols),
        (part, *hidden, dq, d_kv, tail, proj, attn_w, gqk, cosine, sine, normed, w_out_grad, mlp_gain_rows),
        prefetch=1,
        grid=(parts,),
        in_specs=[pl.BlockSpec((tokens, width), fixed)] * parts
        + [
            pl.BlockSpec((tokens, q_cols), place),
            pl.BlockSpec((2, tokens, kv_cols), kv_place),
            pl.BlockSpec((2, tokens, kv_cols), tail_place),
            pl.BlockSpec((tokens, q_cols + kv_cols), place),
            pl.BlockSpec((width, attn_cols), fixed),
            pl.BlockSpec((2, HEAD_WIDTH), fixed),
            pl.BlockSpec((tokens, HEAD_WIDTH), place),
            pl.BlockSpec((tokens, HEAD_WIDTH), place),
            pl.BlockSpec((tokens, width), place),
            pl.BlockSpec((width, q_cols), fixed),
            pl.BlockSpec((8, width), fixed),
        ],
        out_specs=[
            pl.BlockSpec((tokens, width), place),
            pl.BlockSpec((width, total), fixed),
        ],
        scratch=[
            pltpu.VMEM((tokens, width), bf16),
            pltpu.VMEM((tokens, attn_cols), bf16),
            pltpu.VMEM((width, attn_cols), f32),
            pltpu.VMEM((8, width), f32),
            pltpu.VMEM((8, HEAD_WIDTH), f32),
        ],
        mib=48,
        out_shape=[
            shape_of((rows, width), bf16),
            shape_of((width, total), bf16),
        ],
        estimate=cost(4 * rows * width * attn_cols, 16 << 20, scale=1),
        name="project_back",
        after=after,
    )


def out_grad_kernel(parts, *refs):
    d_projs = refs[:parts]
    attns = refs[parts : 2 * parts]
    out_ref = refs[2 * parts]
    total = None
    for d_proj, attn in zip(d_projs, attns):
        term = tn_dot(d_proj[...], attn[...])
        total = term if total is None else total + term
    out_ref[...] = total.astype(bf16)


def out_grad_sums(d_projs, attns, after=()):
    parts = len(attns)
    tokens, q_cols = attns[0].shape
    width = d_projs[0].shape[1]
    cols = width // 4
    return call(
        functools.partial(out_grad_kernel, parts),
        (*d_projs, *attns,),
        grid=(4,),
        in_specs=[pl.BlockSpec((tokens, cols), lambda i: (0, i))] * parts
        + [pl.BlockSpec((tokens, q_cols), lambda i: (0, 0))] * parts,
        out_specs=pl.BlockSpec((cols, q_cols), lambda i: (i, 0)),
        out_shape=shape_of((width, q_cols), bf16),
        mib=32,
        estimate=cost(2 * parts * tokens * width * q_cols, 4 << 20, scale=1),
        name="out_grad",
        after=after,
    )


def chunk_mask(low, high, chunk):
    key = lax.broadcasted_iota(jnp.int32, (QROWS, QROWS), 0) + chunk * QROWS
    mask = (key >= low) & (key <= high)
    if chunk == TAIL_CHUNKS:
        own = lax.broadcasted_iota(jnp.int32, (QROWS, QROWS), 1) + WINDOW_TOKENS
        mask = mask | (key == own)
    return mask


def head_span(g):
    return slice(g * HEAD_WIDTH, (g + 1) * HEAD_WIDTH)


def attend_own_kernel(q_ref, k_ref, v_ref, bounds_ref, out_ref, total_ref):
    for block in range(q_ref.shape[0] // QROWS):
        here = slice(block * QROWS, (block + 1) * QROWS)
        sums = [jnp.zeros((1, QROWS), f32) for g in range(GROUP)]
        outs = [jnp.zeros((HEAD_WIDTH, QROWS), f32) for g in range(GROUP)]
        for chunk in range(max(TAIL_CHUNKS - block, 0), TAIL_CHUNKS + 1):
            row = (block + chunk - TAIL_CHUNKS) * QROWS
            there = slice(row, row + QROWS)
            mask = chunk_mask(bounds_ref[block, 0:1, :], bounds_ref[block, 1:2, :], chunk)
            for g in range(GROUP):
                scores = nt_dot(k_ref[there, :], q_ref[here, head_span(g)])
                weights = jnp.where(mask, jnp.exp2(scores * (score_scale * log2_e)), 0.0)
                sums[g] = sums[g] + jnp.sum(weights, axis=0, keepdims=True)
                outs[g] = outs[g] + tn_dot(v_ref[there, :], weights.astype(bf16))
        for g in range(GROUP):
            out_ref[head_span(g), here] = outs[g]
            total_ref[g : g + 1, here] = sums[g]


def chunk_pairs(chunks, kv_heads):
    return chunks * kv_heads * GROUP * QROWS * QROWS


def attend_own(queries, kv_own, bounds, after=()):
    rows = queries.shape[0]
    kv_heads = kv_own.shape[1] // (2 * HEAD_WIDTH)
    blocks = rows // QROWS
    wide = GROUP * HEAD_WIDTH
    pairs = chunk_pairs(sum(min(b, TAIL_CHUNKS) + 1 for b in range(blocks)), kv_heads)
    return call(
        attend_own_kernel,
        (queries, kv_own, kv_own, bounds,),
        grid=(kv_heads,),
        in_specs=[
            pl.BlockSpec((rows, wide), lambda j: (0, j)),
            pl.BlockSpec((rows, HEAD_WIDTH), lambda j: (0, j)),
            pl.BlockSpec((rows, HEAD_WIDTH), lambda j: (0, kv_heads + j)),
            pl.BlockSpec((blocks, 8, QROWS), lambda j: (0, 0, 0)),
        ],
        out_specs=[
            pl.BlockSpec((wide, rows), lambda j: (j, 0)),
            pl.BlockSpec((None, 8, rows), lambda j: (j, 0, 0)),
        ],
        out_shape=[shape_of((kv_heads * wide, rows), f32), shape_of((kv_heads, 8, rows), f32)],
        mib=32,
        estimate=cost(4 * pairs * HEAD_WIDTH, 4 << 20, pairs),
        name="attend_own",
        after=after,
    )


def attend_tail_kernel(
    shift, parts, part_ref, q_ref, k_ref, v_ref, bounds_ref, own_ref, own_total_ref, w_ref,
    attn_ref, total_ref, proj_ref, out_ref, acc_ref
):
    block = (part_ref[0] + shift) % parts
    out_ref[...] = own_ref[...]
    total_ref[...] = own_total_ref[...]
    for chunk in range(TAIL_CHUNKS):

        @pl.when(block + chunk < TAIL_CHUNKS)
        def add(chunk=chunk):
            there = pl.ds(pl.multiple_of((block + chunk) * QROWS, QROWS), QROWS)
            keys = k_ref[there, :]
            values = v_ref[there, :]
            mask = chunk_mask(bounds_ref[0:1, :], bounds_ref[1:2, :], chunk)
            for g in range(GROUP):
                scores = nt_dot(keys, q_ref[:, head_span(g)])
                weights = jnp.where(mask, jnp.exp2(scores * (score_scale * log2_e)), 0.0)
                total_ref[g : g + 1, :] += jnp.sum(weights, axis=0, keepdims=True)
                out_ref[head_span(g), :] += tn_dot(values, weights.astype(bf16))

    for g in range(GROUP):
        share = 1.0 / total_ref[g : g + 1, :]
        attn_ref[:, head_span(g)] = (out_ref[head_span(g), :] * share).T.astype(bf16)
    term = nt_dot(attn_ref[...], w_ref[...])
    last = pl.num_programs(0) - 1

    @pl.when(pl.program_id(0) == 0)
    def start():
        acc_ref[...] = term

    @pl.when(pl.program_id(0) > 0)
    def add_up():
        acc_ref[...] += term

    @pl.when(pl.program_id(0) == last)
    def finish():
        proj_ref[...] = acc_ref[...].astype(bf16)


def attend_tail(shift, part, parts, queries, kv_tail, bounds, outs, totals, attn_w, attn_cols, after=()):
    q_cols = queries.shape[1]
    width = attn_w.shape[0]
    kv_heads = kv_tail.shape[1] // (2 * HEAD_WIDTH)
    wide = GROUP * HEAD_WIDTH
    at = lambda p: (p[0] + shift) % parts
    pairs = chunk_pairs(TAIL_CHUNKS // 2, kv_heads)
    return call(
        functools.partial(attend_tail_kernel, shift, parts),
        (part, queries, kv_tail, kv_tail, bounds, outs, totals, attn_w,),
        prefetch=1,
        grid=(kv_heads,),
        in_specs=[
            pl.BlockSpec((QROWS, wide), lambda j, p: (at(p), j)),
            pl.BlockSpec((WINDOW_TOKENS, HEAD_WIDTH), lambda j, p: (0, j)),
            pl.BlockSpec((WINDOW_TOKENS, HEAD_WIDTH), lambda j, p: (0, kv_heads + j)),
            pl.BlockSpec((None, 8, QROWS), lambda j, p: (at(p), 0, 0)),
            pl.BlockSpec((wide, QROWS), lambda j, p: (j, at(p))),
            pl.BlockSpec((None, 8, QROWS), lambda j, p: (j, 0, at(p))),
            pl.BlockSpec((width, wide), lambda j, p: (0, attn_cols // wide + j)),
        ],
        out_specs=[
            pl.BlockSpec((QROWS, wide), lambda j, p: (0, j)),
            pl.BlockSpec((None, 8, QROWS), lambda j, p: (j, 0, 0)),
            pl.BlockSpec((QROWS, width), lambda j, p: (0, 0)),
        ],
        scratch=[pltpu.VMEM((wide, QROWS), f32), pltpu.VMEM((QROWS, width), f32)],
        out_shape=[
            shape_of((QROWS, q_cols), bf16),
            shape_of((kv_heads, 8, QROWS), f32),
            shape_of((QROWS, width), bf16),
        ],
        mib=32,
        estimate=cost(
            4 * pairs * HEAD_WIDTH + 2 * QROWS * width * q_cols, 4 << 20, pairs
        ),
        name="attend_tail",
        after=after,
    )


def chunk_backward(keys, values, queries, d_outs, mask, shares, deltas, turned):
    d_key = None
    d_value = None
    for g in range(GROUP):
        scores = nt_dot(keys, queries[g])
        probs = jnp.where(mask, jnp.exp2(scores * (score_scale * log2_e)) * shares[g], 0.0)
        d_probs = nt_dot(values, d_outs[g])
        d_scores = (probs * (d_probs - deltas[g]) * score_scale).astype(bf16)
        d_value_now = nn_dot(probs.astype(bf16), d_outs[g])
        d_key_now = nn_dot(d_scores, queries[g])
        d_value = d_value_now if g == 0 else d_value + d_value_now
        d_key = d_key_now if g == 0 else d_key + d_key_now
        turned[g] = turned[g] + tn_dot(keys, d_scores)
    return d_key, d_value


def attend_back_tail_kernel(
    q_ref, k_ref, v_ref, bounds_ref, total_ref, attn_ref, d_proj_ref, w_ref,
    d_out_ref, turned_ref, delta_ref, d_kv_ref, dk_ref, dv_ref
):
    d_out_ref[...] = nn_dot(d_proj_ref[...], w_ref[...]).astype(bf16)
    for block in range(q_ref.shape[0] // QROWS):
        here = slice(block * QROWS, (block + 1) * QROWS)
        shares = [1.0 / total_ref[g : g + 1, here] for g in range(GROUP)]
        queries = [q_ref[here, head_span(g)] for g in range(GROUP)]
        d_outs = [d_out_ref[here, head_span(g)] for g in range(GROUP)]
        deltas = []
        for g in range(GROUP):
            product = d_outs[g].astype(f32) * attn_ref[here, head_span(g)].astype(f32)
            deltas.append(jnp.sum(product.T, axis=0, keepdims=True))
            delta_ref[g : g + 1, here] = deltas[g]
        turned = [jnp.zeros((HEAD_WIDTH, QROWS), f32) for g in range(GROUP)]
        for chunk in range(0, max(TAIL_CHUNKS - block, 0)):
            there = slice((block + chunk) * QROWS, (block + chunk + 1) * QROWS)
            mask = chunk_mask(bounds_ref[block, 0:1, :], bounds_ref[block, 1:2, :], chunk)
            d_key, d_value = chunk_backward(
                k_ref[there, :], v_ref[there, :], queries, d_outs, mask, shares, deltas, turned
            )
            if block == 0:
                dk_ref[there, :] = d_key
                dv_ref[there, :] = d_value
            else:
                dk_ref[there, :] += d_key
                dv_ref[there, :] += d_value
        for g in range(GROUP):
            turned_ref[head_span(g), here] = turned[g]
    d_kv_ref[0] = dk_ref[...].astype(bf16)
    d_kv_ref[1] = dv_ref[...].astype(bf16)


def attend_back_own_kernel(
    q_ref, k_ref, v_ref, bounds_ref, total_ref, d_out_ref, turned_ref, delta_ref, dq_ref, d_kv_ref
):
    for block in range(q_ref.shape[0] // QROWS):
        here = slice(block * QROWS, (block + 1) * QROWS)
        shares = [1.0 / total_ref[g : g + 1, here] for g in range(GROUP)]
        queries = [q_ref[here, head_span(g)] for g in range(GROUP)]
        d_outs = [d_out_ref[here, head_span(g)] for g in range(GROUP)]
        deltas = [delta_ref[g : g + 1, here] for g in range(GROUP)]
        turned = [turned_ref[head_span(g), here] for g in range(GROUP)]
        for chunk in range(max(TAIL_CHUNKS - block, 0), TAIL_CHUNKS + 1):
            row = (block + chunk - TAIL_CHUNKS) * QROWS
            there = slice(row, row + QROWS)
            mask = chunk_mask(bounds_ref[block, 0:1, :], bounds_ref[block, 1:2, :], chunk)
            d_key, d_value = chunk_backward(
                k_ref[there, :], v_ref[there, :], queries, d_outs, mask, shares, deltas, turned
            )
            if chunk == TAIL_CHUNKS:
                d_kv_ref[0, there, :] = d_key
                d_kv_ref[1, there, :] = d_value
            else:
                d_kv_ref[0, there, :] += d_key
                d_kv_ref[1, there, :] += d_value
        for g in range(GROUP):
            dq_ref[here, head_span(g)] = turned[g].T.astype(bf16)


def attend_back_tail(
    queries, kv_tail, bounds, totals, attn, d_proj, attn_w, attn_cols, after=()
):
    rows, q_cols = queries.shape
    width = attn_w.shape[0]
    kv_heads = kv_tail.shape[1] // (2 * HEAD_WIDTH)
    blocks = rows // QROWS
    wide = GROUP * HEAD_WIDTH
    pairs = chunk_pairs(sum(max(TAIL_CHUNKS - b, 0) for b in range(blocks)), kv_heads)
    head_spec = pl.BlockSpec((rows, wide), lambda j: (0, j))
    row_spec = pl.BlockSpec((None, 8, rows), lambda j: (j, 0, 0))
    return call(
        attend_back_tail_kernel,
        (queries, kv_tail, kv_tail, bounds, totals, attn, d_proj, attn_w),
        grid=(kv_heads,),
        in_specs=[
            head_spec,
            pl.BlockSpec((WINDOW_TOKENS, HEAD_WIDTH), lambda j: (0, j)),
            pl.BlockSpec((WINDOW_TOKENS, HEAD_WIDTH), lambda j: (0, kv_heads + j)),
            pl.BlockSpec((blocks, 8, QROWS), lambda j: (0, 0, 0)),
            row_spec,
            head_spec,
            pl.BlockSpec((rows, width), lambda j: (0, 0)),
            pl.BlockSpec((width, wide), lambda j: (0, attn_cols // wide + j)),
        ],
        out_specs=[
            head_spec,
            pl.BlockSpec((wide, rows), lambda j: (j, 0)),
            row_spec,
            pl.BlockSpec((2, WINDOW_TOKENS, HEAD_WIDTH), lambda j: (0, 0, j)),
        ],
        scratch=[pltpu.VMEM((WINDOW_TOKENS, HEAD_WIDTH), f32)] * 2,
        out_shape=[
            shape_of((rows, q_cols), bf16),
            shape_of((kv_heads * wide, rows), f32),
            shape_of((kv_heads, 8, rows), f32),
            shape_of((2, WINDOW_TOKENS, kv_heads * HEAD_WIDTH), bf16),
        ],
        mib=40,
        estimate=cost(10 * pairs * HEAD_WIDTH + 2 * rows * width * q_cols, 8 << 20, pairs),
        name="attend_back_tail",
        after=after,
    )


def attend_back_own(queries, kv_own, bounds, totals, d_outs, turned, deltas, after=()):
    rows, q_cols = queries.shape
    kv_heads = kv_own.shape[1] // (2 * HEAD_WIDTH)
    blocks = rows // QROWS
    wide = GROUP * HEAD_WIDTH
    pairs = chunk_pairs(sum(min(b, TAIL_CHUNKS) + 1 for b in range(blocks)), kv_heads)
    head_spec = pl.BlockSpec((rows, wide), lambda j: (0, j))
    row_spec = pl.BlockSpec((None, 8, rows), lambda j: (j, 0, 0))
    return call(
        attend_back_own_kernel,
        (queries, kv_own, kv_own, bounds, totals, d_outs, turned, deltas),
        grid=(kv_heads,),
        in_specs=[
            head_spec,
            pl.BlockSpec((rows, HEAD_WIDTH), lambda j: (0, j)),
            pl.BlockSpec((rows, HEAD_WIDTH), lambda j: (0, kv_heads + j)),
            pl.BlockSpec((blocks, 8, QROWS), lambda j: (0, 0, 0)),
            row_spec,
            head_spec,
            pl.BlockSpec((wide, rows), lambda j: (j, 0)),
            row_spec,
        ],
        out_specs=[
            head_spec,
            pl.BlockSpec((2, rows, HEAD_WIDTH), lambda j: (0, 0, j)),
        ],
        out_shape=[
            shape_of((rows, q_cols), bf16),
            shape_of((2, rows, kv_heads * HEAD_WIDTH), f32),
        ],
        mib=40,
        estimate=cost(10 * pairs * HEAD_WIDTH, 8 << 20, pairs, scale=1),
        name="attend_back_own",
        after=after,
    )


def mid_norm_kernel(x_ref, gain_ref, *refs):
    middle = x_ref[...].astype(f32)
    for ref in refs[:-2]:
        middle = middle + ref[...].astype(f32)
    refs[-2][...] = middle
    refs[-1][...] = (middle * norm_stats(middle) * gain_ref[...]).astype(bf16)


def mid_norm(hidden, gain, terms, after=()):
    rows, cols = hidden.shape
    spec = pl.BlockSpec((rows // 4, cols), lambda i: (i, 0))
    return call(
        mid_norm_kernel,
        (hidden, gain, *terms),
        grid=(4,),
        in_specs=[spec, pl.BlockSpec((1, cols), lambda i: (0, 0))] + [spec] * len(terms),
        out_specs=[spec, spec],
        out_shape=[shape_of((rows, cols), f32), shape_of((rows, cols), bf16)],
        estimate=cost(20 * rows * cols, 20 * rows * cols),
        name="mid_norm",
        after=after,
    )


def mid_back_kernel(own_ref, got_ref, middle_ref, grad_ref, gain_ref, out_ref, low_ref, sum_ref):
    @pl.when(pl.program_id(0) == 0)
    def clear():
        sum_ref[...] = jnp.zeros_like(sum_ref)

    d_normed = own_ref[...] + got_ref[...].astype(f32)
    middle = middle_ref[...]
    stats = norm_stats(middle)
    sum_ref[0:1, :] += jnp.sum(d_normed * (middle * stats), axis=0, keepdims=True)
    d_middle = grad_ref[...].astype(f32) + norm_back(d_normed, middle, stats, gain_ref[...])
    out_ref[...] = d_middle
    low_ref[...] = d_middle.astype(bf16)


def mid_back(own, got, middle, out_grad, gain, after=()):
    rows, cols = own.shape
    spec = pl.BlockSpec((rows // 4, cols), lambda i: (i, 0))
    return call(
        mid_back_kernel,
        (own, got, middle, out_grad, gain),
        grid=(4,),
        in_specs=[spec] * 4 + [pl.BlockSpec((1, cols), lambda i: (0, 0))],
        out_specs=[spec, spec, pl.BlockSpec((8, cols), lambda i: (0, 0))],
        out_shape=[
            shape_of((rows, cols), f32),
            shape_of((rows, cols), bf16),
            shape_of((8, cols), f32),
        ],
        estimate=cost(30 * rows * cols, 20 * rows * cols),
        name="mid_back",
        after=after,
    )


def mlp_kernel(
    x_own_ref, x_got_ref, g_own_ref, g_got_ref, wg_ref, wu_ref, wd_ref,
    mixed_ref, d_gate_ref, d_up_ref, d_mid_ref, d_mid_give_ref, out_ref, out_give_ref,
    x_ref, g_ref, d_mid_acc, out_acc
):
    step = pl.program_id(0)
    tokens = x_own_ref.shape[0]

    @pl.when(step == 0)
    def start():
        x_ref[:tokens, :] = x_own_ref[...]
        x_ref[tokens:, :] = x_got_ref[...]
        g_ref[:tokens, :] = g_own_ref[...]
        g_ref[tokens:, :] = g_got_ref[...]
        d_mid_acc[...] = jnp.zeros_like(d_mid_acc)
        out_acc[...] = jnp.zeros_like(out_acc)

    gate = nn_dot(x_ref[...], wg_ref[...])
    up = nn_dot(x_ref[...], wu_ref[...])
    d_mixed = nn_dot(g_ref[...], wd_ref[...])
    sig = 1.0 / (1.0 + jnp.exp(-gate))
    gated = gate * sig
    mixed = (gated * up).astype(bf16)
    d_gate = (d_mixed * up * sig * (1.0 + gate * (1.0 - sig))).astype(bf16)
    d_up = (d_mixed * gated).astype(bf16)
    mixed_ref[...] = mixed
    d_gate_ref[...] = d_gate
    d_up_ref[...] = d_up
    d_mid_acc[...] += nt_dot(d_gate, wg_ref[...]) + nt_dot(d_up, wu_ref[...])
    out_acc[...] += nt_dot(mixed, wd_ref[...])

    @pl.when(step == pl.num_programs(0) - 1)
    def finish():
        d_mid_ref[...] = d_mid_acc[:tokens, :]
        d_mid_give_ref[...] = d_mid_acc[tokens:, :].astype(bf16)
        out_ref[...] = out_acc[:tokens, :]
        out_give_ref[...] = out_acc[tokens:, :].astype(bf16)


def mlp(x_own, x_got, g_own, g_got, mlp_w, after=()):
    tokens, width = x_own.shape
    units = mlp_w.shape[1] // 3
    tile = 512
    steps = units // tile
    fixed = lambda j: (0, 0)
    rows_spec = pl.BlockSpec((tokens, width), fixed)
    tile_spec = pl.BlockSpec((2 * tokens, tile), lambda j: (0, j))
    tile_shape = shape_of((2 * tokens, units), bf16)
    return call(
        mlp_kernel,
        (x_own, x_got, g_own, g_got, mlp_w, mlp_w, mlp_w,),
        grid=(steps,),
        in_specs=[rows_spec] * 4
        + [
            pl.BlockSpec((width, tile), lambda j: (0, j)),
            pl.BlockSpec((width, tile), lambda j: (0, steps + j)),
            pl.BlockSpec((width, tile), lambda j: (0, 2 * steps + j)),
        ],
        out_specs=[tile_spec] * 3 + [rows_spec] * 4,
        out_shape=[tile_shape] * 3
        + [
            shape_of((tokens, width), f32),
            shape_of((tokens, width), bf16),
            shape_of((tokens, width), f32),
            shape_of((tokens, width), bf16),
        ],
        scratch=[
            pltpu.VMEM((2 * tokens, width), bf16),
            pltpu.VMEM((2 * tokens, width), bf16),
            pltpu.VMEM((2 * tokens, width), f32),
            pltpu.VMEM((2 * tokens, width), f32),
        ],
        mib=48,
        estimate=cost(12 * 2 * tokens * width * units, 16 << 20),
        name="mlp",
        after=after,
    )


def mlp_grad_kernel(own_ref, got_ref, d_ref, out_ref, turned_ref):
    tokens = own_ref.shape[0]

    @pl.when(pl.program_id(0) == 0)
    def start():
        turned_ref[:, :tokens] = own_ref[...].T
        turned_ref[:, tokens:] = got_ref[...].T

    out_ref[...] = nn_dot(turned_ref[...], d_ref[...]).astype(bf16)


def mlp_grad(own, got, d_units, after=()):
    tokens, width = own.shape
    units = d_units.shape[1]
    tile = 512
    fixed = lambda j: (0, 0)
    return call(
        mlp_grad_kernel,
        (own, got, d_units,),
        grid=(units // tile,),
        in_specs=[
            pl.BlockSpec((tokens, width), fixed),
            pl.BlockSpec((tokens, width), fixed),
            pl.BlockSpec((2 * tokens, tile), lambda j: (0, j)),
        ],
        out_specs=pl.BlockSpec((width, tile), lambda j: (0, j)),
        out_shape=shape_of((width, units), bf16),
        scratch=[pltpu.VMEM((width, 2 * tokens), bf16)],
        mib=32,
        estimate=cost(4 * tokens * width * units, 8 << 20),
        name="mlp_grad",
        after=after,
    )


def mlp_grad_pair_kernel(
    steps, own_a_ref, got_a_ref, d_a_ref, own_b_ref, got_b_ref, d_b_ref, out_ref, turned_ref
):
    step = pl.program_id(0)
    tokens = own_a_ref.shape[0]

    @pl.when(step == 0)
    def first():
        turned_ref[:, :tokens] = own_a_ref[...].T
        turned_ref[:, tokens:] = got_a_ref[...].T

    @pl.when(step == steps)
    def second():
        turned_ref[:, :tokens] = own_b_ref[...].T
        turned_ref[:, tokens:] = got_b_ref[...].T

    @pl.when(step < steps)
    def left():
        out_ref[...] = nn_dot(turned_ref[...], d_a_ref[...]).astype(bf16)

    @pl.when(step >= steps)
    def right():
        out_ref[...] = nn_dot(turned_ref[...], d_b_ref[...]).astype(bf16)


def mlp_grad_pair(own_a, got_a, d_a, own_b, got_b, d_b, after=()):
    tokens, width = own_a.shape
    units = d_a.shape[1]
    tile = 512
    steps = units // tile
    rows = pl.BlockSpec((tokens, width), lambda j: (0, 0))
    return call(
        functools.partial(mlp_grad_pair_kernel, steps),
        (own_a, got_a, d_a, own_b, got_b, d_b),
        grid=(2 * steps,),
        in_specs=[
            rows,
            rows,
            pl.BlockSpec((2 * tokens, tile), lambda j: (0, jnp.minimum(j, steps - 1))),
            rows,
            rows,
            pl.BlockSpec((2 * tokens, tile), lambda j: (0, jnp.maximum(j - steps, 0))),
        ],
        out_specs=pl.BlockSpec((width, tile), lambda j: (0, j)),
        scratch=[pltpu.VMEM((width, 2 * tokens), bf16)],
        out_shape=shape_of((width, 2 * units), bf16),
        mib=48,
        estimate=cost(8 * tokens * width * units, 16 << 20),
        name="mlp_grad_pair",
        after=after,
    )


def body(
    hidden_in,
    doc_lengths,
    pad_lengths,
    w_query,
    key_matrix,
    value_matrix,
    w_output,
    w_gate,
    w_up,
    w_down,
    attn_gain,
    mlp_gain,
    query_gain,
    key_gain,
    out_grad,
):
    core = lax.axis_index("c")
    chip = lax.axis_index("q")
    chips = lax.axis_size("q")
    group = chip * 2 + core
    part = lax.axis_index("seq")
    groups = chips * 2
    parts = lax.axis_size("seq")
    tokens, width = hidden_in.shape
    group_rows = tokens * parts
    slice_rows = width // groups
    units = FEEDFWD_UNITS // 2
    q_cols = QUERY_HEADS * HEAD_WIDTH // parts
    kv_cols = KEY_VALUE_HEADS * HEAD_WIDTH // parts
    attn_cols = q_cols + 2 * kv_cols
    pack_cols = attn_cols + q_cols
    core_at = core.astype(jnp.int32).reshape(1)
    part_at = part.astype(jnp.int32).reshape(1)
    chip_at = chip.astype(jnp.int32).reshape(1)

    def swapped(value):
        return lax.ppermute(value, "c", core_swap)

    def sent(value, shift):
        return lax.ppermute(value, "seq", [(i, (i + shift) % parts) for i in range(parts)])

    def from_all(value):
        return [value] + [sent(value, shift) for shift in range(1, parts)]

    def sent_chips(value, shift):
        return lax.ppermute(value, "q", [(i, (i + shift) % chips) for i in range(chips)])

    def line_step(value, step):
        return lax.ppermute(value, "seq", [(step - 1, step), (parts - step, parts - step - 1)])

    hidden_blocks = from_all(hidden_in)

    packed = pack_attn(
        part_at, parts, w_query, key_matrix, value_matrix, w_output,
        (attn_gain, mlp_gain, query_gain, key_gain),
    )
    attn_w = lax.all_gather(packed, dp_axes, axis=0, tiled=True)

    mlp_pack, mlp_give = pack_mlp(core_at, w_gate, w_up, w_down, after=(packed,))
    mlp_pack = lax.dynamic_update_slice_in_dim(
        mlp_pack, swapped(mlp_give), (1 - core) * slice_rows, 0
    )
    mlp_w = lax.all_gather(mlp_pack, "q", axis=0, tiled=True)
    grad_spread = jnp.where(
        (jnp.arange(2) == core)[:, None, None], jnp.zeros((), bf16), out_grad[None]
    )
    grad_got = lax.psum_scatter(grad_spread, "c", scatter_dimension=0, tiled=True)
    grad_got = grad_got.reshape(tokens, width)

    gains = read_gains(attn_w, pack_cols)
    head_piece = query_gain.shape[0]
    ga = gains[0:1]
    gm = gains[1:2]
    gqk = gains[2:4].reshape(2, groups, slice_rows)[:, :, :head_piece].reshape(2, HEAD_WIDTH)

    doc_ends = jnp.cumsum(doc_lengths)
    doc_starts = doc_ends - doc_lengths
    pad_starts = doc_ends - pad_lengths
    first = group * group_rows
    token = first + jnp.arange(group_rows, dtype=jnp.int32)
    inside = (token[:, None] >= doc_starts[None, :]) & (token[:, None] < doc_ends[None, :])
    start = jnp.sum(jnp.where(inside, doc_starts[None, :], 0), axis=1)
    pad_start = jnp.sum(jnp.where(inside, pad_starts[None, :], 0), axis=1)
    inv_freq = rope_base ** (-jnp.arange(HEAD_WIDTH // 2, dtype=f32) * 2.0 / HEAD_WIDTH)
    angles = (token - start).astype(f32)[:, None] * inv_freq[None, :]
    cosine = jnp.cos(angles)
    sine = jnp.sin(angles)
    cosine = jnp.concatenate([cosine, cosine], axis=1)
    sine = jnp.concatenate([-sine, sine], axis=1)
    offset = (token // QROWS) * QROWS - WINDOW_TOKENS
    low = jnp.maximum(start, token - (WINDOW_TOKENS - 1)) - offset
    high = jnp.minimum(token, pad_start - 1) - offset
    bounds = jnp.pad(
        jnp.stack([low.reshape(parts, QROWS), high.reshape(parts, QROWS)], axis=1),
        ((0, 0), (0, 6), (0, 0)),
    )

    normed_all, queries, kv_own, qk_proj = project(
        part_at, hidden_blocks, attn_w, ga, gqk, cosine, sine, q_cols, kv_cols
    )
    kv_tail = lax.ppermute(
        kv_own[group_rows - WINDOW_TOKENS :], dp_axes, [(i, i + 1) for i in range(groups - 1)]
    )
    own_outs, own_totals = attend_own(queries, kv_own, bounds)
    terms = []
    attn = [None] * parts
    totals = [None] * parts
    order = [shift for shift in range(1, parts)] + [0]
    for shift in order:
        attn[shift], totals[shift], term = attend_tail(
            shift, part_at, parts, queries, kv_tail, bounds, own_outs, own_totals, attn_w, attn_cols
        )
        terms.append(sent(term, shift) if shift else term)
    attn_all = jnp.zeros((group_rows, q_cols), bf16)
    totals_all = jnp.zeros((kv_cols // HEAD_WIDTH, 8, group_rows), f32)
    for shift in range(parts):
        row = (part + shift) % parts * tokens
        attn_all = lax.dynamic_update_slice_in_dim(attn_all, attn[shift], row, 0)
        totals_all = lax.dynamic_update_slice_in_dim(totals_all, totals[shift], row, 2)
    middle, normed_mid = mid_norm(hidden_in, gm, terms)

    mid_got = swapped(normed_mid)
    mixed, d_gate, d_up, d_mid, d_mid_give, out_part, out_give = mlp(
        normed_mid, mid_got, out_grad, grad_got, mlp_w
    )
    d_middle, d_proj, mlp_gain_rows = mid_back(
        d_mid, swapped(d_mid_give), middle, out_grad, gm
    )
    term_pair = mlp_grad_pair(
        out_grad, grad_got, mixed, normed_mid, mid_got, d_gate, after=(d_proj,)
    )
    d_proj_all = lax.all_gather(d_proj, "seq", axis=0, tiled=True)
    output_act = (middle + out_part + swapped(out_give).astype(f32)).astype(bf16)

    def chip_sums(grad):
        return lax.psum_scatter(grad, "q", scatter_dimension=0, tiled=True)

    own_pair = chip_sums(term_pair)
    term_up = mlp_grad(normed_mid, mid_got, d_up, after=(d_proj,))
    own_up = chip_sums(term_up)
    line = list(range(parts))

    def unpacked(sums, column, turned, after=()):
        give = lax.dynamic_slice(
            sums, ((1 - core) * slice_rows, column * units), (slice_rows, units)
        )
        return unpack_half(core_at, sums, swapped(give), column, turned, after=after)

    d_attn, turned, deltas, d_tail = attend_back_tail(
        queries, kv_tail, bounds, totals_all, attn_all, d_proj_all, attn_w, attn_cols,
        after=(term_up,),
    )
    d_tail = lax.ppermute(d_tail, dp_axes, [(i + 1, i) for i in range(groups - 1)])
    d_queries, d_kv = attend_back_own(
        queries, kv_own, bounds, totals_all, d_attn, turned, deltas
    )
    own_pair = touch(own_pair, after=(d_attn,))
    sum_pair = lax.psum(own_pair, "seq")
    w_out_grad = out_grad_sums([d_proj_all], [attn_all], after=(d_queries,))
    d_in, attn_term = project_back(
        part_at, groups, [hidden_blocks[(parts - k) % parts] for k in range(parts)],
        d_queries, d_kv, d_tail, qk_proj, attn_w, gqk, cosine, sine, normed_all, w_out_grad,
        mlp_gain_rows,
    )
    d_in = lax.psum_scatter(d_in, "seq", scatter_dimension=0, tiled=True)

    attn_grad = lax.psum_scatter(attn_term, dp_axes, scatter_dimension=0, tiled=True)
    got_up = [line_step(own_up, 1)]
    grad_down = unpacked(sum_pair, 0, True)
    grad_gate = unpacked(sum_pair, 1, False, after=(grad_down,))
    last = grad_gate
    for step in range(2, parts):
        last = add(own_up, got_up[-1], after=(last,))
        got_up.append(line_step(last, step))
    attn_grad = touch(attn_grad, after=(last,))
    attn_grads = lax.all_gather(attn_grad, "seq", axis=0)
    in_grad = finish_in(d_in, d_middle, hidden_in, ga)
    sum_up = sum_all([own_up, *got_up], after=(attn_grad,))
    grad_up = unpacked(sum_up, 0, False)
    gain_sums = jnp.sum(attn_grads[:, :, pack_cols : pack_cols + 4].astype(f32), axis=0)
    grad_query, grad_key, grad_value, grad_output = unpack_attn(
        attn_grads, q_cols, kv_cols, after=(grad_up, in_grad)
    )
    return (
        output_act,
        in_grad,
        grad_query,
        grad_key,
        grad_value,
        grad_output,
        grad_gate,
        grad_up,
        grad_down,
        gain_sums[:, 0],
        gain_sums[:, 1],
        gain_sums[:head_piece, 2],
        gain_sums[:head_piece, 3],
    )


def solution(mesh):
    groups, parts = mesh.devices.shape
    mesh = Mesh(mesh.devices.reshape(groups // 2, 2, parts), ("q", "c", "seq"))
    tokens = P(("q", "c", "seq"), None)
    rows = P(dp_axes, None)
    cols = P(None, dp_axes)
    flat = P(dp_axes)
    in_specs = (
        tokens, P(), P(), rows, rows, rows, cols, rows, rows, cols, flat, flat, flat, flat, tokens,
    )
    out_specs = (
        tokens, tokens, rows, rows, rows, cols, rows, rows, cols, flat, flat, flat, flat,
    )
    return jax.shard_map(body, mesh=mesh, in_specs=in_specs, out_specs=out_specs, check_vma=False)
```

time: 564 us -> 484 us (0.86)
  waiting for transfers between devices: 303 us -> 219 us
  local copies, waits for them, and re-layouts: 16.7 us -> 54.8 us
  matrix products: 32.2 us -> 0 us
  Pallas kernels: 98.4 us -> 124 us
  other arithmetic: 29.3 us -> 6.7 us
  starting transfers between devices: 60.7 us -> 52.9 us
    psum x1, waiting for transfers between devices: 129 us -> 19.2 us  [body(): sum_pair = lax.psum(own_pair, 'seq')]
    ppermute x12 -> x6, waiting for transfers between devices: 75.6 us -> 10.6 us  [sent(): lax.ppermute(value, 'seq', [(i, (i + shift) % parts) for i in range(parts)])]
    ppermute x8 -> x11, waiting for transfers between devices: 9.14 us -> 73.6 us  [the longest x3 72.4 us: line_step(): lax.ppermute(value, 'seq', [(step - 1, step), (parts - step, parts - step...]
    unnamed x52 -> x144, local copies, waits for them, and re-layouts: 5.1 us -> 47.2 us
    dot_general x7 -> x0, matrix products: 32.2 us -> none  [the longest x3 11.5 us: tn_dot(): lax.dot_general(left, right, (((0,), (0,)), ((), ())), preferred_element_...]
    pallas_call x12 -> x28, Pallas kernels: 98.4 us -> 124 us  [call(): pl.pallas_call(body_of, grid_spec=pltpu.PrefetchScalarGridSpec(num_scalar...]
    reduce_scatter x2 -> x5, waiting for transfers between devices: 37.4 us -> 55.8 us  [the longest x2 25.6 us: chip_sums(): return lax.psum_scatter(grad, 'q', scatter_dimension=0, tiled=True)]
    all_gather x1, waiting for transfers between devices: 0.01 us -> 11.1 us  [body(): mlp_w = lax.all_gather(mlp_pack, 'q', axis=0, tiled=True)]
  transfers between devices with their start and end apart: 27 -> 28, of which waited for: 12 -> 14; matrix products, arithmetic and copies ran while one was open for 9% -> 3% of each run, Pallas kernels for 17% -> 22%
where the time goes in v3:
time: 484 us; the launch traced here: 475 us
  waiting for transfers between devices  219 us (45%)
  Pallas kernels  124 us (26%)
  local copies, waits for them, and re-layouts  54.8 us (11%)
  starting transfers between devices  52.9 us (11%)
  between operations  17 us (4%)
  other arithmetic  6.7 us (1%)
    pallas_call x28, Pallas kernels, call(): pl.pallas_call(body_of, grid_spec=pltpu.PrefetchScalarGridSpec(num_scalar...  124 us
    ppermute x3, waiting for transfers between devices, line_step(): lax.ppermute(value, 'seq', [(step - 1, step), (parts - step, parts - step...  72.4 us
    unnamed x144, local copies, waits for them, and re-layouts  47.2 us
    all_gather x1, waiting for transfers between devices, body(): d_proj_all = lax.all_gather(d_proj, 'seq', axis=0, tiled=True)  32.9 us
    reduce_scatter x2, waiting for transfers between devices, chip_sums(): return lax.psum_scatter(grad, 'q', scatter_dimension=0, tiled=True)  25.6 us
    ppermute x6, starting transfers between devices, sent(): lax.ppermute(value, 'seq', [(i, (i + shift) % parts) for i in range(parts)])  25.1 us
    psum x1, waiting for transfers between devices, body(): sum_pair = lax.psum(own_pair, 'seq')  19.2 us
    reduce_scatter x1, waiting for transfers between devices, body(): lax.psum_scatter(attn_term, dp_axes, scatter_dimension=0, tiled=True)  18.5 us
  transfers between devices with their start and end apart: 28, of which 14 were waited for; matrix products, arithmetic and copies ran while one was open for 3% of the time, Pallas kernels for 22%

profile of v3, /device:TPU:0, one launch (start us, length us, event | category | flops | bytes accessed | tf_op | source)
XLA Modules:
  0.0 474.9 jit_solution(8591914921716966686)
XLA Ops:
  10.2 3.1 collective-permute-start
  13.3 2.6 collective-permute-start.1
  32.2 15.3 %all-gather.6.cloned.1.call-done.refs_0_.refs_5_.refs_7_.refs_9_ = bf16[1024,1664]{1,0:T(8,128)(2,1)} async-done(((bf16[128,1664]{1,0:T(8,128)(2,1)}), bf16[1024,1664]{1,0:T(8,128)(2,1)}) %all-gather.6.cloned.1.call-update) | async-done | bytes 3407888 | tf_op jit(solution)/shard_map/all_gather | solution.py:1191
  53.5 5.9 %project.1 = (bf16[1024,1024]{1,0:T(8,128)(2,1)S(1)}, bf16[1024,512]{1,0:T(8,128)(2,1)S(1)}, bf16[1024,512]{1,0:T(8,128)(2,1)S(1)}, f32[1024,768]{1,0:T(8,128)S(1)}) custom-call(s32[1]{0:T(128)} %bitcast.refs_0_, bf16[256,1024]{1,0:T(8,128)(2,1)} %refs_2_.7, bf16[256,1024]{1,0:T(8,128)(2,1)} %collective-permute-done.refs_2_.refs_4_, ...), custom_call_target="tpu_custom_call" | custom-call | flops 214748364800 | bytes 1258291200 | tf_op jit(solution)/shard_map/project/pallas_call | solution.py:54
  62.3 2.2 collective-permute-start.3
  64.6 5.3 %attend_own.1 = (f32[512,1024]{1,0:T(8,128)S(1)}, f32[2,8,1024]{2,1,0:T(8,128)S(1)}) custom-call(bf16[1024,512]{1,0:T(8,128)(2,1)S(1)} %get-tuple-element.57.refs_0_.refs_1_, bf16[1024,512]{1,0:T(8,128)(2,1)S(1)} %get-tuple-element.58.refs_1_.refs_2_, bf16[1024,512]{1,0:T(8,128)(2,1)S(1)} %get-tuple-element.58.refs_1_.refs_2_, ...), custom_call_target="tpu_custom_call" | custom-call | flops 134217728000 | bytes 419430400 | tf_op jit(solution)/shard_map/attend_own/pallas_call | solution.py:54
  69.9 3.5 attend_tail.6
  74.1 12.2 %collective-permute-start.6 = (bf16[256,1024]{1,0:T(8,128)(2,1)}, bf16[256,1024]{1,0:T(8,128)(2,1)}, u32[]{:S(2)}, u32[]{:S(2)}) collective-permute-start(bf16[256,1024]{1,0:T(8,128)(2,1)} %get-tuple-element.63), channel_id=1, source_target_pairs={{0,3},{1,0},{2,1},{3,2},{4,7},{5,4},{6,5},{7,6},{8,11},{9,8},{10,9... | collective-permute-start | bytes 1572872 | tf_op jit(solution)/shard_map/ppermute | solution.py:1174
  86.3 3.9 attend_tail.5
  90.9 5.9 %collective-permute-start.5 = (bf16[256,1024]{1,0:T(8,128)(2,1)S(1)}, bf16[256,1024]{1,0:T(8,128)(2,1)S(1)}, u32[]{:S(2)}, u32[]{:S(2)}) collective-permute-start(bf16[256,1024]{1,0:T(8,128)(2,1)S(1)} %get-tuple-element.62), channel_id=1, source_target_pairs={{0,2},{1,3},{2,0},{3,1},{4,6},{5,7},{6,4},{7,5},{8,10},{9,11},{10,... | collective-permute-start | bytes 1572872 | tf_op jit(solution)/shard_map/ppermute | solution.py:1174
  96.8 5.1 %attend_tail.4 = (bf16[256,512]{1,0:T(8,128)(2,1)S(1)}, f32[2,8,256]{2,1,0:T(8,128)S(1)}, bf16[256,1024]{1,0:T(8,128)(2,1)S(1)}) custom-call(s32[1]{0:T(128)} %bitcast.refs_0_, bf16[1024,512]{1,0:T(8,128)(2,1)S(1)} %get-tuple-element.57.refs_0_.refs_1_, bf16[1024,512]{1,0:T(8,128)(2,1)S(1)} %collective-permute-done.3.refs_2_.refs_3_.refs_1_, ...), custom_call_target="tpu_custom_call" | custom-call | flops 53687091200 | bytes 419430400 | tf_op jit(solution)/shard_map/attend_tail/pallas_call | solution.py:54
  102.6 6.4 %attend_tail.7 = (bf16[256,512]{1,0:T(8,128)(2,1)S(1)}, f32[2,8,256]{2,1,0:T(8,128)S(1)}, bf16[256,1024]{1,0:T(8,128)(2,1)S(1)}) custom-call(s32[1]{0:T(128)} %bitcast.refs_0_, bf16[1024,512]{1,0:T(8,128)(2,1)S(1)} %get-tuple-element.57.refs_0_.refs_1_, bf16[1024,512]{1,0:T(8,128)(2,1)S(1)} %collective-permute-done.3.refs_2_.refs_3_.refs_1_, ...), custom_call_target="tpu_custom_call" | custom-call | flops 53687091200 | bytes 419430400 | tf_op jit(solution)/shard_map/attend_tail/pallas_call | solution.py:54
  109.6 9.6 %collective-permute-done.4.refs_2_ = bf16[256,1024]{1,0:T(8,128)(2,1)S(1)} collective-permute-done((bf16[256,1024]{1,0:T(8,128)(2,1)S(1)}, bf16[256,1024]{1,0:T(8,128)(2,1)S(1)}, u32[]{:S(2)}, u32[]{:S(2)}) %collective-permute-start.4) | collective-permute-done | bytes 524320 | tf_op jit(solution)/shard_map/ppermute | solution.py:1174
  119.2 2.6 mid_norm.1
  121.7 17.2 %collective-permute-start.7 = (bf16[256,1024]{1,0:T(8,128)(2,1)S(1)}, bf16[256,1024]{1,0:T(8,128)(2,1)S(1)}, u32[]{:S(2)}, u32[]{:S(2)}) collective-permute-start(bf16[256,1024]{1,0:T(8,128)(2,1)S(1)} %get-tuple-element.66.refs_0_.refs_3_), channel_id=1, source_target_pairs={{0,4},{4,0},{1,5},{5,1},{2,6},{6,2},{3,7},{7,3},{8,12},{12,8},{9,1... | collective-permute-start | bytes 1572872 | tf_op jit(solution)/shard_map/ppermute | solution.py:1171
  141.4 11.1 %all-gather.8.cloned.1.call-done.refs_4_.refs_5_.refs_6_ = bf16[1024,4608]{1,0:T(8,128)(2,1)} async-done(((bf16[256,4608]{1,0:T(8,128)(2,1)}), bf16[1024,4608]{1,0:T(8,128)(2,1)}) %all-gather.8.cloned.1.call-update) | async-done | bytes 9437200 | tf_op jit(solution)/shard_map/all_gather | solution.py:1197
  153.5 14.8 %mlp.1 = (bf16[512,1536]{1,0:T(8,128)(2,1)}, bf16[512,1536]{1,0:T(8,128)(2,1)}, bf16[512,1536]{1,0:T(8,128)(2,1)}, f32[256,1024]{1,0:T(8,128)S(1)}, bf16[256,102...) custom-call(bf16[256,1024]{1,0:T(8,128)(2,1)S(1)} %get-tuple-element.66.refs_0_.refs_3_, ...), custom_call_target="tpu_custom_call" | custom-call | flops 966367641600 | bytes 1677721600 | tf_op jit(solution)/shard_map/mlp/pallas_call | solution.py:54
  177.2 6.8 %mlp_grad_pair.1 = bf16[1024,3072]{1,0:T(8,128)(2,1)} custom-call(bf16[256,1024]{1,0:T(8,128)(2,1)S(1)} %copy-done.26, bf16[256,1024]{1,0:T(8,128)(2,1)S(1)} %bitcast.23, bf16[512,1536]{1,0:T(8,128)(2,1)S(1)} %copy-done.67, bf16[256,1024]{1,0:T(8,128)(2,1)S(1)} %get-tuple-element.66.refs_0_.refs_3_, ...), custom_call_target="tpu_custom_call" | custom-call | flops 322122547200 | bytes 1677721600 | tf_op jit(solution)/shard_map/mlp_grad_pair/pallas_call | solution.py:54
  185.6 2.8 mlp_grad.1.refs_8_
  190.2 32.9 %all-gather.10.cloned.1.call-done.refs_6_.refs_0_ = bf16[1024,1024]{1,0:T(8,128)(2,1)} async-done(((bf16[256,1024]{1,0:T(8,128)(2,1)}), bf16[1024,1024]{1,0:T(8,128)(2,1)}) %all-gather.10.cloned.1.call-update) | async-done | bytes 2097168 | tf_op jit(solution)/shard_map/all_gather | solution.py:1266
  227.9 14.4 %attend_back_tail.1 = (bf16[1024,512]{1,0:T(8,128)(2,1)S(1)}, f32[512,1024]{1,0:T(8,128)S(1)}, f32[2,8,1024]{2,1,0:T(8,128)S(1)}, bf16[2,1024,256]{2,1,0:T(8,128)(2,1)S(1)}) custom-call(bf16[1024,512]{1,0:T(8,128)(2,1)S(1)} %copy-done.64, bf16[1024,512]{1,0:T(8,128)(2,1)S(1)} %copy-done.56, bf16[1024,512]{1,0:T(8,128)(2,1)S(1)} %copy-done.56, ...), custom_call_target="tpu_custom_call" | custom-call | flops 442918502400 | bytes 838860800 | tf_op jit(solution)/shard_map/attend_back_tail/pallas_call | solution.py:54
  244.7 13.1 %reduce-scatter.14.cloned.1.call-done.refs_0_ = bf16[256,3072]{1,0:T(8,128)(2,1)} async-done(((bf16[1024,3072]{1,0:T(8,128)(2,1)}), bf16[256,3072]{1,0:T(8,128)(2,1)}) %reduce-scatter.14.cloned.1.call-update) | async-done | bytes 1572880 | tf_op jit(solution)/shard_map/reduce_scatter | solution.py:1270
  265.3 12.7 %attend_back_own.1 = (bf16[1024,512]{1,0:T(8,128)(2,1)S(1)}, f32[2,1024,256]{2,1,0:T(8,128)S(1)}) custom-call(bf16[1024,512]{1,0:T(8,128)(2,1)S(1)} %copy-done.65, bf16[1024,512]{1,0:T(8,128)(2,1)S(1)} %copy-done.54, bf16[1024,512]{1,0:T(8,128)(2,1)S(1)} %copy-done.54, s32[4,8,256]{2,1,0:T(8,128)S(1)} %pad.4.refs_3_.refs_4_, ...), custom_call_target="tpu_custom_call" | custom-call | flops 3355443200 | bytes 8388608 | tf_op jit(solution)/shard_map/attend_back_own/pallas_call | solution.py:54
  278.1 2.2 out_grad.1.refs_14_
  281.4 18.8 %project_back.1 = (bf16[1024,1024]{1,0:T(8,128)(2,1)}, bf16[1024,1664]{1,0:T(8,128)(2,1)}) custom-call(s32[1]{0:T(128)} %bitcast.refs_0_, bf16[256,1024]{1,0:T(8,128)(2,1)} %refs_2_.7, bf16[256,1024]{1,0:T(8,128)(2,1)} %collective-permute-done.2.refs_4_.refs_2_, bf16[256,1024]{1,0:T(8,128)(2,1)} %collective-permute-done.1.refs_3_, ...), custom_call_target="tpu_custom_call" | custom-call | flops 4294967296 | bytes 16777216 | tf_op jit(solution)/shard_map/project_back/pallas_call | solution.py:54
  300.8 12.5 %reduce-scatter.12.cloned.1.call-done.refs_0_ = bf16[256,1536]{1,0:T(8,128)(2,1)} async-done(((bf16[1024,1536]{1,0:T(8,128)(2,1)}), bf16[256,1536]{1,0:T(8,128)(2,1)}) %reduce-scatter.12.cloned.1.call-update) | async-done | bytes 786448 | tf_op jit(solution)/shard_map/reduce_scatter | solution.py:1270
  313.3 3.4 collective-permute-start.12
  316.7 19.2 %all-reduce.3.cloned.1.call-done.refs_1_ = bf16[256,3072]{1,0:T(8,128)(2,1)} async-done(((bf16[256,3072]{1,0:T(8,128)(2,1)}), bf16[256,3072]{1,0:T(8,128)(2,1)}) %all-reduce.3.cloned.1.call-update) | async-done | bytes 1572880 | tf_op jit(solution)/shard_map/psum | solution.py:1292
  346.0 18.5 %reduce-scatter.10.cloned.1.call-done.refs_0_ = bf16[128,1664]{1,0:T(8,128)(2,1)} async-done(((bf16[1024,1664]{1,0:T(8,128)(2,1)}), bf16[128,1664]{1,0:T(8,128)(2,1)}) %reduce-scatter.10.cloned.1.call-update) | async-done | bytes 426000 | tf_op jit(solution)/shard_map/reduce_scatter | solution.py:1301
  368.3 72.1 %collective-permute-done.16.refs_3_ = bf16[256,1536]{1,0:T(8,128)(2,1)S(1)} collective-permute-done((bf16[256,1536]{1,0:T(8,128)(2,1)S(1)}, bf16[256,1536]{1,0:T(8,128)(2,1)S(1)}, u32[]{:S(2)}, u32[]{:S(2)}) %collective-permute-start.16) | collective-permute-done | bytes 786464 | tf_op jit(solution)/shard_map/ppermute | solution.py:1183
  442.0 11.7 %reduce-scatter.8.cloned.1.call-done.refs_0_ = bf16[256,1024]{1,0:T(8,128)(2,1)} async-done(((bf16[1024,1024]{1,0:T(8,128)(2,1)}), bf16[256,1024]{1,0:T(8,128)(2,1)}) %reduce-scatter.8.cloned.1.call-update) | async-done | bytes 524304 | tf_op jit(solution)/shard_map/reduce_scatter | solution.py:1299
  454.7 3.6 finish_in.1.refs_2_
  (239 shorter events, 86.8 us)
Async XLA Ops:
  8.0 39.4 %all-gather.6.cloned.1.call-start = ((), (), s32[]{:S(2)}) async-start(), calls=%async_computation.5 | async-start | bytes 3833856 | tf_op jit(solution)/shard_map/all_gather | solution.py:1191
  10.1 131.3 %reduce-scatter.6.cloned.1.call-start = ((), (), s32[]{:S(2)}) async-start(), calls=%async_computation.6 | async-start | bytes 1572864 | tf_op jit(solution)/shard_map/reduce_scatter | solution.py:1201
  10.2 39.5 %collective-permute-start = (bf16[256,1024]{1,0:T(8,128)(2,1)}, bf16[256,1024]{1,0:T(8,128)(2,1)}, u32[]{:S(2)}, u32[]{:S(2)}) collective-permute-start(bf16[256,1024]{1,0:T(8,128)(2,1)} %refs_2_.7), channel_id=1, source_target_pairs={{0,1},{1,2},{2,3},{3,0},{4,5},{5,6},{6,7},{7,4},{8,9},{9,10},{10,1... | collective-permute-start | bytes 1572872 | tf_op jit(solution)/shard_map/ppermute | solution.py:1174
  13.3 36.9 %collective-permute-start.1 = (bf16[256,1024]{1,0:T(8,128)(2,1)}, bf16[256,1024]{1,0:T(8,128)(2,1)}, u32[]{:S(2)}, u32[]{:S(2)}) collective-permute-start(bf16[256,1024]{1,0:T(8,128)(2,1)} %refs_2_.7), channel_id=1, source_target_pairs={{0,2},{1,3},{2,0},{3,1},{4,6},{5,7},{6,4},{7,5},{8,10},{9,11},{10,... | collective-permute-start | bytes 1572872 | tf_op jit(solution)/shard_map/ppermute | solution.py:1174
  15.9 34.3 %collective-permute-start.2 = (bf16[256,1024]{1,0:T(8,128)(2,1)}, bf16[256,1024]{1,0:T(8,128)(2,1)}, u32[]{:S(2)}, u32[]{:S(2)}) collective-permute-start(bf16[256,1024]{1,0:T(8,128)(2,1)} %refs_2_.7), channel_id=1, source_target_pairs={{0,3},{1,0},{2,1},{3,2},{4,7},{5,4},{6,5},{7,6},{8,11},{9,8},{10,9... | collective-permute-start | bytes 1572872 | tf_op jit(solution)/shard_map/ppermute | solution.py:1174
  24.2 4.9 %collective-permute-start.8 = (bf16[128,4608]{1,0:T(8,128)(2,1)}, bf16[128,4608]{1,0:T(8,128)(2,1)}, u32[]{:S(2)}, u32[]{:S(2)}) collective-permute-start(bf16[128,4608]{1,0:T(8,128)(2,1)} %get-tuple-element.68), channel_id=1, source_target_pairs={{0,4},{4,0},{1,5},{5,1},{2,6},{6,2},{3,7},{7,3},{8,12},{12,8},{9,1... | collective-permute-start | bytes 3538952 | tf_op jit(solution)/shard_map/ppermute | solution.py:1171
  25.4 127.1 %all-gather.8.cloned.1.call-start = ((), (), s32[]{:S(2)}) async-start(), calls=%async_computation.7 | async-start | bytes 11796480 | tf_op jit(solution)/shard_map/all_gather | solution.py:1197
  32.1 191.0 %all-gather.10.cloned.1.call-start = ((), (), s32[]{:S(2)}) async-start(), calls=%async_computation.8 | async-start | bytes 2621440 | tf_op jit(solution)/shard_map/all_gather | solution.py:1266
  49.7 69.5 %copy-start.47 = (f32[1,1024]{1,0:T(1,128)}, f32[1,1024]{1,0:T(1,128)S(1)}, u32[]{:S(2)}) copy-start(f32[1,1024]{1,0:T(1,128)S(1)} %get-tuple-element.110.refs_1_.refs_4_) | copy-start | bytes 12292
  62.3 7.5 %collective-permute-start.3 = (bf16[1024,512]{1,0:T(8,128)(2,1)S(1)}, bf16[1024,512]{1,0:T(8,128)(2,1)S(1)}, u32[]{:S(2)}, u32[]{:S(2)}) collective-permute-start(bf16[1024,512]{1,0:T(8,128)(2,1)S(1)} %get-tuple-element.58.refs_1_.refs_2_), channel_id=1, source_target_pairs={{0,4},{4,8},{8,12},{12,16},{16,20},{20,24},{24,28},{1,5},{5,9},{9,... | collective-permute-start | bytes 3145736 | tf_op jit(solution)/shard_map/ppermute | solution.py:1235
  74.1 34.9 %collective-permute-start.6 = (bf16[256,1024]{1,0:T(8,128)(2,1)}, bf16[256,1024]{1,0:T(8,128)(2,1)}, u32[]{:S(2)}, u32[]{:S(2)}) collective-permute-start(bf16[256,1024]{1,0:T(8,128)(2,1)} %get-tuple-element.63), channel_id=1, source_target_pairs={{0,3},{1,0},{2,1},{3,2},{4,7},{5,4},{6,5},{7,6},{8,11},{9,8},{10,9... | collective-permute-start | bytes 1572872 | tf_op jit(solution)/shard_map/ppermute | solution.py:1174
  90.9 18.7 %collective-permute-start.5 = (bf16[256,1024]{1,0:T(8,128)(2,1)S(1)}, bf16[256,1024]{1,0:T(8,128)(2,1)S(1)}, u32[]{:S(2)}, u32[]{:S(2)}) collective-permute-start(bf16[256,1024]{1,0:T(8,128)(2,1)S(1)} %get-tuple-element.62), channel_id=1, source_target_pairs={{0,2},{1,3},{2,0},{3,1},{4,6},{5,7},{6,4},{7,5},{8,10},{9,11},{10,... | collective-permute-start | bytes 1572872 | tf_op jit(solution)/shard_map/ppermute | solution.py:1174
  102.6 16.6 %collective-permute-start.4 = (bf16[256,1024]{1,0:T(8,128)(2,1)S(1)}, bf16[256,1024]{1,0:T(8,128)(2,1)S(1)}, u32[]{:S(2)}, u32[]{:S(2)}) collective-permute-start(bf16[256,1024]{1,0:T(8,128)(2,1)S(1)} %get-tuple-element.61), channel_id=1, source_target_pairs={{0,1},{1,2},{2,3},{3,0},{4,5},{5,6},{6,7},{7,4},{8,9},{9,10},{10,1... | collective-permute-start | bytes 1572872 | tf_op jit(solution)/shard_map/ppermute | solution.py:1174
  121.7 49.3 %copy-start.8 = (f32[256,1024]{1,0:T(8,128)}, f32[256,1024]{1,0:T(8,128)S(1)}, u32[]{:S(2)}) copy-start(f32[256,1024]{1,0:T(8,128)S(1)} %get-tuple-element.65.refs_2_) | copy-start | bytes 3145732
  121.7 19.7 %collective-permute-start.7 = (bf16[256,1024]{1,0:T(8,128)(2,1)S(1)}, bf16[256,1024]{1,0:T(8,128)(2,1)S(1)}, u32[]{:S(2)}, u32[]{:S(2)}) collective-permute-start(bf16[256,1024]{1,0:T(8,128)(2,1)S(1)} %get-tuple-element.66.refs_0_.refs_3_), channel_id=1, source_target_pairs={{0,4},{4,0},{1,5},{5,1},{2,6},{6,2},{3,7},{7,3},{8,12},{12,8},{9,1... | collective-permute-start | bytes 1572872 | tf_op jit(solution)/shard_map/ppermute | solution.py:1171
  168.4 2.6 collective-permute-start.10
  174.1 83.7 %reduce-scatter.14.cloned.1.call-start = ((), (), s32[]{:S(2)}) async-start(), calls=%async_computation.12 | async-start | bytes 7864320 | tf_op jit(solution)/shard_map/reduce_scatter | solution.py:1270
  184.1 129.2 %reduce-scatter.12.cloned.1.call-start = ((), (), s32[]{:S(2)}) async-start(), calls=%async_computation.11 | async-start | bytes 3932160 | tf_op jit(solution)/shard_map/reduce_scatter | solution.py:1270
  190.2 145.7 %all-reduce.3.cloned.1.call-start = ((), (), s32[]{:S(2)}) async-start(), calls=%async_computation.13 | async-start | bytes 3145728 | tf_op jit(solution)/shard_map/psum | solution.py:1292
  260.9 103.6 %reduce-scatter.10.cloned.1.call-start = ((), (), s32[]{:S(2)}) async-start(), calls=%async_computation.10 | async-start | bytes 3833856 | tf_op jit(solution)/shard_map/reduce_scatter | solution.py:1301
  261.0 20.4 %collective-permute-start.11 = (bf16[2,1024,256]{2,1,0:T(8,128)(2,1)}, bf16[2,1024,256]{2,1,0:T(8,128)(2,1)S(1)}, u32[]{:S(2)}, u32[]{:S(2)}) collective-permute-start(bf16[2,1024,256]{2,1,0:T(8,128)(2,1)} %copy-done.57), channel_id=1, source_target_pairs={{4,0},{8,4},{12,8},{16,12},{20,16},{24,20},{28,24},{5,1},{9,5},{13... | collective-permute-start | bytes 3145736 | tf_op jit(solution)/shard_map/ppermute | solution.py:1287
  300.1 153.5 %reduce-scatter.8.cloned.1.call-start = ((), (), s32[]{:S(2)}) async-start(), calls=%async_computation.9 | async-start | bytes 2621440 | tf_op jit(solution)/shard_map/reduce_scatter | solution.py:1299
  300.7 158.8 %all-gather.12.cloned.1.call-start = ((), (), s32[]{:S(2)}) async-start(), calls=%async_computation.14 | async-start | bytes 2129920 | tf_op jit(solution)/shard_map/all_gather | solution.py:1310
  313.3 30.1 %collective-permute-start.12 = (bf16[256,1536]{1,0:T(8,128)(2,1)}, bf16[256,1536]{1,0:T(8,128)(2,1)S(1)}, u32[]{:S(2)}, u32[]{:S(2)}) collective-permute-start(bf16[256,1536]{1,0:T(8,128)(2,1)} %reduce-scatter.12.cloned.1.call-done.refs_0_), channel_id=1, source_target_pairs={{0,1},{3,2},{4,5},{7,6},{8,9},{11,10},{12,13},{15,14},{16,17},{19,... | collective-permute-start | bytes 2359304 | tf_op jit(solution)/shard_map/ppermute | solution.py:1183
  337.2 1.8 collective-permute-start.14
  337.3 3.1 collective-permute-start.13
  345.0 0.7 collective-permute-start.15
  366.9 73.5 %collective-permute-start.16 = (bf16[256,1536]{1,0:T(8,128)(2,1)S(1)}, bf16[256,1536]{1,0:T(8,128)(2,1)S(1)}, u32[]{:S(2)}, u32[]{:S(2)}) collective-permute-start(bf16[256,1536]{1,0:T(8,128)(2,1)S(1)} %add.213.refs_1_), channel_id=1, source_target_pairs={{2,3},{1,0},{6,7},{5,4},{10,11},{9,8},{14,15},{13,12},{18,19},{17,... | collective-permute-start | bytes 2359304 | tf_op jit(solution)/shard_map/ppermute | solution.py:1183
  368.2 72.8 %copy-start.9 = (f32[256,1024]{1,0:T(8,128)S(1)}, f32[256,1024]{1,0:T(8,128)}, u32[]{:S(2)}) copy-start(f32[256,1024]{1,0:T(8,128)} %copy-done.8) | copy-start | bytes 3145732
  368.2 72.8 %copy-start.34 = (f32[256,1024]{1,0:T(8,128)S(1)}, f32[256,1024]{1,0:T(8,128)}, u32[]{:S(2)}) copy-start(f32[256,1024]{1,0:T(8,128)} %copy-done.33) | copy-start | bytes 3145732
  368.2 72.7 %collective-permute-start.9 = (bf16[256,1024]{1,0:T(8,128)(2,1)}, bf16[256,1024]{1,0:T(8,128)(2,1)S(1)}, u32[]{:S(2)}, u32[]{:S(2)}) collective-permute-start(bf16[256,1024]{1,0:T(8,128)(2,1)} %copy-done.60), channel_id=1, source_target_pairs={{0,4},{4,0},{1,5},{5,1},{2,6},{6,2},{3,7},{7,3},{8,12},{12,8},{9,1... | collective-permute-start | bytes 1572872 | tf_op jit(solution)/shard_map/ppermute | solution.py:1171
  440.9 17.5 %collective-permute-start.17 = (bf16[128,1536]{1,0:T(8,128)(2,1)S(1)}, bf16[128,1536]{1,0:T(8,128)(2,1)S(1)}, u32[]{:S(2)}, u32[]{:S(2)}) collective-permute-start(bf16[128,1536]{1,0:T(8,128)(2,1)S(1)} %constant_dynamic-slice_fusion), channel_id=1, source_target_pairs={{0,4},{4,0},{1,5},{5,1},{2,6},{6,2},{3,7},{7,3},{8,12},{12,8},{9,1... | collective-permute-start | bytes 1179656 | tf_op jit(solution)/shard_map/ppermute | solution.py:1171
  (67 other events, 370.3 us)
Sparse Core Ops, SparseCore 0:
  11.3 36.1 all-gather.5
  49.4 103.0 all-gather.7
  184.2 73.5 reduce-scatter.13
  260.9 52.3 reduce-scatter.11
  317.0 47.4 reduce-scatter.9
  366.7 86.9 reduce-scatter.7
Sparse Core Ops, SparseCore 1:
  25.5 6.9 reduce-scatter.5
  174.2 48.8 all-gather.9
  261.0 74.8 all-reduce.2
  367.0 84.7 all-gather.11

commit v4 on v3

--- a/solution.py
+++ b/solution.py
@@ -130,26 +130,6 @@
     )
 
 
-def add_kernel(left_ref, right_ref, out_ref):
-    out_ref[...] = (left_ref[...].astype(f32) + right_ref[...].astype(f32)).astype(bf16)
-
-
-def add(left, right, after=()):
-    rows, cols = left.shape
-    spec = pl.BlockSpec((rows // 4, cols), lambda i: (i, 0))
-    return call(
-        add_kernel,
-        (left, right),
-        grid=(4,),
-        in_specs=[spec, spec],
-        out_specs=spec,
-        out_shape=shape_of((rows, cols), bf16),
-        estimate=cost(rows * cols, 6 * rows * cols),
-        name="add",
-        after=after,
-    )
-
-
 def touch_kernel(in_ref, out_ref):
     out_ref[...] = in_ref[...]
 
@@ -170,30 +150,6 @@
     )
 
 
-def sum_kernel(*refs):
-    total = refs[0][...].astype(f32)
-    for ref in refs[1:-1]:
-        total = total + ref[...].astype(f32)
-    refs[-1][...] = total.astype(bf16)
-
-
-def sum_all(terms, after=()):
-    rows, cols = terms[0].shape
-    steps = 4 if rows % 64 == 0 else 1
-    spec = pl.BlockSpec((rows // steps, cols), lambda i: (i, 0))
-    return call(
-        sum_kernel,
-        tuple(terms),
-        grid=(steps,),
-        in_specs=[spec] * len(terms),
-        out_specs=spec,
-        out_shape=shape_of((rows, cols), bf16),
-        estimate=cost(len(terms) * rows * cols, 2 * (len(terms) + 1) * rows * cols),
-        name="sum_all",
-        after=after,
-    )
-
-
 def finish_in_kernel(d_normed_ref, d_middle_ref, x_ref, gain_ref, out_ref):
     rows = x_ref[...].astype(f32)
     back = norm_back(d_normed_ref[...].astype(f32), rows, norm_stats(rows), gain_ref[...])
@@ -212,28 +168,6 @@
         out_shape=shape_of((rows, cols), bf16),
         estimate=cost(20 * rows * cols, 12 * rows * cols, scale=1),
         name="finish_in",
-        after=after,
-    )
-
-
-def sum_blocks_kernel(in_ref, out_ref):
-    total = in_ref[0].astype(f32)
-    for index in range(1, in_ref.shape[0]):
-        total = total + in_ref[index].astype(f32)
-    out_ref[...] = total.astype(bf16)
-
-
-def sum_blocks(stacked, after=()):
-    count, rows, cols = stacked.shape
-    return call(
-        sum_blocks_kernel,
-        (stacked,),
-        grid=(4,),
-        in_specs=[pl.BlockSpec((count, rows // 4, cols), lambda i: (0, i, 0))],
-        out_specs=pl.BlockSpec((rows // 4, cols), lambda i: (i, 0)),
-        out_shape=shape_of((rows, cols), bf16),
-        estimate=cost(count * rows * cols, 2 * (count + 1) * rows * cols),
-        name="sum_blocks",
         after=after,
     )
 
@@ -335,6 +269,55 @@
         out_shape=out_shape,
         estimate=cost(0, rows * units * 12, scale=1),
         name="unpack_half",
+        after=after,
+    )
+
+
+def join_halves_kernel(core_ref, own_ref, got_ref, out_ref):
+    @pl.when(pl.program_id(0) == 0)
+    def first():
+        out_ref[...] = own_ref[...]
+
+    @pl.when(pl.program_id(0) == 1)
+    def second():
+        out_ref[...] = got_ref[...]
+
+
+def join_halves(core, sums, got, after=()):
+    rows, units = got.shape
+    return call(
+        join_halves_kernel,
+        (core, sums, got),
+        prefetch=1,
+        grid=(2,),
+        in_specs=[
+            pl.BlockSpec((rows, units), lambda i, c: (c[0], 0)),
+            pl.BlockSpec((rows, units), lambda i, c: (0, 0)),
+        ],
+        out_specs=pl.BlockSpec((rows, units), lambda i, c: (0, (c[0] + i) % 2)),
+        out_shape=shape_of((rows, 2 * units), bf16),
+        estimate=cost(0, rows * units * 8, scale=1),
+        name="join_halves",
+        after=after,
+    )
+
+
+def widened_kernel(in_ref, out_ref):
+    out_ref[...] = in_ref[...].astype(f32)
+
+
+def widened(value, after=()):
+    rows, cols = value.shape
+    spec = pl.BlockSpec((rows, cols // 2), lambda i: (0, i))
+    return call(
+        widened_kernel,
+        (value,),
+        grid=(2,),
+        in_specs=[spec],
+        out_specs=spec,
+        out_shape=shape_of((rows, cols), f32),
+        estimate=cost(0, rows * cols * 6, scale=1),
+        name="widened",
         after=after,
     )
 
@@ -1165,7 +1148,6 @@
     pack_cols = attn_cols + q_cols
     core_at = core.astype(jnp.int32).reshape(1)
     part_at = part.astype(jnp.int32).reshape(1)
-    chip_at = chip.astype(jnp.int32).reshape(1)
 
     def swapped(value):
         return lax.ppermute(value, "c", core_swap)
@@ -1175,12 +1157,6 @@
 
     def from_all(value):
         return [value] + [sent(value, shift) for shift in range(1, parts)]
-
-    def sent_chips(value, shift):
-        return lax.ppermute(value, "q", [(i, (i + shift) % chips) for i in range(chips)])
-
-    def line_step(value, step):
-        return lax.ppermute(value, "seq", [(step - 1, step), (parts - step, parts - step - 1)])
 
     hidden_blocks = from_all(hidden_in)
 
@@ -1299,21 +1275,18 @@
     d_in = lax.psum_scatter(d_in, "seq", scatter_dimension=0, tiled=True)
 
     attn_grad = lax.psum_scatter(attn_term, dp_axes, scatter_dimension=0, tiled=True)
-    got_up = [line_step(own_up, 1)]
+    give = lax.dynamic_slice_in_dim(own_up, (1 - core) * slice_rows, slice_rows, 0)
+    own_up = join_halves(core_at, own_up, swapped(give), after=(sum_pair,))
+    sum_up = lax.psum(own_up, "seq", axis_index_groups=[line[::-1]])
     grad_down = unpacked(sum_pair, 0, True)
     grad_gate = unpacked(sum_pair, 1, False, after=(grad_down,))
-    last = grad_gate
-    for step in range(2, parts):
-        last = add(own_up, got_up[-1], after=(last,))
-        got_up.append(line_step(last, step))
-    attn_grad = touch(attn_grad, after=(last,))
+    attn_grad = touch(attn_grad, after=(grad_gate, sum_up))
     attn_grads = lax.all_gather(attn_grad, "seq", axis=0)
     in_grad = finish_in(d_in, d_middle, hidden_in, ga)
-    sum_up = sum_all([own_up, *got_up], after=(attn_grad,))
-    grad_up = unpacked(sum_up, 0, False)
+    grad_up = widened(sum_up, after=(in_grad,))
     gain_sums = jnp.sum(attn_grads[:, :, pack_cols : pack_cols + 4].astype(f32), axis=0)
     grad_query, grad_key, grad_value, grad_output = unpack_attn(
-        attn_grads, q_cols, kv_cols, after=(grad_up, in_grad)
+        attn_grads, q_cols, kv_cols, after=(grad_up,)
     )
     return (
         output_act,

time: 484 us -> 461 us (0.952)
  starting transfers between devices: 52.9 us -> 37.5 us
  waiting for transfers between devices: 219 us -> 207 us
  local copies, waits for them, and re-layouts: 54.8 us -> 60.1 us
    ppermute x3 -> x0, waiting for transfers between devices: 72.4 us -> none  [line_step(): lax.ppermute(value, 'seq', [(step - 1, step), (parts - step, parts - step...]
    psum x0 -> x1, waiting for transfers between devices: none -> 21.3 us  [body(): sum_up = lax.psum(own_up, 'seq', axis_index_groups=[line[::-1]])]
    all_gather x1, waiting for transfers between devices: 0.01 us -> 18.1 us  [body(): attn_grads = lax.all_gather(attn_grad, 'seq', axis=0)]
    ppermute x6, starting transfers between devices: 25.1 us -> 14.8 us  [sent(): lax.ppermute(value, 'seq', [(i, (i + shift) % parts) for i in range(parts)])]
    ppermute x6, waiting for transfers between devices: 10.6 us -> 20.2 us  [sent(): lax.ppermute(value, 'seq', [(i, (i + shift) % parts) for i in range(parts)])]
    unnamed x144 -> x152, local copies, waits for them, and re-layouts: 47.2 us -> 53 us
    psum x1, waiting for transfers between devices: 19.2 us -> 13.7 us  [body(): sum_pair = lax.psum(own_pair, 'seq')]
    ppermute x3 -> x0, starting transfers between devices: 5.44 us -> none  [line_step(): lax.ppermute(value, 'seq', [(step - 1, step), (parts - step, parts - step...]
  transfers between devices with their start and end apart: 28 -> 26, of which waited for: 14 -> 16; matrix products, arithmetic and copies ran while one was open for 3% -> 3% of each run, Pallas kernels for 22% -> 23%
where the time goes in v4:
time: 461 us; the launch traced here: 452 us
  waiting for transfers between devices  207 us (45%)
  Pallas kernels  124 us (27%)
  local copies, waits for them, and re-layouts  60.1 us (13%)
  starting transfers between devices  37.5 us (8%)
  between operations  16.9 us (4%)
  other arithmetic  6.71 us (1%)
    pallas_call x26, Pallas kernels, call(): pl.pallas_call(body_of, grid_spec=pltpu.PrefetchScalarGridSpec(num_scalar...  124 us
    unnamed x152, local copies, waits for them, and re-layouts  53 us
    all_gather x1, waiting for transfers between devices, body(): d_proj_all = lax.all_gather(d_proj, 'seq', axis=0, tiled=True)  30.2 us
    reduce_scatter x2, waiting for transfers between devices, chip_sums(): return lax.psum_scatter(grad, 'q', scatter_dimension=0, tiled=True)  26.3 us
    reduce_scatter x1, waiting for transfers between devices, body(): lax.psum_scatter(attn_term, dp_axes, scatter_dimension=0, tiled=True)  23.6 us
    psum x1, waiting for transfers between devices, body(): sum_up = lax.psum(own_up, 'seq', axis_index_groups=[line[::-1]])  21.3 us
    ppermute x6, waiting for transfers between devices, sent(): lax.ppermute(value, 'seq', [(i, (i + shift) % parts) for i in range(parts)])  20.2 us
    ppermute x7, starting transfers between devices, swapped(): return lax.ppermute(value, 'c', core_swap)  19.1 us
  transfers between devices with their start and end apart: 26, of which 16 were waited for; matrix products, arithmetic and copies ran while one was open for 3% of the time, Pallas kernels for 23%

profile of v4, /device:TPU:0, one launch (start us, length us, event | category | flops | bytes accessed | tf_op | source)
XLA Modules:
  0.0 452.2 jit_solution(16571190939178474612)
XLA Ops:
  10.2 5.1 %collective-permute-start.2 = (bf16[256,1024]{1,0:T(8,128)(2,1)}, bf16[256,1024]{1,0:T(8,128)(2,1)}, u32[]{:S(2)}, u32[]{:S(2)}) collective-permute-start(bf16[256,1024]{1,0:T(8,128)(2,1)} %refs_2_.7), channel_id=1, source_target_pairs={{0,3},{1,0},{2,1},{3,2},{4,7},{5,4},{6,5},{7,6},{8,11},{9,8},{10,9... | collective-permute-start | bytes 1572872 | tf_op jit(solution)/shard_map/ppermute | solution.py:1156
  31.1 16.4 %all-gather.6.cloned.1.call-done.refs_0_.refs_5_.refs_7_.refs_9_ = bf16[1024,1664]{1,0:T(8,128)(2,1)} async-done(((bf16[128,1664]{1,0:T(8,128)(2,1)}), bf16[1024,1664]{1,0:T(8,128)(2,1)}) %all-gather.6.cloned.1.call-update) | async-done | bytes 3407888 | tf_op jit(solution)/shard_map/all_gather | solution.py:1167
  49.7 10.7 %collective-permute-done.1.refs_3_ = bf16[256,1024]{1,0:T(8,128)(2,1)} collective-permute-done((bf16[256,1024]{1,0:T(8,128)(2,1)}, bf16[256,1024]{1,0:T(8,128)(2,1)}, u32[]{:S(2)}, u32[]{:S(2)}) %collective-permute-start.1) | collective-permute-done | bytes 524320 | tf_op jit(solution)/shard_map/ppermute | solution.py:1156
  62.6 5.9 %project.1 = (bf16[1024,1024]{1,0:T(8,128)(2,1)S(1)}, bf16[1024,512]{1,0:T(8,128)(2,1)S(1)}, bf16[1024,512]{1,0:T(8,128)(2,1)S(1)}, f32[1024,768]{1,0:T(8,128)S(1)}) custom-call(s32[1]{0:T(128)} %bitcast.refs_0_, bf16[256,1024]{1,0:T(8,128)(2,1)} %refs_2_.7, bf16[256,1024]{1,0:T(8,128)(2,1)} %collective-permute-done.refs_2_.refs_4_, ...), custom_call_target="tpu_custom_call" | custom-call | flops 214748364800 | bytes 1258291200 | tf_op jit(solution)/shard_map/project/pallas_call | solution.py:54
  72.8 5.3 %attend_own.1 = (f32[512,1024]{1,0:T(8,128)S(1)}, f32[2,8,1024]{2,1,0:T(8,128)S(1)}) custom-call(bf16[1024,512]{1,0:T(8,128)(2,1)S(1)} %get-tuple-element.57.refs_0_.refs_1_, bf16[1024,512]{1,0:T(8,128)(2,1)S(1)} %get-tuple-element.58.refs_1_.refs_2_, bf16[1024,512]{1,0:T(8,128)(2,1)S(1)} %get-tuple-element.58.refs_1_.refs_2_, ...), custom_call_target="tpu_custom_call" | custom-call | flops 134217728000 | bytes 419430400 | tf_op jit(solution)/shard_map/attend_own/pallas_call | solution.py:54
  78.1 3.5 attend_tail.6
  82.5 4.0 attend_tail.5
  87.2 8.5 %collective-permute-start.5 = (bf16[256,1024]{1,0:T(8,128)(2,1)S(1)}, bf16[256,1024]{1,0:T(8,128)(2,1)S(1)}, u32[]{:S(2)}, u32[]{:S(2)}) collective-permute-start(bf16[256,1024]{1,0:T(8,128)(2,1)S(1)} %get-tuple-element.62), channel_id=1, source_target_pairs={{0,2},{1,3},{2,0},{3,1},{4,6},{5,7},{6,4},{7,5},{8,10},{9,11},{10,... | collective-permute-start | bytes 1572872 | tf_op jit(solution)/shard_map/ppermute | solution.py:1156
  95.7 5.1 %attend_tail.4 = (bf16[256,512]{1,0:T(8,128)(2,1)S(1)}, f32[2,8,256]{2,1,0:T(8,128)S(1)}, bf16[256,1024]{1,0:T(8,128)(2,1)S(1)}) custom-call(s32[1]{0:T(128)} %bitcast.refs_0_, bf16[1024,512]{1,0:T(8,128)(2,1)S(1)} %get-tuple-element.57.refs_0_.refs_1_, bf16[1024,512]{1,0:T(8,128)(2,1)S(1)} %collective-permute-done.3.refs_2_.refs_3_.refs_1_, ...), custom_call_target="tpu_custom_call" | custom-call | flops 53687091200 | bytes 419430400 | tf_op jit(solution)/shard_map/attend_tail/pallas_call | solution.py:54
  101.5 6.4 %attend_tail.7 = (bf16[256,512]{1,0:T(8,128)(2,1)S(1)}, f32[2,8,256]{2,1,0:T(8,128)S(1)}, bf16[256,1024]{1,0:T(8,128)(2,1)S(1)}) custom-call(s32[1]{0:T(128)} %bitcast.refs_0_, bf16[1024,512]{1,0:T(8,128)(2,1)S(1)} %get-tuple-element.57.refs_0_.refs_1_, bf16[1024,512]{1,0:T(8,128)(2,1)S(1)} %collective-permute-done.3.refs_2_.refs_3_.refs_1_, ...), custom_call_target="tpu_custom_call" | custom-call | flops 53687091200 | bytes 419430400 | tf_op jit(solution)/shard_map/attend_tail/pallas_call | solution.py:54
  107.9 2.8 collective-permute-done.5.refs_3_
  110.7 6.8 %collective-permute-done.4.refs_2_ = bf16[256,1024]{1,0:T(8,128)(2,1)S(1)} collective-permute-done((bf16[256,1024]{1,0:T(8,128)(2,1)S(1)}, bf16[256,1024]{1,0:T(8,128)(2,1)S(1)}, u32[]{:S(2)}, u32[]{:S(2)}) %collective-permute-start.4) | collective-permute-done | bytes 524320 | tf_op jit(solution)/shard_map/ppermute | solution.py:1156
  117.4 2.6 mid_norm.1
  120.0 18.4 %collective-permute-start.7 = (bf16[256,1024]{1,0:T(8,128)(2,1)S(1)}, bf16[256,1024]{1,0:T(8,128)(2,1)S(1)}, u32[]{:S(2)}, u32[]{:S(2)}) collective-permute-start(bf16[256,1024]{1,0:T(8,128)(2,1)S(1)} %get-tuple-element.66.refs_0_.refs_3_), channel_id=1, source_target_pairs={{0,4},{4,0},{1,5},{5,1},{2,6},{6,2},{3,7},{7,3},{8,12},{12,8},{9,1... | collective-permute-start | bytes 1572872 | tf_op jit(solution)/shard_map/ppermute | solution.py:1153
  140.8 14.4 %all-gather.8.cloned.1.call-done.refs_4_.refs_5_.refs_6_ = bf16[1024,4608]{1,0:T(8,128)(2,1)} async-done(((bf16[256,4608]{1,0:T(8,128)(2,1)}), bf16[1024,4608]{1,0:T(8,128)(2,1)}) %all-gather.8.cloned.1.call-update) | async-done | bytes 9437200 | tf_op jit(solution)/shard_map/all_gather | solution.py:1173
  156.3 14.8 %mlp.1 = (bf16[512,1536]{1,0:T(8,128)(2,1)}, bf16[512,1536]{1,0:T(8,128)(2,1)}, bf16[512,1536]{1,0:T(8,128)(2,1)}, f32[256,1024]{1,0:T(8,128)S(1)}, bf16[256,102...) custom-call(bf16[256,1024]{1,0:T(8,128)(2,1)S(1)} %get-tuple-element.66.refs_0_.refs_3_, ...), custom_call_target="tpu_custom_call" | custom-call | flops 966367641600 | bytes 1677721600 | tf_op jit(solution)/shard_map/mlp/pallas_call | solution.py:54
  180.0 6.9 %mlp_grad_pair.1 = bf16[1024,3072]{1,0:T(8,128)(2,1)} custom-call(bf16[256,1024]{1,0:T(8,128)(2,1)S(1)} %copy-done.29, bf16[256,1024]{1,0:T(8,128)(2,1)S(1)} %bitcast.23, bf16[512,1536]{1,0:T(8,128)(2,1)S(1)} %copy-done.71, bf16[256,1024]{1,0:T(8,128)(2,1)S(1)} %get-tuple-element.66.refs_0_.refs_3_, ...), custom_call_target="tpu_custom_call" | custom-call | flops 322122547200 | bytes 1677721600 | tf_op jit(solution)/shard_map/mlp_grad_pair/pallas_call | solution.py:54
  188.3 2.8 mlp_grad.1.refs_8_
  192.9 30.2 %all-gather.10.cloned.1.call-done.refs_6_.refs_0_ = bf16[1024,1024]{1,0:T(8,128)(2,1)} async-done(((bf16[256,1024]{1,0:T(8,128)(2,1)}), bf16[1024,1024]{1,0:T(8,128)(2,1)}) %all-gather.10.cloned.1.call-update) | async-done | bytes 2097168 | tf_op jit(solution)/shard_map/all_gather | solution.py:1242
  227.9 14.4 %attend_back_tail.1 = (bf16[1024,512]{1,0:T(8,128)(2,1)S(1)}, f32[512,1024]{1,0:T(8,128)S(1)}, f32[2,8,1024]{2,1,0:T(8,128)S(1)}, bf16[2,1024,256]{2,1,0:T(8,128)(2,1)S(1)}) custom-call(bf16[1024,512]{1,0:T(8,128)(2,1)S(1)} %copy-done.68, bf16[1024,512]{1,0:T(8,128)(2,1)S(1)} %copy-done.59, bf16[1024,512]{1,0:T(8,128)(2,1)S(1)} %copy-done.59, ...), custom_call_target="tpu_custom_call" | custom-call | flops 442918502400 | bytes 838860800 | tf_op jit(solution)/shard_map/attend_back_tail/pallas_call | solution.py:54
  244.7 13.1 %reduce-scatter.12.cloned.1.call-done.refs_0_ = bf16[256,3072]{1,0:T(8,128)(2,1)} async-done(((bf16[1024,3072]{1,0:T(8,128)(2,1)}), bf16[256,3072]{1,0:T(8,128)(2,1)}) %reduce-scatter.12.cloned.1.call-update) | async-done | bytes 1572880 | tf_op jit(solution)/shard_map/reduce_scatter | solution.py:1246
  265.3 12.7 %attend_back_own.1 = (bf16[1024,512]{1,0:T(8,128)(2,1)S(1)}, f32[2,1024,256]{2,1,0:T(8,128)S(1)}) custom-call(bf16[1024,512]{1,0:T(8,128)(2,1)S(1)} %copy-done.69, bf16[1024,512]{1,0:T(8,128)(2,1)S(1)} %copy-done.57, bf16[1024,512]{1,0:T(8,128)(2,1)S(1)} %copy-done.57, s32[4,8,256]{2,1,0:T(8,128)S(1)} %pad.4.refs_3_.refs_4_, ...), custom_call_target="tpu_custom_call" | custom-call | flops 3355443200 | bytes 8388608 | tf_op jit(solution)/shard_map/attend_back_own/pallas_call | solution.py:54
  278.1 2.2 out_grad.1.refs_14_
  281.3 18.7 %project_back.1 = (bf16[1024,1024]{1,0:T(8,128)(2,1)}, bf16[1024,1664]{1,0:T(8,128)(2,1)}) custom-call(s32[1]{0:T(128)} %bitcast.refs_0_, bf16[256,1024]{1,0:T(8,128)(2,1)} %refs_2_.7, bf16[256,1024]{1,0:T(8,128)(2,1)} %collective-permute-done.2.refs_4_.refs_2_, bf16[256,1024]{1,0:T(8,128)(2,1)} %collective-permute-done.1.refs_3_, ...), custom_call_target="tpu_custom_call" | custom-call | flops 4294967296 | bytes 16777216 | tf_op jit(solution)/shard_map/project_back/pallas_call | solution.py:54
  300.1 13.2 %reduce-scatter.14.cloned.1.call-done.refs_1_ = bf16[256,1536]{1,0:T(8,128)(2,1)} async-done(((bf16[1024,1536]{1,0:T(8,128)(2,1)}), bf16[256,1536]{1,0:T(8,128)(2,1)}) %reduce-scatter.14.cloned.1.call-update) | async-done | bytes 786448 | tf_op jit(solution)/shard_map/reduce_scatter | solution.py:1246
  316.1 13.7 %all-reduce.4.cloned.1.call-done.refs_1_.refs_3_ = bf16[256,3072]{1,0:T(8,128)(2,1)} async-done(((bf16[256,3072]{1,0:T(8,128)(2,1)}), bf16[256,3072]{1,0:T(8,128)(2,1)}) %all-reduce.4.cloned.1.call-update) | async-done | bytes 1572880 | tf_op jit(solution)/shard_map/psum | solution.py:1268
  340.9 23.6 %reduce-scatter.10.cloned.1.call-done.refs_0_ = bf16[128,1664]{1,0:T(8,128)(2,1)} async-done(((bf16[1024,1664]{1,0:T(8,128)(2,1)}), bf16[128,1664]{1,0:T(8,128)(2,1)}) %reduce-scatter.10.cloned.1.call-update) | async-done | bytes 426000 | tf_op jit(solution)/shard_map/reduce_scatter | solution.py:1277
  364.5 21.3 %all-reduce.6.cloned.1.call-done.refs_2_.refs_0_ = bf16[128,3072]{1,0:T(8,128)(2,1)} async-done(((bf16[128,3072]{1,0:T(8,128)(2,1)}), bf16[128,3072]{1,0:T(8,128)(2,1)}) %all-reduce.6.cloned.1.call-update) | async-done | bytes 786448 | tf_op jit(solution)/shard_map/psum | solution.py:1280
  393.7 16.9 %reduce-scatter.8.cloned.1.call-done.refs_0_ = bf16[256,1024]{1,0:T(8,128)(2,1)} async-done(((bf16[1024,1024]{1,0:T(8,128)(2,1)}), bf16[256,1024]{1,0:T(8,128)(2,1)}) %reduce-scatter.8.cloned.1.call-update) | async-done | bytes 524304 | tf_op jit(solution)/shard_map/reduce_scatter | solution.py:1275
  412.9 3.6 finish_in.1.refs_1_
  418.8 18.1 %all-gather.12.cloned.1.call-done = bf16[512,1664]{1,0:T(8,128)(2,1)} async-done(((bf16[128,1664]{1,0:T(8,128)(2,1)}), bf16[512,1664]{1,0:T(8,128)(2,1)}) %all-gather.12.cloned.1.call-update) | async-done | bytes 1703952 | tf_op jit(solution)/shard_map/all_gather | solution.py:1284
  442.1 2.1 unpack_attn.1
  (242 shorter events, 91.5 us)
Async XLA Ops:
  8.0 39.4 %all-gather.6.cloned.1.call-start = ((), (), s32[]{:S(2)}) async-start(), calls=%async_computation.5 | async-start | bytes 3833856 | tf_op jit(solution)/shard_map/all_gather | solution.py:1167
  10.1 130.7 %reduce-scatter.6.cloned.1.call-start = ((), (), s32[]{:S(2)}) async-start(), calls=%async_computation.6 | async-start | bytes 1572864 | tf_op jit(solution)/shard_map/reduce_scatter | solution.py:1177
  10.2 39.5 %collective-permute-start.2 = (bf16[256,1024]{1,0:T(8,128)(2,1)}, bf16[256,1024]{1,0:T(8,128)(2,1)}, u32[]{:S(2)}, u32[]{:S(2)}) collective-permute-start(bf16[256,1024]{1,0:T(8,128)(2,1)} %refs_2_.7), channel_id=1, source_target_pairs={{0,3},{1,0},{2,1},{3,2},{4,7},{5,4},{6,5},{7,6},{8,11},{9,8},{10,9... | collective-permute-start | bytes 1572872 | tf_op jit(solution)/shard_map/ppermute | solution.py:1156
  15.3 45.1 %collective-permute-start.1 = (bf16[256,1024]{1,0:T(8,128)(2,1)}, bf16[256,1024]{1,0:T(8,128)(2,1)}, u32[]{:S(2)}, u32[]{:S(2)}) collective-permute-start(bf16[256,1024]{1,0:T(8,128)(2,1)} %refs_2_.7), channel_id=1, source_target_pairs={{0,2},{1,3},{2,0},{3,1},{4,6},{5,7},{6,4},{7,5},{8,10},{9,11},{10,... | collective-permute-start | bytes 1572872 | tf_op jit(solution)/shard_map/ppermute | solution.py:1156
  15.3 45.1 %collective-permute-start = (bf16[256,1024]{1,0:T(8,128)(2,1)}, bf16[256,1024]{1,0:T(8,128)(2,1)}, u32[]{:S(2)}, u32[]{:S(2)}) collective-permute-start(bf16[256,1024]{1,0:T(8,128)(2,1)} %refs_2_.7), channel_id=1, source_target_pairs={{0,1},{1,2},{2,3},{3,0},{4,5},{5,6},{6,7},{7,4},{8,9},{9,10},{10,1... | collective-permute-start | bytes 1572872 | tf_op jit(solution)/shard_map/ppermute | solution.py:1156
  23.3 4.9 %collective-permute-start.8 = (bf16[128,4608]{1,0:T(8,128)(2,1)}, bf16[128,4608]{1,0:T(8,128)(2,1)}, u32[]{:S(2)}, u32[]{:S(2)}) collective-permute-start(bf16[128,4608]{1,0:T(8,128)(2,1)} %get-tuple-element.68), channel_id=1, source_target_pairs={{0,4},{4,0},{1,5},{5,1},{2,6},{6,2},{3,7},{7,3},{8,12},{12,8},{9,1... | collective-permute-start | bytes 3538952 | tf_op jit(solution)/shard_map/ppermute | solution.py:1153
  24.5 130.8 %all-gather.8.cloned.1.call-start = ((), (), s32[]{:S(2)}) async-start(), calls=%async_computation.7 | async-start | bytes 11796480 | tf_op jit(solution)/shard_map/all_gather | solution.py:1173
  31.0 192.1 %all-gather.10.cloned.1.call-start = ((), (), s32[]{:S(2)}) async-start(), calls=%async_computation.8 | async-start | bytes 2621440 | tf_op jit(solution)/shard_map/all_gather | solution.py:1242
  49.7 67.8 %copy-start.50 = (f32[1,1024]{1,0:T(1,128)}, f32[1,1024]{1,0:T(1,128)S(1)}, u32[]{:S(2)}) copy-start(f32[1,1024]{1,0:T(1,128)S(1)} %get-tuple-element.110.refs_1_.refs_4_) | copy-start | bytes 12292
  71.5 6.6 %collective-permute-start.3 = (bf16[1024,512]{1,0:T(8,128)(2,1)S(1)}, bf16[1024,512]{1,0:T(8,128)(2,1)S(1)}, u32[]{:S(2)}, u32[]{:S(2)}) collective-permute-start(bf16[1024,512]{1,0:T(8,128)(2,1)S(1)} %get-tuple-element.58.refs_1_.refs_2_), channel_id=1, source_target_pairs={{0,4},{4,8},{8,12},{12,16},{16,20},{20,24},{24,28},{1,5},{5,9},{9,... | collective-permute-start | bytes 3145736 | tf_op jit(solution)/shard_map/ppermute | solution.py:1211
  82.3 25.6 %collective-permute-start.6 = (bf16[256,1024]{1,0:T(8,128)(2,1)}, bf16[256,1024]{1,0:T(8,128)(2,1)}, u32[]{:S(2)}, u32[]{:S(2)}) collective-permute-start(bf16[256,1024]{1,0:T(8,128)(2,1)} %get-tuple-element.63), channel_id=1, source_target_pairs={{0,3},{1,0},{2,1},{3,2},{4,7},{5,4},{6,5},{7,6},{8,11},{9,8},{10,9... | collective-permute-start | bytes 1572872 | tf_op jit(solution)/shard_map/ppermute | solution.py:1156
  87.2 23.5 %collective-permute-start.5 = (bf16[256,1024]{1,0:T(8,128)(2,1)S(1)}, bf16[256,1024]{1,0:T(8,128)(2,1)S(1)}, u32[]{:S(2)}, u32[]{:S(2)}) collective-permute-start(bf16[256,1024]{1,0:T(8,128)(2,1)S(1)} %get-tuple-element.62), channel_id=1, source_target_pairs={{0,2},{1,3},{2,0},{3,1},{4,6},{5,7},{6,4},{7,5},{8,10},{9,11},{10,... | collective-permute-start | bytes 1572872 | tf_op jit(solution)/shard_map/ppermute | solution.py:1156
  101.5 15.9 %collective-permute-start.4 = (bf16[256,1024]{1,0:T(8,128)(2,1)S(1)}, bf16[256,1024]{1,0:T(8,128)(2,1)S(1)}, u32[]{:S(2)}, u32[]{:S(2)}) collective-permute-start(bf16[256,1024]{1,0:T(8,128)(2,1)S(1)} %get-tuple-element.61), channel_id=1, source_target_pairs={{0,1},{1,2},{2,3},{3,0},{4,5},{5,6},{6,7},{7,4},{8,9},{9,10},{10,1... | collective-permute-start | bytes 1572872 | tf_op jit(solution)/shard_map/ppermute | solution.py:1156
  107.9 47.4 %copy-start.29 = (bf16[256,1024]{1,0:T(8,128)(2,1)S(1)}, bf16[256,1024]{1,0:T(8,128)(2,1)}, u32[]{:S(2)}) copy-start(bf16[256,1024]{1,0:T(8,128)(2,1)} %refs_0_.3) | copy-start | bytes 1572868
  120.0 53.8 %copy-start.8 = (f32[256,1024]{1,0:T(8,128)}, f32[256,1024]{1,0:T(8,128)S(1)}, u32[]{:S(2)}) copy-start(f32[256,1024]{1,0:T(8,128)S(1)} %get-tuple-element.65.refs_2_) | copy-start | bytes 3145732
  120.0 20.8 %collective-permute-start.7 = (bf16[256,1024]{1,0:T(8,128)(2,1)S(1)}, bf16[256,1024]{1,0:T(8,128)(2,1)S(1)}, u32[]{:S(2)}, u32[]{:S(2)}) collective-permute-start(bf16[256,1024]{1,0:T(8,128)(2,1)S(1)} %get-tuple-element.66.refs_0_.refs_3_), channel_id=1, source_target_pairs={{0,4},{4,0},{1,5},{5,1},{2,6},{6,2},{3,7},{7,3},{8,12},{12,8},{9,1... | collective-permute-start | bytes 1572872 | tf_op jit(solution)/shard_map/ppermute | solution.py:1153
  171.1 2.6 collective-permute-start.10
  176.9 80.9 %reduce-scatter.12.cloned.1.call-start = ((), (), s32[]{:S(2)}) async-start(), calls=%async_computation.11 | async-start | bytes 7864320 | tf_op jit(solution)/shard_map/reduce_scatter | solution.py:1246
  186.9 126.4 %reduce-scatter.14.cloned.1.call-start = ((), (), s32[]{:S(2)}) async-start(), calls=%async_computation.13 | async-start | bytes 3932160 | tf_op jit(solution)/shard_map/reduce_scatter | solution.py:1246
  192.8 30.3 %copy-start.59 = (bf16[1024,512]{1,0:T(8,128)(2,1)S(1)}, bf16[1024,512]{1,0:T(8,128)(2,1)}, u32[]{:S(2)}) copy-start(bf16[1024,512]{1,0:T(8,128)(2,1)} %copy-done.58) | copy-start | bytes 3145732
  192.8 136.9 %all-reduce.4.cloned.1.call-start = ((), (), s32[]{:S(2)}) async-start(), calls=%async_computation.12 | async-start | bytes 3145728 | tf_op jit(solution)/shard_map/psum | solution.py:1268
  260.9 103.6 %reduce-scatter.10.cloned.1.call-start = ((), (), s32[]{:S(2)}) async-start(), calls=%async_computation.10 | async-start | bytes 3833856 | tf_op jit(solution)/shard_map/reduce_scatter | solution.py:1277
  260.9 20.4 %collective-permute-start.11 = (bf16[2,1024,256]{2,1,0:T(8,128)(2,1)}, bf16[2,1024,256]{2,1,0:T(8,128)(2,1)S(1)}, u32[]{:S(2)}, u32[]{:S(2)}) collective-permute-start(bf16[2,1024,256]{2,1,0:T(8,128)(2,1)} %copy-done.60), channel_id=1, source_target_pairs={{4,0},{8,4},{12,8},{16,12},{20,16},{24,20},{28,24},{5,1},{9,5},{13... | collective-permute-start | bytes 3145736 | tf_op jit(solution)/shard_map/ppermute | solution.py:1263
  300.1 85.7 %all-reduce.6.cloned.1.call-start = ((), (), s32[]{:S(2)}) async-start(), calls=%async_computation.14 | async-start | bytes 1572864 | tf_op jit(solution)/shard_map/psum | solution.py:1280
  314.3 1.8 collective-permute-start.14
  333.3 77.3 %reduce-scatter.8.cloned.1.call-start = ((), (), s32[]{:S(2)}) async-start(), calls=%async_computation.9 | async-start | bytes 2621440 | tf_op jit(solution)/shard_map/reduce_scatter | solution.py:1275
  333.9 103.0 %all-gather.12.cloned.1.call-start = ((), (), s32[]{:S(2)}) async-start(), calls=%async_computation.15 | async-start | bytes 2129920 | tf_op jit(solution)/shard_map/all_gather | solution.py:1284
  334.7 1.8 collective-permute-start.13
  334.8 3.1 collective-permute-start.12
  339.7 51.0 %copy-start.64 = (bf16[256,1024]{1,0:T(8,128)(2,1)S(1)}, bf16[256,1024]{1,0:T(8,128)(2,1)}, u32[]{:S(2)}) copy-start(bf16[256,1024]{1,0:T(8,128)(2,1)} %copy-done.63) | copy-start | bytes 1572868
  339.7 53.0 %copy-start.9 = (f32[256,1024]{1,0:T(8,128)S(1)}, f32[256,1024]{1,0:T(8,128)}, u32[]{:S(2)}) copy-start(f32[256,1024]{1,0:T(8,128)} %copy-done.8) | copy-start | bytes 3145732
  390.7 2.0 collective-permute-start.9
  (69 other events, 317.8 us)
Sparse Core Ops, SparseCore 0:
  11.3 36.1 all-gather.5
  49.4 105.7 all-gather.7
  187.0 70.7 reduce-scatter.11
  260.9 52.3 reduce-scatter.13
  317.0 47.4 reduce-scatter.9
  366.6 43.9 reduce-scatter.7
Sparse Core Ops, SparseCore 1:
  24.6 9.0 reduce-scatter.5
  177.0 46.1 all-gather.9
  261.0 68.8 all-reduce.3
  333.4 52.3 all-reduce.5
  390.8 46.1 all-gather.11

commit v5 on v4

--- a/solution.py
+++ b/solution.py
@@ -1264,7 +1264,6 @@
     d_queries, d_kv = attend_back_own(
         queries, kv_own, bounds, totals_all, d_attn, turned, deltas
     )
-    own_pair = touch(own_pair, after=(d_attn,))
     sum_pair = lax.psum(own_pair, "seq")
     w_out_grad = out_grad_sums([d_proj_all], [attn_all], after=(d_queries,))
     d_in, attn_term = project_back(

time: 461 us -> 458 us (level)
  local copies, waits for them, and re-layouts: 60.1 us -> 43.7 us
  waiting for transfers between devices: 207 us -> 215 us
  starting transfers between devices: 37.5 us -> 44.1 us
    reduce_scatter x2, waiting for transfers between devices: 26.3 us -> 63.9 us  [chip_sums(): return lax.psum_scatter(grad, 'q', scatter_dimension=0, tiled=True)]
    all_gather x1, waiting for transfers between devices: 30.2 us -> 0.03 us  [body(): d_proj_all = lax.all_gather(d_proj, 'seq', axis=0, tiled=True)]
    reduce_scatter x1, waiting for transfers between devices: 16.9 us -> 44.5 us  [body(): d_in = lax.psum_scatter(d_in, 'seq', scatter_dimension=0, tiled=True)]
    all_gather x1, waiting for transfers between devices: 18.1 us -> 1.31 us  [body(): attn_grads = lax.all_gather(attn_grad, 'seq', axis=0)]
    unnamed x152 -> x136, local copies, waits for them, and re-layouts: 53 us -> 39.6 us
    psum x1, waiting for transfers between devices: 21.3 us -> 9.68 us  [body(): sum_up = lax.psum(own_up, 'seq', axis_index_groups=[line[::-1]])]
    ppermute x7, starting transfers between devices: 19.1 us -> 25.8 us  [swapped(): return lax.ppermute(value, 'c', core_swap)]
    psum x1, waiting for transfers between devices: 13.7 us -> 7.98 us  [body(): sum_pair = lax.psum(own_pair, 'seq')]
  transfers between devices with their start and end apart: 26 -> 26, of which waited for: 16 -> 16; matrix products, arithmetic and copies ran while one was open for 3% -> 2% of each run, Pallas kernels for 23% -> 21%
where the time goes in v5:
time: 458 us; the launch traced here: 450 us
  waiting for transfers between devices  215 us (47%)
  Pallas kernels  123 us (27%)
  starting transfers between devices  44.1 us (10%)
  local copies, waits for them, and re-layouts  43.7 us (10%)
  between operations  17 us (4%)
  other arithmetic  6.71 us (1%)
    pallas_call x25, Pallas kernels, call(): pl.pallas_call(body_of, grid_spec=pltpu.PrefetchScalarGridSpec(num_scalar...  123 us
    reduce_scatter x2, waiting for transfers between devices, chip_sums(): return lax.psum_scatter(grad, 'q', scatter_dimension=0, tiled=True)  63.9 us
    reduce_scatter x1, waiting for transfers between devices, body(): d_in = lax.psum_scatter(d_in, 'seq', scatter_dimension=0, tiled=True)  44.5 us
    unnamed x136, local copies, waits for them, and re-layouts  39.6 us
    reduce_scatter x1, waiting for transfers between devices, body(): lax.psum_scatter(attn_term, dp_axes, scatter_dimension=0, tiled=True)  25.9 us
    ppermute x7, starting transfers between devices, swapped(): return lax.ppermute(value, 'c', core_swap)  25.8 us
    ppermute x6, waiting for transfers between devices, sent(): lax.ppermute(value, 'seq', [(i, (i + shift) % parts) for i in range(parts)])  18.9 us
    all_gather x1, waiting for transfers between devices, body(): mlp_w = lax.all_gather(mlp_pack, 'q', axis=0, tiled=True)  17.3 us
  transfers between devices with their start and end apart: 26, of which 16 were waited for; matrix products, arithmetic and copies ran while one was open for 2% of the time, Pallas kernels for 21%

profile of v5, /device:TPU:0, one launch (start us, length us, event | category | flops | bytes accessed | tf_op | source)
XLA Modules:
  0.0 449.5 jit_solution(12518000887825382356)
XLA Ops:
  8.1 2.1 pack_attn.1.refs_4_
  10.2 5.1 %collective-permute-start.2 = (bf16[256,1024]{1,0:T(8,128)(2,1)}, bf16[256,1024]{1,0:T(8,128)(2,1)}, u32[]{:S(2)}, u32[]{:S(2)}) collective-permute-start(bf16[256,1024]{1,0:T(8,128)(2,1)} %refs_2_.7), channel_id=1, source_target_pairs={{0,3},{1,0},{2,1},{3,2},{4,7},{5,4},{6,5},{7,6},{8,11},{9,8},{10,9... | collective-permute-start | bytes 1572872 | tf_op jit(solution)/shard_map/ppermute | solution.py:1156
  31.1 16.3 %all-gather.6.cloned.1.call-done.refs_0_.refs_5_.refs_7_.refs_9_ = bf16[1024,1664]{1,0:T(8,128)(2,1)} async-done(((bf16[128,1664]{1,0:T(8,128)(2,1)}), bf16[1024,1664]{1,0:T(8,128)(2,1)}) %all-gather.6.cloned.1.call-update) | async-done | bytes 3407888 | tf_op jit(solution)/shard_map/all_gather | solution.py:1167
  49.7 10.7 %collective-permute-done.1.refs_3_ = bf16[256,1024]{1,0:T(8,128)(2,1)} collective-permute-done((bf16[256,1024]{1,0:T(8,128)(2,1)}, bf16[256,1024]{1,0:T(8,128)(2,1)}, u32[]{:S(2)}, u32[]{:S(2)}) %collective-permute-start.1) | collective-permute-done | bytes 524320 | tf_op jit(solution)/shard_map/ppermute | solution.py:1156
  62.6 5.9 %project.1 = (bf16[1024,1024]{1,0:T(8,128)(2,1)S(1)}, bf16[1024,512]{1,0:T(8,128)(2,1)S(1)}, bf16[1024,512]{1,0:T(8,128)(2,1)S(1)}, f32[1024,768]{1,0:T(8,128)S(1)}) custom-call(s32[1]{0:T(128)} %bitcast.refs_0_, bf16[256,1024]{1,0:T(8,128)(2,1)} %refs_2_.7, bf16[256,1024]{1,0:T(8,128)(2,1)} %collective-permute-done.refs_2_.refs_4_, ...), custom_call_target="tpu_custom_call" | custom-call | flops 214748364800 | bytes 1258291200 | tf_op jit(solution)/shard_map/project/pallas_call | solution.py:54
  71.5 5.3 %attend_own.1 = (f32[512,1024]{1,0:T(8,128)S(1)}, f32[2,8,1024]{2,1,0:T(8,128)S(1)}) custom-call(bf16[1024,512]{1,0:T(8,128)(2,1)S(1)} %get-tuple-element.57.refs_0_.refs_1_, bf16[1024,512]{1,0:T(8,128)(2,1)S(1)} %get-tuple-element.58.refs_1_.refs_2_, bf16[1024,512]{1,0:T(8,128)(2,1)S(1)} %get-tuple-element.58.refs_1_.refs_2_, ...), custom_call_target="tpu_custom_call" | custom-call | flops 134217728000 | bytes 419430400 | tf_op jit(solution)/shard_map/attend_own/pallas_call | solution.py:54
  76.8 3.5 attend_tail.6
  81.2 4.0 attend_tail.5
  85.9 8.5 %collective-permute-start.5 = (bf16[256,1024]{1,0:T(8,128)(2,1)S(1)}, bf16[256,1024]{1,0:T(8,128)(2,1)S(1)}, u32[]{:S(2)}, u32[]{:S(2)}) collective-permute-start(bf16[256,1024]{1,0:T(8,128)(2,1)S(1)} %get-tuple-element.62), channel_id=1, source_target_pairs={{0,2},{1,3},{2,0},{3,1},{4,6},{5,7},{6,4},{7,5},{8,10},{9,11},{10,... | collective-permute-start | bytes 1572872 | tf_op jit(solution)/shard_map/ppermute | solution.py:1156
  94.3 5.1 %attend_tail.4 = (bf16[256,512]{1,0:T(8,128)(2,1)S(1)}, f32[2,8,256]{2,1,0:T(8,128)S(1)}, bf16[256,1024]{1,0:T(8,128)(2,1)S(1)}) custom-call(s32[1]{0:T(128)} %bitcast.refs_0_, bf16[1024,512]{1,0:T(8,128)(2,1)S(1)} %get-tuple-element.57.refs_0_.refs_1_, bf16[1024,512]{1,0:T(8,128)(2,1)S(1)} %collective-permute-done.3.refs_2_.refs_3_.refs_1_, ...), custom_call_target="tpu_custom_call" | custom-call | flops 53687091200 | bytes 419430400 | tf_op jit(solution)/shard_map/attend_tail/pallas_call | solution.py:54
  100.2 6.4 %attend_tail.7 = (bf16[256,512]{1,0:T(8,128)(2,1)S(1)}, f32[2,8,256]{2,1,0:T(8,128)S(1)}, bf16[256,1024]{1,0:T(8,128)(2,1)S(1)}) custom-call(s32[1]{0:T(128)} %bitcast.refs_0_, bf16[1024,512]{1,0:T(8,128)(2,1)S(1)} %get-tuple-element.57.refs_0_.refs_1_, bf16[1024,512]{1,0:T(8,128)(2,1)S(1)} %collective-permute-done.3.refs_2_.refs_3_.refs_1_, ...), custom_call_target="tpu_custom_call" | custom-call | flops 53687091200 | bytes 419430400 | tf_op jit(solution)/shard_map/attend_tail/pallas_call | solution.py:54
  106.6 4.1 collective-permute-done.5.refs_3_
  110.7 4.0 collective-permute-done.4.refs_2_
  114.8 2.6 mid_norm.1
  117.3 19.7 %collective-permute-start.7 = (bf16[256,1024]{1,0:T(8,128)(2,1)S(1)}, bf16[256,1024]{1,0:T(8,128)(2,1)S(1)}, u32[]{:S(2)}, u32[]{:S(2)}) collective-permute-start(bf16[256,1024]{1,0:T(8,128)(2,1)S(1)} %get-tuple-element.66.refs_0_.refs_3_), channel_id=1, source_target_pairs={{0,4},{4,0},{1,5},{5,1},{2,6},{6,2},{3,7},{7,3},{8,12},{12,8},{9,1... | collective-permute-start | bytes 1572872 | tf_op jit(solution)/shard_map/ppermute | solution.py:1153
  138.6 17.3 %all-gather.8.cloned.1.call-done.refs_4_.refs_5_.refs_6_ = bf16[1024,4608]{1,0:T(8,128)(2,1)} async-done(((bf16[256,4608]{1,0:T(8,128)(2,1)}), bf16[1024,4608]{1,0:T(8,128)(2,1)}) %all-gather.8.cloned.1.call-update) | async-done | bytes 9437200 | tf_op jit(solution)/shard_map/all_gather | solution.py:1173
  157.0 14.8 %mlp.1 = (bf16[512,1536]{1,0:T(8,128)(2,1)}, bf16[512,1536]{1,0:T(8,128)(2,1)}, bf16[512,1536]{1,0:T(8,128)(2,1)}, f32[256,1024]{1,0:T(8,128)S(1)}, bf16[256,102...) custom-call(bf16[256,1024]{1,0:T(8,128)(2,1)S(1)} %get-tuple-element.66.refs_0_.refs_3_, ...), custom_call_target="tpu_custom_call" | custom-call | flops 966367641600 | bytes 1677721600 | tf_op jit(solution)/shard_map/mlp/pallas_call | solution.py:54
  173.7 2.0 mid_back.1
  179.7 6.8 %mlp_grad_pair.1 = bf16[1024,3072]{1,0:T(8,128)(2,1)} custom-call(bf16[256,1024]{1,0:T(8,128)(2,1)S(1)} %copy-done.25, bf16[256,1024]{1,0:T(8,128)(2,1)S(1)} %bitcast.23, bf16[512,1536]{1,0:T(8,128)(2,1)S(1)} %copy-done.63, bf16[256,1024]{1,0:T(8,128)(2,1)S(1)} %get-tuple-element.66.refs_0_.refs_3_, ...), custom_call_target="tpu_custom_call" | custom-call | flops 322122547200 | bytes 1677721600 | tf_op jit(solution)/shard_map/mlp_grad_pair/pallas_call | solution.py:54
  187.9 3.9 mlp_grad.1.refs_8_
  193.1 63.9 %reduce-scatter.12.cloned.1.call-done = bf16[256,3072]{1,0:T(8,128)(2,1)} async-done(((bf16[1024,3072]{1,0:T(8,128)(2,1)}), bf16[256,3072]{1,0:T(8,128)(2,1)}) %reduce-scatter.12.cloned.1.call-update) | async-done | bytes 1572880 | tf_op jit(solution)/shard_map/reduce_scatter | solution.py:1246
  260.1 14.5 %attend_back_tail.1 = (bf16[1024,512]{1,0:T(8,128)(2,1)S(1)}, f32[512,1024]{1,0:T(8,128)S(1)}, f32[2,8,1024]{2,1,0:T(8,128)S(1)}, bf16[2,1024,256]{2,1,0:T(8,128)(2,1)S(1)}) custom-call(bf16[1024,512]{1,0:T(8,128)(2,1)S(1)} %copy-done.60, bf16[1024,512]{1,0:T(8,128)(2,1)S(1)} %copy-done.54, bf16[1024,512]{1,0:T(8,128)(2,1)S(1)} %copy-done.54, ...), custom_call_target="tpu_custom_call" | custom-call | flops 442918502400 | bytes 838860800 | tf_op jit(solution)/shard_map/attend_back_tail/pallas_call | solution.py:54
  276.2 12.1 %attend_back_own.1 = (bf16[1024,512]{1,0:T(8,128)(2,1)S(1)}, f32[2,1024,256]{2,1,0:T(8,128)S(1)}) custom-call(bf16[1024,512]{1,0:T(8,128)(2,1)S(1)} %copy-done.61, bf16[1024,512]{1,0:T(8,128)(2,1)S(1)} %copy-done.52, bf16[1024,512]{1,0:T(8,128)(2,1)S(1)} %copy-done.52, s32[4,8,256]{2,1,0:T(8,128)S(1)} %pad.4.refs_3_.refs_4_, ...), custom_call_target="tpu_custom_call" | custom-call | flops 3355443200 | bytes 8388608 | tf_op jit(solution)/shard_map/attend_back_own/pallas_call | solution.py:54
  288.3 2.2 out_grad.1.refs_14_
  291.5 18.5 %project_back.1 = (bf16[1024,1024]{1,0:T(8,128)(2,1)}, bf16[1024,1664]{1,0:T(8,128)(2,1)}) custom-call(s32[1]{0:T(128)} %bitcast.refs_0_, bf16[256,1024]{1,0:T(8,128)(2,1)} %refs_2_.7, bf16[256,1024]{1,0:T(8,128)(2,1)} %collective-permute-done.2.refs_4_.refs_2_, bf16[256,1024]{1,0:T(8,128)(2,1)} %collective-permute-done.1.refs_3_, ...), custom_call_target="tpu_custom_call" | custom-call | flops 4294967296 | bytes 16777216 | tf_op jit(solution)/shard_map/project_back/pallas_call | solution.py:54
  311.2 5.3 %collective-permute-start.14 = (bf16[128,1536]{1,0:T(8,128)(2,1)S(1)}, bf16[128,1536]{1,0:T(8,128)(2,1)S(1)}, u32[]{:S(2)}, u32[]{:S(2)}) collective-permute-start(bf16[128,1536]{1,0:T(8,128)(2,1)S(1)} %constant_dynamic-slice_fusion), channel_id=1, source_target_pairs={{0,4},{4,0},{1,5},{5,1},{2,6},{6,2},{3,7},{7,3},{8,12},{12,8},{9,1... | collective-permute-start | bytes 1179656 | tf_op jit(solution)/shard_map/ppermute | solution.py:1153
  317.9 8.0 %all-reduce.4.cloned.1.call-done.refs_1_.refs_3_ = bf16[256,3072]{1,0:T(8,128)(2,1)} async-done(((bf16[256,3072]{1,0:T(8,128)(2,1)}), bf16[256,3072]{1,0:T(8,128)(2,1)}) %all-reduce.4.cloned.1.call-update) | async-done | bytes 1572880 | tf_op jit(solution)/shard_map/psum | solution.py:1267
  336.7 25.9 %reduce-scatter.10.cloned.1.call-done.refs_0_ = bf16[128,1664]{1,0:T(8,128)(2,1)} async-done(((bf16[1024,1664]{1,0:T(8,128)(2,1)}), bf16[128,1664]{1,0:T(8,128)(2,1)}) %reduce-scatter.10.cloned.1.call-update) | async-done | bytes 426000 | tf_op jit(solution)/shard_map/reduce_scatter | solution.py:1276
  362.6 9.7 %all-reduce.6.cloned.1.call-done.refs_2_.refs_0_ = bf16[128,3072]{1,0:T(8,128)(2,1)} async-done(((bf16[128,3072]{1,0:T(8,128)(2,1)}), bf16[128,3072]{1,0:T(8,128)(2,1)}) %all-reduce.6.cloned.1.call-update) | async-done | bytes 786448 | tf_op jit(solution)/shard_map/psum | solution.py:1279
  380.3 44.5 %reduce-scatter.8.cloned.1.call-done.refs_0_ = bf16[256,1024]{1,0:T(8,128)(2,1)} async-done(((bf16[1024,1024]{1,0:T(8,128)(2,1)}), bf16[256,1024]{1,0:T(8,128)(2,1)}) %reduce-scatter.8.cloned.1.call-update) | async-done | bytes 524304 | tf_op jit(solution)/shard_map/reduce_scatter | solution.py:1274
  427.0 3.6 finish_in.1.refs_1_
  439.4 2.1 unpack_attn.1
  (225 shorter events, 74.2 us)
Async XLA Ops:
  8.0 39.4 %all-gather.6.cloned.1.call-start = ((), (), s32[]{:S(2)}) async-start(), calls=%async_computation.5 | async-start | bytes 3833856 | tf_op jit(solution)/shard_map/all_gather | solution.py:1167
  10.1 126.9 %reduce-scatter.6.cloned.1.call-start = ((), (), s32[]{:S(2)}) async-start(), calls=%async_computation.6 | async-start | bytes 1572864 | tf_op jit(solution)/shard_map/reduce_scatter | solution.py:1177
  10.2 39.5 %collective-permute-start.2 = (bf16[256,1024]{1,0:T(8,128)(2,1)}, bf16[256,1024]{1,0:T(8,128)(2,1)}, u32[]{:S(2)}, u32[]{:S(2)}) collective-permute-start(bf16[256,1024]{1,0:T(8,128)(2,1)} %refs_2_.7), channel_id=1, source_target_pairs={{0,3},{1,0},{2,1},{3,2},{4,7},{5,4},{6,5},{7,6},{8,11},{9,8},{10,9... | collective-permute-start | bytes 1572872 | tf_op jit(solution)/shard_map/ppermute | solution.py:1156
  15.3 45.1 %collective-permute-start.1 = (bf16[256,1024]{1,0:T(8,128)(2,1)}, bf16[256,1024]{1,0:T(8,128)(2,1)}, u32[]{:S(2)}, u32[]{:S(2)}) collective-permute-start(bf16[256,1024]{1,0:T(8,128)(2,1)} %refs_2_.7), channel_id=1, source_target_pairs={{0,2},{1,3},{2,0},{3,1},{4,6},{5,7},{6,4},{7,5},{8,10},{9,11},{10,... | collective-permute-start | bytes 1572872 | tf_op jit(solution)/shard_map/ppermute | solution.py:1156
  15.3 45.1 %collective-permute-start = (bf16[256,1024]{1,0:T(8,128)(2,1)}, bf16[256,1024]{1,0:T(8,128)(2,1)}, u32[]{:S(2)}, u32[]{:S(2)}) collective-permute-start(bf16[256,1024]{1,0:T(8,128)(2,1)} %refs_2_.7), channel_id=1, source_target_pairs={{0,1},{1,2},{2,3},{3,0},{4,5},{5,6},{6,7},{7,4},{8,9},{9,10},{10,1... | collective-permute-start | bytes 1572872 | tf_op jit(solution)/shard_map/ppermute | solution.py:1156
  23.3 4.9 %collective-permute-start.8 = (bf16[128,4608]{1,0:T(8,128)(2,1)}, bf16[128,4608]{1,0:T(8,128)(2,1)}, u32[]{:S(2)}, u32[]{:S(2)}) collective-permute-start(bf16[128,4608]{1,0:T(8,128)(2,1)} %get-tuple-element.68), channel_id=1, source_target_pairs={{0,4},{4,0},{1,5},{5,1},{2,6},{6,2},{3,7},{7,3},{8,12},{12,8},{9,1... | collective-permute-start | bytes 3538952 | tf_op jit(solution)/shard_map/ppermute | solution.py:1153
  24.5 131.4 %all-gather.8.cloned.1.call-start = ((), (), s32[]{:S(2)}) async-start(), calls=%async_computation.7 | async-start | bytes 11796480 | tf_op jit(solution)/shard_map/all_gather | solution.py:1173
  31.1 225.9 %reduce-scatter.12.cloned.1.call-start = ((), (), s32[]{:S(2)}) async-start(), calls=%async_computation.11 | async-start | bytes 7864320 | tf_op jit(solution)/shard_map/reduce_scatter | solution.py:1246
  49.7 65.1 %copy-start.45 = (f32[1,1024]{1,0:T(1,128)}, f32[1,1024]{1,0:T(1,128)S(1)}, u32[]{:S(2)}) copy-start(f32[1,1024]{1,0:T(1,128)S(1)} %get-tuple-element.110.refs_1_.refs_4_) | copy-start | bytes 12292
  70.1 6.7 %collective-permute-start.3 = (bf16[1024,512]{1,0:T(8,128)(2,1)S(1)}, bf16[1024,512]{1,0:T(8,128)(2,1)S(1)}, u32[]{:S(2)}, u32[]{:S(2)}) collective-permute-start(bf16[1024,512]{1,0:T(8,128)(2,1)S(1)} %get-tuple-element.58.refs_1_.refs_2_), channel_id=1, source_target_pairs={{0,4},{4,8},{8,12},{12,16},{16,20},{20,24},{24,28},{1,5},{5,9},{9,... | collective-permute-start | bytes 3145736 | tf_op jit(solution)/shard_map/ppermute | solution.py:1211
  81.0 25.6 %collective-permute-start.6 = (bf16[256,1024]{1,0:T(8,128)(2,1)}, bf16[256,1024]{1,0:T(8,128)(2,1)}, u32[]{:S(2)}, u32[]{:S(2)}) collective-permute-start(bf16[256,1024]{1,0:T(8,128)(2,1)} %get-tuple-element.63), channel_id=1, source_target_pairs={{0,3},{1,0},{2,1},{3,2},{4,7},{5,4},{6,5},{7,6},{8,11},{9,8},{10,9... | collective-permute-start | bytes 1572872 | tf_op jit(solution)/shard_map/ppermute | solution.py:1156
  85.9 24.9 %collective-permute-start.5 = (bf16[256,1024]{1,0:T(8,128)(2,1)S(1)}, bf16[256,1024]{1,0:T(8,128)(2,1)S(1)}, u32[]{:S(2)}, u32[]{:S(2)}) collective-permute-start(bf16[256,1024]{1,0:T(8,128)(2,1)S(1)} %get-tuple-element.62), channel_id=1, source_target_pairs={{0,2},{1,3},{2,0},{3,1},{4,6},{5,7},{6,4},{7,5},{8,10},{9,11},{10,... | collective-permute-start | bytes 1572872 | tf_op jit(solution)/shard_map/ppermute | solution.py:1156
  100.2 14.6 %collective-permute-start.4 = (bf16[256,1024]{1,0:T(8,128)(2,1)S(1)}, bf16[256,1024]{1,0:T(8,128)(2,1)S(1)}, u32[]{:S(2)}, u32[]{:S(2)}) collective-permute-start(bf16[256,1024]{1,0:T(8,128)(2,1)S(1)} %get-tuple-element.61), channel_id=1, source_target_pairs={{0,1},{1,2},{2,3},{3,0},{4,5},{5,6},{6,7},{7,4},{8,9},{9,10},{10,1... | collective-permute-start | bytes 1572872 | tf_op jit(solution)/shard_map/ppermute | solution.py:1156
  106.6 49.4 %copy-start.25 = (bf16[256,1024]{1,0:T(8,128)(2,1)S(1)}, bf16[256,1024]{1,0:T(8,128)(2,1)}, u32[]{:S(2)}) copy-start(bf16[256,1024]{1,0:T(8,128)(2,1)} %refs_0_.3) | copy-start | bytes 1572868
  117.3 56.4 %copy-start.8 = (f32[256,1024]{1,0:T(8,128)}, f32[256,1024]{1,0:T(8,128)S(1)}, u32[]{:S(2)}) copy-start(f32[256,1024]{1,0:T(8,128)S(1)} %get-tuple-element.65.refs_2_) | copy-start | bytes 3145732
  117.3 21.3 %collective-permute-start.7 = (bf16[256,1024]{1,0:T(8,128)(2,1)S(1)}, bf16[256,1024]{1,0:T(8,128)(2,1)S(1)}, u32[]{:S(2)}, u32[]{:S(2)}) collective-permute-start(bf16[256,1024]{1,0:T(8,128)(2,1)S(1)} %get-tuple-element.66.refs_0_.refs_3_), channel_id=1, source_target_pairs={{0,4},{4,0},{1,5},{5,1},{2,6},{6,2},{3,7},{7,3},{8,12},{12,8},{9,1... | collective-permute-start | bytes 1572872 | tf_op jit(solution)/shard_map/ppermute | solution.py:1153
  171.8 2.0 collective-permute-start.10
  186.5 70.7 %all-gather.10.cloned.1.call-start = ((), (), s32[]{:S(2)}) async-start(), calls=%async_computation.8 | async-start | bytes 2621440 | tf_op jit(solution)/shard_map/all_gather | solution.py:1242
  187.1 123.0 %reduce-scatter.14.cloned.1.call-start = ((), (), s32[]{:S(2)}) async-start(), calls=%async_computation.13 | async-start | bytes 3932160 | tf_op jit(solution)/shard_map/reduce_scatter | solution.py:1246
  191.9 134.0 %all-reduce.4.cloned.1.call-start = ((), (), s32[]{:S(2)}) async-start(), calls=%async_computation.12 | async-start | bytes 3145728 | tf_op jit(solution)/shard_map/psum | solution.py:1267
  192.8 64.4 %copy-start.54 = (bf16[1024,512]{1,0:T(8,128)(2,1)S(1)}, bf16[1024,512]{1,0:T(8,128)(2,1)}, u32[]{:S(2)}) copy-start(bf16[1024,512]{1,0:T(8,128)(2,1)} %copy-done.53) | copy-start | bytes 3145732
  257.0 105.7 %reduce-scatter.10.cloned.1.call-start = ((), (), s32[]{:S(2)}) async-start(), calls=%async_computation.10 | async-start | bytes 3833856 | tf_op jit(solution)/shard_map/reduce_scatter | solution.py:1276
  274.6 16.9 %collective-permute-start.11 = (bf16[2,1024,256]{2,1,0:T(8,128)(2,1)S(1)}, bf16[2,1024,256]{2,1,0:T(8,128)(2,1)S(1)}, u32[]{:S(2)}, u32[]{:S(2)}) collective-permute-start(bf16[2,1024,256]{2,1,0:T(8,128)(2,1)S(1)} %get-tuple-element.88), channel_id=1, source_target_pairs={{4,0},{8,4},{12,8},{16,12},{20,16},{24,20},{28,24},{5,1},{9,5},{13... | collective-permute-start | bytes 3145736 | tf_op jit(solution)/shard_map/ppermute | solution.py:1263
  310.1 62.3 %all-reduce.6.cloned.1.call-start = ((), (), s32[]{:S(2)}) async-start(), calls=%async_computation.14 | async-start | bytes 1572864 | tf_op jit(solution)/shard_map/psum | solution.py:1279
  311.2 6.7 %collective-permute-start.14 = (bf16[128,1536]{1,0:T(8,128)(2,1)S(1)}, bf16[128,1536]{1,0:T(8,128)(2,1)S(1)}, u32[]{:S(2)}, u32[]{:S(2)}) collective-permute-start(bf16[128,1536]{1,0:T(8,128)(2,1)S(1)} %constant_dynamic-slice_fusion), channel_id=1, source_target_pairs={{0,4},{4,0},{1,5},{5,1},{2,6},{6,2},{3,7},{7,3},{8,12},{12,8},{9,1... | collective-permute-start | bytes 1179656 | tf_op jit(solution)/shard_map/ppermute | solution.py:1153
  329.5 95.3 %reduce-scatter.8.cloned.1.call-start = ((), (), s32[]{:S(2)}) async-start(), calls=%async_computation.9 | async-start | bytes 2621440 | tf_op jit(solution)/shard_map/reduce_scatter | solution.py:1274
  330.1 104.2 %all-gather.12.cloned.1.call-start = ((), (), s32[]{:S(2)}) async-start(), calls=%async_computation.15 | async-start | bytes 2129920 | tf_op jit(solution)/shard_map/all_gather | solution.py:1283
  330.9 1.8 collective-permute-start.13
  331.0 3.1 collective-permute-start.12
  377.2 47.5 %copy-start.48 = (f32[1,1024]{1,0:T(1,128)S(1)}, f32[1,1024]{1,0:T(1,128)}, u32[]{:S(2)}) copy-start(f32[1,1024]{1,0:T(1,128)} %copy-done.47) | copy-start | bytes 12292
  377.2 2.0 collective-permute-start.9
  380.3 50.3 %copy-start.13 = (bf16[128,3072]{1,0:T(8,128)(2,1)S(1)}, bf16[128,3072]{1,0:T(8,128)(2,1)}, u32[]{:S(2)}) copy-start(bf16[128,3072]{1,0:T(8,128)(2,1)} %all-reduce.6.cloned.1.call-done.refs_2_.refs_0_) | copy-start | bytes 2359300
  (61 other events, 350.8 us)
Sparse Core Ops, SparseCore 0:
  11.3 36.1 all-gather.5
  49.4 106.4 all-gather.7
  186.7 70.2 reduce-scatter.11
  260.0 47.0 reduce-scatter.13
  310.9 51.7 reduce-scatter.9
  364.8 59.9 reduce-scatter.7
Sparse Core Ops, SparseCore 1:
  24.6 9.0 reduce-scatter.5
  189.2 45.6 all-gather.9
  257.0 68.8 all-reduce.3
  329.6 42.7 all-reduce.5
  377.3 56.8 all-gather.11

commit v6 on v5

--- a/solution.py
+++ b/solution.py
@@ -351,6 +351,7 @@
             shape_of((parts * q_cols, rows), f32),
         ],
         estimate=cost(0, parts * rows * total * 6, scale=1),
+        mib=60,
         name="unpack_attn",
         after=after,
     )

time: 458 us -> 457 us (level)
    unnamed x136 -> x132, local copies, waits for them, and re-layouts: 39.6 us -> 36.7 us
where the time goes in v6:
time: 457 us; the launch traced here: 448 us
  waiting for transfers between devices  215 us (47%)
  Pallas kernels  125 us (27%)
  starting transfers between devices  44.1 us (10%)
  local copies, waits for them, and re-layouts  40.9 us (9%)
  between operations  17 us (4%)
  other arithmetic  6.71 us (1%)
    pallas_call x25, Pallas kernels, call(): pl.pallas_call(body_of, grid_spec=pltpu.PrefetchScalarGridSpec(num_scalar...  125 us
    reduce_scatter x2, waiting for transfers between devices, chip_sums(): return lax.psum_scatter(grad, 'q', scatter_dimension=0, tiled=True)  63.9 us
    reduce_scatter x1, waiting for transfers between devices, body(): d_in = lax.psum_scatter(d_in, 'seq', scatter_dimension=0, tiled=True)  44.4 us
    unnamed x132, local copies, waits for them, and re-layouts  36.7 us
    reduce_scatter x1, waiting for transfers between devices, body(): lax.psum_scatter(attn_term, dp_axes, scatter_dimension=0, tiled=True)  25.9 us
    ppermute x7, starting transfers between devices, swapped(): return lax.ppermute(value, 'c', core_swap)  25.8 us
    ppermute x6, waiting for transfers between devices, sent(): lax.ppermute(value, 'seq', [(i, (i + shift) % parts) for i in range(parts)])  18.9 us
    all_gather x1, waiting for transfers between devices, body(): mlp_w = lax.all_gather(mlp_pack, 'q', axis=0, tiled=True)  17.3 us
  transfers between devices with their start and end apart: 26, of which 16 were waited for; matrix products, arithmetic and copies ran while one was open for 2% of the time, Pallas kernels for 21%

profile of v6, /device:TPU:0, one launch (start us, length us, event | category | flops | bytes accessed | tf_op | source)
XLA Modules:
  0.0 448.5 jit_solution(10073778009660273056)
XLA Ops:
  8.1 2.1 pack_attn.1.refs_4_
  10.2 5.1 %collective-permute-start.2 = (bf16[256,1024]{1,0:T(8,128)(2,1)}, bf16[256,1024]{1,0:T(8,128)(2,1)}, u32[]{:S(2)}, u32[]{:S(2)}) collective-permute-start(bf16[256,1024]{1,0:T(8,128)(2,1)} %refs_2_.7), channel_id=1, source_target_pairs={{0,3},{1,0},{2,1},{3,2},{4,7},{5,4},{6,5},{7,6},{8,11},{9,8},{10,9... | collective-permute-start | bytes 1572872 | tf_op jit(solution)/shard_map/ppermute | solution.py:1157
  31.1 16.4 %all-gather.6.cloned.1.call-done.refs_0_.refs_5_.refs_7_.refs_9_ = bf16[1024,1664]{1,0:T(8,128)(2,1)} async-done(((bf16[128,1664]{1,0:T(8,128)(2,1)}), bf16[1024,1664]{1,0:T(8,128)(2,1)}) %all-gather.6.cloned.1.call-update) | async-done | bytes 3407888 | tf_op jit(solution)/shard_map/all_gather | solution.py:1168
  49.7 10.7 %collective-permute-done.1.refs_3_ = bf16[256,1024]{1,0:T(8,128)(2,1)} collective-permute-done((bf16[256,1024]{1,0:T(8,128)(2,1)}, bf16[256,1024]{1,0:T(8,128)(2,1)}, u32[]{:S(2)}, u32[]{:S(2)}) %collective-permute-start.1) | collective-permute-done | bytes 524320 | tf_op jit(solution)/shard_map/ppermute | solution.py:1157
  62.6 5.9 %project.1 = (bf16[1024,1024]{1,0:T(8,128)(2,1)S(1)}, bf16[1024,512]{1,0:T(8,128)(2,1)S(1)}, bf16[1024,512]{1,0:T(8,128)(2,1)S(1)}, f32[1024,768]{1,0:T(8,128)S(1)}) custom-call(s32[1]{0:T(128)} %bitcast.refs_0_, bf16[256,1024]{1,0:T(8,128)(2,1)} %refs_2_.7, bf16[256,1024]{1,0:T(8,128)(2,1)} %collective-permute-done.refs_2_.refs_4_, ...), custom_call_target="tpu_custom_call" | custom-call | flops 214748364800 | bytes 1258291200 | tf_op jit(solution)/shard_map/project/pallas_call | solution.py:54
  71.5 5.3 %attend_own.1 = (f32[512,1024]{1,0:T(8,128)S(1)}, f32[2,8,1024]{2,1,0:T(8,128)S(1)}) custom-call(bf16[1024,512]{1,0:T(8,128)(2,1)S(1)} %get-tuple-element.57.refs_0_.refs_1_, bf16[1024,512]{1,0:T(8,128)(2,1)S(1)} %get-tuple-element.58.refs_1_.refs_2_, bf16[1024,512]{1,0:T(8,128)(2,1)S(1)} %get-tuple-element.58.refs_1_.refs_2_, ...), custom_call_target="tpu_custom_call" | custom-call | flops 134217728000 | bytes 419430400 | tf_op jit(solution)/shard_map/attend_own/pallas_call | solution.py:54
  76.8 3.5 attend_tail.6
  81.2 4.0 attend_tail.5
  85.8 8.5 %collective-permute-start.5 = (bf16[256,1024]{1,0:T(8,128)(2,1)S(1)}, bf16[256,1024]{1,0:T(8,128)(2,1)S(1)}, u32[]{:S(2)}, u32[]{:S(2)}) collective-permute-start(bf16[256,1024]{1,0:T(8,128)(2,1)S(1)} %get-tuple-element.62), channel_id=1, source_target_pairs={{0,2},{1,3},{2,0},{3,1},{4,6},{5,7},{6,4},{7,5},{8,10},{9,11},{10,... | collective-permute-start | bytes 1572872 | tf_op jit(solution)/shard_map/ppermute | solution.py:1157
  94.3 5.1 %attend_tail.4 = (bf16[256,512]{1,0:T(8,128)(2,1)S(1)}, f32[2,8,256]{2,1,0:T(8,128)S(1)}, bf16[256,1024]{1,0:T(8,128)(2,1)S(1)}) custom-call(s32[1]{0:T(128)} %bitcast.refs_0_, bf16[1024,512]{1,0:T(8,128)(2,1)S(1)} %get-tuple-element.57.refs_0_.refs_1_, bf16[1024,512]{1,0:T(8,128)(2,1)S(1)} %collective-permute-done.3.refs_2_.refs_3_.refs_1_, ...), custom_call_target="tpu_custom_call" | custom-call | flops 53687091200 | bytes 419430400 | tf_op jit(solution)/shard_map/attend_tail/pallas_call | solution.py:54
  100.2 6.4 %attend_tail.7 = (bf16[256,512]{1,0:T(8,128)(2,1)S(1)}, f32[2,8,256]{2,1,0:T(8,128)S(1)}, bf16[256,1024]{1,0:T(8,128)(2,1)S(1)}) custom-call(s32[1]{0:T(128)} %bitcast.refs_0_, bf16[1024,512]{1,0:T(8,128)(2,1)S(1)} %get-tuple-element.57.refs_0_.refs_1_, bf16[1024,512]{1,0:T(8,128)(2,1)S(1)} %collective-permute-done.3.refs_2_.refs_3_.refs_1_, ...), custom_call_target="tpu_custom_call" | custom-call | flops 53687091200 | bytes 419430400 | tf_op jit(solution)/shard_map/attend_tail/pallas_call | solution.py:54
  106.6 4.1 collective-permute-done.5.refs_3_
  110.7 4.1 collective-permute-done.4.refs_2_
  114.8 2.6 mid_norm.1
  117.3 19.7 %collective-permute-start.7 = (bf16[256,1024]{1,0:T(8,128)(2,1)S(1)}, bf16[256,1024]{1,0:T(8,128)(2,1)S(1)}, u32[]{:S(2)}, u32[]{:S(2)}) collective-permute-start(bf16[256,1024]{1,0:T(8,128)(2,1)S(1)} %get-tuple-element.66.refs_0_.refs_3_), channel_id=1, source_target_pairs={{0,4},{4,0},{1,5},{5,1},{2,6},{6,2},{3,7},{7,3},{8,12},{12,8},{9,1... | collective-permute-start | bytes 1572872 | tf_op jit(solution)/shard_map/ppermute | solution.py:1154
  138.6 17.3 %all-gather.8.cloned.1.call-done.refs_4_.refs_5_.refs_6_ = bf16[1024,4608]{1,0:T(8,128)(2,1)} async-done(((bf16[256,4608]{1,0:T(8,128)(2,1)}), bf16[1024,4608]{1,0:T(8,128)(2,1)}) %all-gather.8.cloned.1.call-update) | async-done | bytes 9437200 | tf_op jit(solution)/shard_map/all_gather | solution.py:1174
  157.0 14.8 %mlp.1 = (bf16[512,1536]{1,0:T(8,128)(2,1)}, bf16[512,1536]{1,0:T(8,128)(2,1)}, bf16[512,1536]{1,0:T(8,128)(2,1)}, f32[256,1024]{1,0:T(8,128)S(1)}, bf16[256,102...) custom-call(bf16[256,1024]{1,0:T(8,128)(2,1)S(1)} %get-tuple-element.66.refs_0_.refs_3_, ...), custom_call_target="tpu_custom_call" | custom-call | flops 966367641600 | bytes 1677721600 | tf_op jit(solution)/shard_map/mlp/pallas_call | solution.py:54
  173.7 2.0 mid_back.1
  179.6 6.8 %mlp_grad_pair.1 = bf16[1024,3072]{1,0:T(8,128)(2,1)} custom-call(bf16[256,1024]{1,0:T(8,128)(2,1)S(1)} %copy-done.24, bf16[256,1024]{1,0:T(8,128)(2,1)S(1)} %bitcast.21, bf16[512,1536]{1,0:T(8,128)(2,1)S(1)} %copy-done.61, bf16[256,1024]{1,0:T(8,128)(2,1)S(1)} %get-tuple-element.66.refs_0_.refs_3_, ...), custom_call_target="tpu_custom_call" | custom-call | flops 322122547200 | bytes 1677721600 | tf_op jit(solution)/shard_map/mlp_grad_pair/pallas_call | solution.py:54
  187.9 3.9 mlp_grad.1.refs_8_
  193.1 63.9 %reduce-scatter.12.cloned.1.call-done = bf16[256,3072]{1,0:T(8,128)(2,1)} async-done(((bf16[1024,3072]{1,0:T(8,128)(2,1)}), bf16[256,3072]{1,0:T(8,128)(2,1)}) %reduce-scatter.12.cloned.1.call-update) | async-done | bytes 1572880 | tf_op jit(solution)/shard_map/reduce_scatter | solution.py:1247
  260.1 14.5 %attend_back_tail.1 = (bf16[1024,512]{1,0:T(8,128)(2,1)S(1)}, f32[512,1024]{1,0:T(8,128)S(1)}, f32[2,8,1024]{2,1,0:T(8,128)S(1)}, bf16[2,1024,256]{2,1,0:T(8,128)(2,1)S(1)}) custom-call(bf16[1024,512]{1,0:T(8,128)(2,1)S(1)} %copy-done.58, bf16[1024,512]{1,0:T(8,128)(2,1)S(1)} %copy-done.52, bf16[1024,512]{1,0:T(8,128)(2,1)S(1)} %copy-done.52, ...), custom_call_target="tpu_custom_call" | custom-call | flops 442918502400 | bytes 838860800 | tf_op jit(solution)/shard_map/attend_back_tail/pallas_call | solution.py:54
  276.2 12.1 %attend_back_own.1 = (bf16[1024,512]{1,0:T(8,128)(2,1)S(1)}, f32[2,1024,256]{2,1,0:T(8,128)S(1)}) custom-call(bf16[1024,512]{1,0:T(8,128)(2,1)S(1)} %copy-done.59, bf16[1024,512]{1,0:T(8,128)(2,1)S(1)} %copy-done.50, bf16[1024,512]{1,0:T(8,128)(2,1)S(1)} %copy-done.50, s32[4,8,256]{2,1,0:T(8,128)S(1)} %pad.4.refs_3_.refs_4_, ...), custom_call_target="tpu_custom_call" | custom-call | flops 3355443200 | bytes 8388608 | tf_op jit(solution)/shard_map/attend_back_own/pallas_call | solution.py:54
  288.3 2.2 out_grad.1.refs_14_
  291.6 18.5 %project_back.1 = (bf16[1024,1024]{1,0:T(8,128)(2,1)}, bf16[1024,1664]{1,0:T(8,128)(2,1)}) custom-call(s32[1]{0:T(128)} %bitcast.refs_0_, bf16[256,1024]{1,0:T(8,128)(2,1)} %refs_2_.7, bf16[256,1024]{1,0:T(8,128)(2,1)} %collective-permute-done.2.refs_4_.refs_2_, bf16[256,1024]{1,0:T(8,128)(2,1)} %collective-permute-done.1.refs_3_, ...), custom_call_target="tpu_custom_call" | custom-call | flops 4294967296 | bytes 16777216 | tf_op jit(solution)/shard_map/project_back/pallas_call | solution.py:54
  311.2 5.3 %collective-permute-start.14 = (bf16[128,1536]{1,0:T(8,128)(2,1)S(1)}, bf16[128,1536]{1,0:T(8,128)(2,1)S(1)}, u32[]{:S(2)}, u32[]{:S(2)}) collective-permute-start(bf16[128,1536]{1,0:T(8,128)(2,1)S(1)} %constant_dynamic-slice_fusion), channel_id=1, source_target_pairs={{0,4},{4,0},{1,5},{5,1},{2,6},{6,2},{3,7},{7,3},{8,12},{12,8},{9,1... | collective-permute-start | bytes 1179656 | tf_op jit(solution)/shard_map/ppermute | solution.py:1154
  317.9 8.0 %all-reduce.4.cloned.1.call-done.refs_1_.refs_3_ = bf16[256,3072]{1,0:T(8,128)(2,1)} async-done(((bf16[256,3072]{1,0:T(8,128)(2,1)}), bf16[256,3072]{1,0:T(8,128)(2,1)}) %all-reduce.4.cloned.1.call-update) | async-done | bytes 1572880 | tf_op jit(solution)/shard_map/psum | solution.py:1268
  336.7 25.9 %reduce-scatter.10.cloned.1.call-done.refs_0_ = bf16[128,1664]{1,0:T(8,128)(2,1)} async-done(((bf16[1024,1664]{1,0:T(8,128)(2,1)}), bf16[128,1664]{1,0:T(8,128)(2,1)}) %reduce-scatter.10.cloned.1.call-update) | async-done | bytes 426000 | tf_op jit(solution)/shard_map/reduce_scatter | solution.py:1277
  362.7 9.7 %all-reduce.6.cloned.1.call-done.refs_2_.refs_0_ = bf16[128,3072]{1,0:T(8,128)(2,1)} async-done(((bf16[128,3072]{1,0:T(8,128)(2,1)}), bf16[128,3072]{1,0:T(8,128)(2,1)}) %all-reduce.6.cloned.1.call-update) | async-done | bytes 786448 | tf_op jit(solution)/shard_map/psum | solution.py:1280
  380.3 44.4 %reduce-scatter.8.cloned.1.call-done.refs_0_ = bf16[256,1024]{1,0:T(8,128)(2,1)} async-done(((bf16[1024,1024]{1,0:T(8,128)(2,1)}), bf16[256,1024]{1,0:T(8,128)(2,1)}) %reduce-scatter.8.cloned.1.call-update) | async-done | bytes 524304 | tf_op jit(solution)/shard_map/reduce_scatter | solution.py:1275
  427.0 3.6 finish_in.1.refs_1_
  436.6 3.9 unpack_attn.1
  (221 shorter events, 71.4 us)
Async XLA Ops:
  8.0 39.4 %all-gather.6.cloned.1.call-start = ((), (), s32[]{:S(2)}) async-start(), calls=%async_computation.5 | async-start | bytes 3833856 | tf_op jit(solution)/shard_map/all_gather | solution.py:1168
  10.1 126.9 %reduce-scatter.6.cloned.1.call-start = ((), (), s32[]{:S(2)}) async-start(), calls=%async_computation.6 | async-start | bytes 1572864 | tf_op jit(solution)/shard_map/reduce_scatter | solution.py:1178
  10.2 39.5 %collective-permute-start.2 = (bf16[256,1024]{1,0:T(8,128)(2,1)}, bf16[256,1024]{1,0:T(8,128)(2,1)}, u32[]{:S(2)}, u32[]{:S(2)}) collective-permute-start(bf16[256,1024]{1,0:T(8,128)(2,1)} %refs_2_.7), channel_id=1, source_target_pairs={{0,3},{1,0},{2,1},{3,2},{4,7},{5,4},{6,5},{7,6},{8,11},{9,8},{10,9... | collective-permute-start | bytes 1572872 | tf_op jit(solution)/shard_map/ppermute | solution.py:1157
  15.3 45.1 %collective-permute-start.1 = (bf16[256,1024]{1,0:T(8,128)(2,1)}, bf16[256,1024]{1,0:T(8,128)(2,1)}, u32[]{:S(2)}, u32[]{:S(2)}) collective-permute-start(bf16[256,1024]{1,0:T(8,128)(2,1)} %refs_2_.7), channel_id=1, source_target_pairs={{0,2},{1,3},{2,0},{3,1},{4,6},{5,7},{6,4},{7,5},{8,10},{9,11},{10,... | collective-permute-start | bytes 1572872 | tf_op jit(solution)/shard_map/ppermute | solution.py:1157
  15.3 45.1 %collective-permute-start = (bf16[256,1024]{1,0:T(8,128)(2,1)}, bf16[256,1024]{1,0:T(8,128)(2,1)}, u32[]{:S(2)}, u32[]{:S(2)}) collective-permute-start(bf16[256,1024]{1,0:T(8,128)(2,1)} %refs_2_.7), channel_id=1, source_target_pairs={{0,1},{1,2},{2,3},{3,0},{4,5},{5,6},{6,7},{7,4},{8,9},{9,10},{10,1... | collective-permute-start | bytes 1572872 | tf_op jit(solution)/shard_map/ppermute | solution.py:1157
  23.3 4.9 %collective-permute-start.8 = (bf16[128,4608]{1,0:T(8,128)(2,1)}, bf16[128,4608]{1,0:T(8,128)(2,1)}, u32[]{:S(2)}, u32[]{:S(2)}) collective-permute-start(bf16[128,4608]{1,0:T(8,128)(2,1)} %get-tuple-element.68), channel_id=1, source_target_pairs={{0,4},{4,0},{1,5},{5,1},{2,6},{6,2},{3,7},{7,3},{8,12},{12,8},{9,1... | collective-permute-start | bytes 3538952 | tf_op jit(solution)/shard_map/ppermute | solution.py:1154
  24.5 131.4 %all-gather.8.cloned.1.call-start = ((), (), s32[]{:S(2)}) async-start(), calls=%async_computation.7 | async-start | bytes 11796480 | tf_op jit(solution)/shard_map/all_gather | solution.py:1174
  31.1 225.9 %reduce-scatter.12.cloned.1.call-start = ((), (), s32[]{:S(2)}) async-start(), calls=%async_computation.11 | async-start | bytes 7864320 | tf_op jit(solution)/shard_map/reduce_scatter | solution.py:1247
  49.7 65.1 %copy-start.43 = (f32[1,1024]{1,0:T(1,128)}, f32[1,1024]{1,0:T(1,128)S(1)}, u32[]{:S(2)}) copy-start(f32[1,1024]{1,0:T(1,128)S(1)} %get-tuple-element.110.refs_1_.refs_4_) | copy-start | bytes 12292
  70.1 6.7 %collective-permute-start.3 = (bf16[1024,512]{1,0:T(8,128)(2,1)S(1)}, bf16[1024,512]{1,0:T(8,128)(2,1)S(1)}, u32[]{:S(2)}, u32[]{:S(2)}) collective-permute-start(bf16[1024,512]{1,0:T(8,128)(2,1)S(1)} %get-tuple-element.58.refs_1_.refs_2_), channel_id=1, source_target_pairs={{0,4},{4,8},{8,12},{12,16},{16,20},{20,24},{24,28},{1,5},{5,9},{9,... | collective-permute-start | bytes 3145736 | tf_op jit(solution)/shard_map/ppermute | solution.py:1212
  81.0 25.6 %collective-permute-start.6 = (bf16[256,1024]{1,0:T(8,128)(2,1)}, bf16[256,1024]{1,0:T(8,128)(2,1)}, u32[]{:S(2)}, u32[]{:S(2)}) collective-permute-start(bf16[256,1024]{1,0:T(8,128)(2,1)} %get-tuple-element.63), channel_id=1, source_target_pairs={{0,3},{1,0},{2,1},{3,2},{4,7},{5,4},{6,5},{7,6},{8,11},{9,8},{10,9... | collective-permute-start | bytes 1572872 | tf_op jit(solution)/shard_map/ppermute | solution.py:1157
  85.8 24.9 %collective-permute-start.5 = (bf16[256,1024]{1,0:T(8,128)(2,1)S(1)}, bf16[256,1024]{1,0:T(8,128)(2,1)S(1)}, u32[]{:S(2)}, u32[]{:S(2)}) collective-permute-start(bf16[256,1024]{1,0:T(8,128)(2,1)S(1)} %get-tuple-element.62), channel_id=1, source_target_pairs={{0,2},{1,3},{2,0},{3,1},{4,6},{5,7},{6,4},{7,5},{8,10},{9,11},{10,... | collective-permute-start | bytes 1572872 | tf_op jit(solution)/shard_map/ppermute | solution.py:1157
  100.2 14.6 %collective-permute-start.4 = (bf16[256,1024]{1,0:T(8,128)(2,1)S(1)}, bf16[256,1024]{1,0:T(8,128)(2,1)S(1)}, u32[]{:S(2)}, u32[]{:S(2)}) collective-permute-start(bf16[256,1024]{1,0:T(8,128)(2,1)S(1)} %get-tuple-element.61), channel_id=1, source_target_pairs={{0,1},{1,2},{2,3},{3,0},{4,5},{5,6},{6,7},{7,4},{8,9},{9,10},{10,1... | collective-permute-start | bytes 1572872 | tf_op jit(solution)/shard_map/ppermute | solution.py:1157
  106.6 49.4 %copy-start.24 = (bf16[256,1024]{1,0:T(8,128)(2,1)S(1)}, bf16[256,1024]{1,0:T(8,128)(2,1)}, u32[]{:S(2)}) copy-start(bf16[256,1024]{1,0:T(8,128)(2,1)} %refs_0_.3) | copy-start | bytes 1572868
  117.3 56.4 %copy-start.7 = (f32[256,1024]{1,0:T(8,128)}, f32[256,1024]{1,0:T(8,128)S(1)}, u32[]{:S(2)}) copy-start(f32[256,1024]{1,0:T(8,128)S(1)} %get-tuple-element.65.refs_2_) | copy-start | bytes 3145732
  117.3 21.2 %collective-permute-start.7 = (bf16[256,1024]{1,0:T(8,128)(2,1)S(1)}, bf16[256,1024]{1,0:T(8,128)(2,1)S(1)}, u32[]{:S(2)}, u32[]{:S(2)}) collective-permute-start(bf16[256,1024]{1,0:T(8,128)(2,1)S(1)} %get-tuple-element.66.refs_0_.refs_3_), channel_id=1, source_target_pairs={{0,4},{4,0},{1,5},{5,1},{2,6},{6,2},{3,7},{7,3},{8,12},{12,8},{9,1... | collective-permute-start | bytes 1572872 | tf_op jit(solution)/shard_map/ppermute | solution.py:1154
  171.8 2.0 collective-permute-start.10
  186.5 70.7 %all-gather.10.cloned.1.call-start = ((), (), s32[]{:S(2)}) async-start(), calls=%async_computation.8 | async-start | bytes 2621440 | tf_op jit(solution)/shard_map/all_gather | solution.py:1243
  187.1 123.0 %reduce-scatter.14.cloned.1.call-start = ((), (), s32[]{:S(2)}) async-start(), calls=%async_computation.13 | async-start | bytes 3932160 | tf_op jit(solution)/shard_map/reduce_scatter | solution.py:1247
  191.9 134.0 %all-reduce.4.cloned.1.call-start = ((), (), s32[]{:S(2)}) async-start(), calls=%async_computation.12 | async-start | bytes 3145728 | tf_op jit(solution)/shard_map/psum | solution.py:1268
  192.8 64.5 %copy-start.52 = (bf16[1024,512]{1,0:T(8,128)(2,1)S(1)}, bf16[1024,512]{1,0:T(8,128)(2,1)}, u32[]{:S(2)}) copy-start(bf16[1024,512]{1,0:T(8,128)(2,1)} %copy-done.51) | copy-start | bytes 3145732
  257.0 105.7 %reduce-scatter.10.cloned.1.call-start = ((), (), s32[]{:S(2)}) async-start(), calls=%async_computation.10 | async-start | bytes 3833856 | tf_op jit(solution)/shard_map/reduce_scatter | solution.py:1277
  274.6 16.9 %collective-permute-start.11 = (bf16[2,1024,256]{2,1,0:T(8,128)(2,1)S(1)}, bf16[2,1024,256]{2,1,0:T(8,128)(2,1)S(1)}, u32[]{:S(2)}, u32[]{:S(2)}) collective-permute-start(bf16[2,1024,256]{2,1,0:T(8,128)(2,1)S(1)} %get-tuple-element.88), channel_id=1, source_target_pairs={{4,0},{8,4},{12,8},{16,12},{20,16},{24,20},{28,24},{5,1},{9,5},{13... | collective-permute-start | bytes 3145736 | tf_op jit(solution)/shard_map/ppermute | solution.py:1264
  310.1 62.3 %all-reduce.6.cloned.1.call-start = ((), (), s32[]{:S(2)}) async-start(), calls=%async_computation.14 | async-start | bytes 1572864 | tf_op jit(solution)/shard_map/psum | solution.py:1280
  311.2 6.7 %collective-permute-start.14 = (bf16[128,1536]{1,0:T(8,128)(2,1)S(1)}, bf16[128,1536]{1,0:T(8,128)(2,1)S(1)}, u32[]{:S(2)}, u32[]{:S(2)}) collective-permute-start(bf16[128,1536]{1,0:T(8,128)(2,1)S(1)} %constant_dynamic-slice_fusion), channel_id=1, source_target_pairs={{0,4},{4,0},{1,5},{5,1},{2,6},{6,2},{3,7},{7,3},{8,12},{12,8},{9,1... | collective-permute-start | bytes 1179656 | tf_op jit(solution)/shard_map/ppermute | solution.py:1154
  329.5 95.2 %reduce-scatter.8.cloned.1.call-start = ((), (), s32[]{:S(2)}) async-start(), calls=%async_computation.9 | async-start | bytes 2621440 | tf_op jit(solution)/shard_map/reduce_scatter | solution.py:1275
  330.1 104.2 %all-gather.12.cloned.1.call-start = ((), (), s32[]{:S(2)}) async-start(), calls=%async_computation.15 | async-start | bytes 2129920 | tf_op jit(solution)/shard_map/all_gather | solution.py:1284
  330.9 1.8 collective-permute-start.13
  331.0 3.1 collective-permute-start.12
  377.2 47.5 %copy-start.46 = (f32[1,1024]{1,0:T(1,128)S(1)}, f32[1,1024]{1,0:T(1,128)}, u32[]{:S(2)}) copy-start(f32[1,1024]{1,0:T(1,128)} %copy-done.45) | copy-start | bytes 12292
  377.3 2.0 collective-permute-start.9
  380.3 50.3 %copy-start.12 = (bf16[128,3072]{1,0:T(8,128)(2,1)S(1)}, bf16[128,3072]{1,0:T(8,128)(2,1)}, u32[]{:S(2)}) copy-start(bf16[128,3072]{1,0:T(8,128)(2,1)} %all-reduce.6.cloned.1.call-done.refs_2_.refs_0_) | copy-start | bytes 2359300
  (59 other events, 347.9 us)
Sparse Core Ops, SparseCore 0:
  11.3 36.1 all-gather.5
  49.4 106.4 all-gather.7
  186.6 70.2 reduce-scatter.11
  260.1 47.0 reduce-scatter.13
  310.8 51.7 reduce-scatter.9
  364.8 59.8 reduce-scatter.7
Sparse Core Ops, SparseCore 1:
  24.6 9.0 reduce-scatter.5
  189.2 45.6 all-gather.9
  257.1 68.8 all-reduce.3
  329.6 42.7 all-reduce.5
  377.3 56.8 all-gather.11
